TPU v7x, 512 devices: a whole 4x8x8 slice. The times are simulated.
512 devices in a mesh: seq: 32 (over x, z), batch: 16 (over y, core).
Axes of the slice: x: 4, y: 8, z: 8, core: 2. Of those that a mesh axis runs over, the one named last changes fastest.
Arguments:
- feats: bfloat16 [16, 16384, 512], P('batch', 'seq'), may hold values from -16 to 16
- hilbert_pos: int32 [16, 16384], P('batch', 'seq'), may hold values from 0 to 16383, as said below
- w_qkv: bfloat16 [512, 1536], P('seq'), may hold values from -2 to 2
- w_out: bfloat16 [512, 512], P('seq'), may hold values from -0.25 to 0.25
- grad_out: bfloat16 [16, 16384, 512], P('batch', 'seq'), may hold values from -6 to 6
Outputs:
- mixed_out: bfloat16 [16, 16384, 512], P('batch', 'seq')
- feat_grad: bfloat16 [16, 16384, 512], P('batch', 'seq')
- qkv_wgrad: float32 [512, 1536], P('seq')
- out_wgrad: float32 [512, 512], P('seq')
Inputs may be any that keep to these rules, and one draw needn't show every extreme that they name: `hilbert_pos`: each tile's row is a permutation of the tile's points. Of the 512 points of one aligned block (the points of one index of seq), at most 32 have positions in any one aligned block; every block keeps exactly 32 of its own points, and every block of a tile sends the same list of counts to the blocks 1, 2, ... places after it (cyclically).
All inputs are finite; a program needn't handle non-finite values.
Results may differ from a plain program's by a relative error of at most 0.034.
The roundings to bfloat16 on the way count: a program that leaves them out, or rounds other values in their place, can miss the bound.
Values may be sent and summed in bfloat16 or wider, within the bound.
No kernel may reach another device: no remote copies, remote signals or barrier semaphores. Data moves between devices by JAX's collectives and lax.ppermute only.
A program may use at most 64 MiB of HBM per device.

v0:
```python
import math

import jax
import jax.numpy as jnp
from jax import lax
from jax.sharding import PartitionSpec as P

HEADS = 32
HEAD_CHANNELS = 16
PATCH = 128


eps = 1e-05


def layer_norm(tile_rows):
    row_mean = jnp.mean(tile_rows, axis=-1, keepdims=True)
    centred = tile_rows - row_mean
    spread = jnp.mean(centred * centred, axis=-1, keepdims=True)
    inv_scale = lax.rsqrt(spread + eps)
    return (centred * inv_scale, inv_scale)


def heads_first(matrix):
    stacked = matrix.reshape(matrix.shape[0] // PATCH, PATCH, HEADS, HEAD_CHANNELS).transpose(
        2, 0, 1, 3
    )
    return stacked.reshape(HEADS // 4, 4 * stacked.shape[1], PATCH, HEAD_CHANNELS)


def heads_last(grouped):
    stacked = grouped.reshape(HEADS, grouped.shape[1] // 4, PATCH, HEAD_CHANNELS)
    return stacked.transpose(1, 2, 0, 3).reshape(stacked.shape[1] * PATCH, HEADS * HEAD_CHANNELS)


def attn_probs(query_matrix, key_matrix):
    score_matrix = jnp.einsum(
        "nld,nmd->nlm", query_matrix, key_matrix, preferred_element_type=jnp.float32
    ) * HEAD_CHANNELS ** (-0.5)
    return jax.nn.softmax(score_matrix, axis=-1)


def head_forward(operands):
    query_matrix, key_matrix, value_matrix = operands
    weights_p = attn_probs(query_matrix, key_matrix).astype(jnp.bfloat16)
    return jnp.einsum(
        "nlm,nmd->nld", weights_p, value_matrix, preferred_element_type=jnp.float32
    ).astype(jnp.bfloat16)


def head_backward(operands):
    query_matrix, key_matrix, value_matrix, incoming_gradient = operands
    probability_table = attn_probs(query_matrix, key_matrix)
    value_gradient = jnp.einsum(
        "nlm,nld->nmd",
        probability_table.astype(jnp.bfloat16),
        incoming_gradient,
        preferred_element_type=jnp.float32,
    ).astype(jnp.bfloat16)
    probability_gradient = jnp.einsum(
        "nld,nmd->nlm", incoming_gradient, value_matrix, preferred_element_type=jnp.float32
    )
    score_gradient = (
        probability_table
        * (
            probability_gradient
            - jnp.sum(probability_table * probability_gradient, axis=-1, keepdims=True)
        )
        * HEAD_CHANNELS ** (-0.5)
    ).astype(jnp.bfloat16)
    query_gradient = jnp.einsum(
        "nlm,nmd->nld", score_gradient, key_matrix, preferred_element_type=jnp.float32
    ).astype(jnp.bfloat16)
    key_gradient = jnp.einsum(
        "nlm,nld->nmd", score_gradient, query_matrix, preferred_element_type=jnp.float32
    ).astype(jnp.bfloat16)
    return (query_gradient, key_gradient, value_gradient)


def contract(left, right):
    return lax.dot_general(
        left, right, (((0,), (0,)), ((), ())), preferred_element_type=jnp.float32
    )


def against(left, right):
    return lax.dot_general(
        left, right, (((1,), (1,)), ((), ())), preferred_element_type=jnp.float32
    )


def local(feats, hilbert_pos, w_qkv, w_out, grad_out):
    points = feats.shape[1]
    feature_width = feats.shape[2]
    shards = lax.axis_size("seq")
    capacity = 2 * points // shards
    factor = 1.0 / math.sqrt(feats.shape[0] * lax.axis_size("batch") * points * shards)
    target = hilbert_pos[0]
    owner_dev = target // points
    local_place = target % points
    onehot = (owner_dev[:, None] == jnp.arange(shards)[None, :]).astype(jnp.int32)
    bucket_rank = jnp.sum((jnp.cumsum(onehot, axis=0) - onehot) * onehot, axis=1)
    send_slot = owner_dev * capacity + bucket_rank
    send_rows = (
        jnp.zeros((shards * capacity, feature_width), jnp.bfloat16).at[send_slot].set(feats[0])
    )
    send_place = jnp.full((shards * capacity,), points, jnp.int32).at[send_slot].set(local_place)
    got_rows, got_place = (
        lax.all_to_all(
            send_rows.reshape(shards, capacity, feature_width),
            "seq",
            split_axis=0,
            concat_axis=0,
            tiled=True,
        ),
        lax.all_to_all(
            send_place.reshape(shards, capacity), "seq", split_axis=0, concat_axis=0, tiled=True
        ),
    )
    got_place = got_place.reshape(shards * capacity)
    hilbert = (
        jnp.zeros((points + 1, feature_width), jnp.bfloat16)
        .at[got_place]
        .set(got_rows.reshape(shards * capacity, feature_width))[:points]
    )
    hilbert_full = hilbert.astype(jnp.float32)
    qkv_full, out_full = (
        lax.all_gather(w_qkv, "seq", axis=0, tiled=True),
        lax.all_gather(w_out, "seq", axis=0, tiled=True),
    )
    normal_rows, inv_scale = layer_norm(hilbert_full)
    normed = normal_rows.astype(jnp.bfloat16)
    qkv_rows = jnp.dot(normed, qkv_full, preferred_element_type=jnp.float32).astype(jnp.bfloat16)
    query_matrix = heads_first(qkv_rows[:, :feature_width])
    key_matrix = heads_first(qkv_rows[:, feature_width : 2 * feature_width])
    value_matrix = heads_first(qkv_rows[:, 2 * feature_width :])
    context_rows = heads_last(lax.map(head_forward, (query_matrix, key_matrix, value_matrix)))
    mixed_out = (
        hilbert_full + jnp.dot(context_rows, out_full, preferred_element_type=jnp.float32)
    ).astype(jnp.bfloat16)
    incoming_gradient = grad_out[0]
    ctx_grad = against(incoming_gradient, out_full).astype(jnp.bfloat16)
    query_gradient, key_gradient, value_gradient = lax.map(
        head_backward, (query_matrix, key_matrix, value_matrix, heads_first(ctx_grad))
    )
    qkv_grad = jnp.concatenate(
        [heads_last(query_gradient), heads_last(key_gradient), heads_last(value_gradient)], axis=1
    )
    normed_grad = against(qkv_grad, qkv_full)
    centre_grad = normed_grad - jnp.mean(normed_grad, axis=-1, keepdims=True)
    centre_grad = centre_grad - normal_rows * jnp.mean(
        normed_grad * normal_rows, axis=-1, keepdims=True
    )
    hilbert_grad = (incoming_gradient.astype(jnp.float32) + inv_scale * centre_grad).astype(
        jnp.bfloat16
    )
    padded_grad = jnp.concatenate(
        [hilbert_grad, jnp.zeros((1, feature_width), jnp.bfloat16)], axis=0
    )
    back_rows = padded_grad[got_place].reshape(shards, capacity, feature_width)
    returned = lax.all_to_all(back_rows, "seq", split_axis=0, concat_axis=0, tiled=True)
    feat_grad = returned.reshape(shards * capacity, feature_width)[send_slot]
    grad_term = (
        jnp.concatenate(
            [contract(normed, qkv_grad), contract(context_rows, incoming_gradient)], axis=1
        )
        * factor
    )
    summed = lax.psum(grad_term, "batch")
    grad_share = lax.psum_scatter(summed, "seq", scatter_dimension=0, tiled=True)
    qkv_wgrad = grad_share[:, : 3 * feature_width]
    out_wgrad = grad_share[:, 3 * feature_width :]
    return (mixed_out[None], feat_grad[None], qkv_wgrad, out_wgrad)


def solution(mesh):
    placed = (
        P("batch", "seq", None),
        P("batch", "seq"),
        P("seq", None),
        P("seq", None),
        P("batch", "seq", None),
    )
    return jax.shard_map(
        local,
        mesh=mesh,
        in_specs=placed,
        out_specs=(
            P("batch", "seq", None),
            P("batch", "seq", None),
            P("seq", None),
            P("seq", None),
        ),
        check_vma=False,
    )
```

profile of v0, /device:TPU:1, one launch (start us, length us, event | category | flops | bytes accessed | tf_op | source)
XLA Modules:
  0.0 619.2 jit_solution(14623042384082524313)
XLA Ops:
  14.7 13.7 %all-to-all-start = ((s32[32,1,32]{2,1,0:T(1,128)}), s32[32,1,32]{2,1,0:T(1,128)S(1)}, u32[]{:S(2)}, u32[]{:S(2)}) async-start(s32[32,1,32]{2,1,0:T(1,128)} %all_to_all.12), calls=%async_computation | async-start | bytes 32768 | tf_op jit(solution)/shard_map/all_to_all | solution.py:116
  28.4 3.5 scatter_custom_fusion.1
  32.0 5.0 all-to-all-done
  37.0 4.7 all-to-all-start.1
  41.7 58.2 %all_gather.7 = bf16[512,512]{1,0:T(8,128)(2,1)S(1)} all-gather(bf16[16,512]{1,0:T(8,128)(2,1)S(1)} %copy-done.7), channel_id=1, replica_groups=mesh['seq'=32,'batch'=16] {'seq'}, dimensions={0}, use_global_device_ids=true | all-gather | bytes 540672 | tf_op jit(solution)/shard_map/all_gather | solution.py:129
  103.0 5.8 scatter_custom_fusion.2
  119.5 35.5 %while.24 = (s32[]{:T(128)}, bf16[8,16,128,16]{2,3,1,0:T(8,128)(2,1)}, bf16[8,16,128,16]{2,3,1,0:T(8,128)(2,1)}, bf16[8,16,128,16]{2,3,1,0:T(8,128)(2,1)}, bf16[8,16,128,16]{2,3,1,0:T(8,128)(2,1)}, /*index=5*/s32[]{:T(128)}) while((s32[]{:T(128)}, bf16[8,16,128,16]{2,3,1,0:T(8,128)(2,1)}, bf16[8,16,128,16]{2,3,1,0:T(8,128)(2,1)}, ...), condition=%wide.region_11.12_spmd, body=%wide.region_8.11_spmd.sunk | while | flops 27035904 | bytes 3558477 | solution.py:137
  159.7 89.1 %while.25 = (s32[]{:T(128)}, bf16[8,16,128,16]{2,3,1,0:T(8,128)(2,1)}, bf16[8,16,128,16]{2,3,1,0:T(8,128)(2,1)}, bf16[8,16,128,16]{2,3,1,0:T(8,128)(2,1)}, bf16[...) while((s32[]{:T(128)}, ...), condition=%wide.region_16.17_spmd, body=%wide.region_12.16_spmd.sunk | while | flops 55941632 | bytes 11327589 | solution.py:143
  166.0 2.7 fusion.196
  174.4 2.7 fusion.195
  177.1 2.7 fusion.196
  188.2 2.7 fusion.196
  199.4 2.7 fusion.196
  207.8 2.7 fusion.195
  219.0 2.7 fusion.195
  221.7 2.7 fusion.196
  230.2 2.7 fusion.195
  232.8 2.7 fusion.196
  244.0 2.7 fusion.196
  256.6 3.2 fusion.129
  260.3 5.1 gather_fusion
  265.3 8.4 %all-to-all-start.2 = ((bf16[32,32,512]{2,1,0:T(8,128)(2,1)}), bf16[32,32,512]{2,1,0:T(8,128)(2,1)S(1)}, u32[]{:S(2)}, u32[]{:S(2)}) async-start(bf16[32,32,512]{2,1,0:T(8,128)(2,1)} %bitcast.39), calls=%async_computation.2 | async-start | bytes 2097152 | tf_op jit(solution)/shard_map/all_to_all | solution.py:161
  273.8 217.9 %reduce-scatter.2.cloned.1.call-done = f32[16,2048]{1,0:T(8,128)} async-done(((f32[512,2048]{1,0:T(8,128)}), f32[16,2048]{1,0:T(8,128)}) %reduce-scatter.2.cloned.1.call-update) | async-done | bytes 131088 | tf_op jit(solution)/shard_map/reduce_scatter | solution.py:170
  495.5 114.2 %all-reduce.3.cloned.1.call-done = f32[16,2048]{1,0:T(8,128)} async-done(((f32[16,2048]{1,0:T(8,128)}), f32[16,2048]{1,0:T(8,128)}) %all-reduce.3.cloned.1.call-update) | async-done | bytes 131088 | tf_op jit(solution)/shard_map/psum | solution.py:169
  (135 shorter events, 136.0 us)
Async XLA Ops:
  7.2 21.3 %copy-start = (bf16[1,512,512]{2,1,0:T(8,128)(2,1)S(1)}, bf16[1,512,512]{2,1,0:T(8,128)(2,1)}, u32[]{:S(2)}) copy-start(bf16[1,512,512]{2,1,0:T(8,128)(2,1)} %param.9) | copy-start | bytes 1572868
  7.2 102.1 %all-gather.2.cloned.1.call-start = ((), (), s32[]{:S(2)}) async-start(), calls=%async_computation.4 | async-start | bytes 1622016 | tf_op jit(solution)/shard_map/all_gather | solution.py:128
  14.7 22.3 %all-to-all-start = ((s32[32,1,32]{2,1,0:T(1,128)}), s32[32,1,32]{2,1,0:T(1,128)S(1)}, u32[]{:S(2)}, u32[]{:S(2)}) async-start(s32[32,1,32]{2,1,0:T(1,128)} %all_to_all.12), calls=%async_computation | async-start | bytes 32768 | tf_op jit(solution)/shard_map/all_to_all | solution.py:116
  28.4 13.3 %copy-start.7 = (bf16[16,512]{1,0:T(8,128)(2,1)S(1)}, bf16[16,512]{1,0:T(8,128)(2,1)}, u32[]{:S(2)}) copy-start(bf16[16,512]{1,0:T(8,128)(2,1)} %param.12) | copy-start | bytes 49156
  32.0 67.9 %copy-start.1 = (bf16[1,512,512]{2,1,0:T(8,128)(2,1)S(1)}, bf16[1,512,512]{2,1,0:T(8,128)(2,1)}, u32[]{:S(2)}) copy-start(bf16[1,512,512]{2,1,0:T(8,128)(2,1)} %param.13) | copy-start | bytes 1572868
  37.0 66.0 %all-to-all-start.1 = ((bf16[32,32,512]{2,1,0:T(8,128)(2,1)}), bf16[32,32,512]{2,1,0:T(8,128)(2,1)}, u32[]{:S(2)}, u32[]{:S(2)}) async-start(bf16[32,32,512]{2,1,0:T(8,128)(2,1)} %bitcast.19), calls=%async_computation.1 | async-start | bytes 2097152 | tf_op jit(solution)/shard_map/all_to_all | solution.py:109
  41.7 450.0 %reduce-scatter.2.cloned.1.call-start = ((), (), s32[]{:S(2)}) async-start(), calls=%async_computation.5 | async-start | bytes 4325376 | tf_op jit(solution)/shard_map/reduce_scatter | solution.py:170
  248.8 1.5 copy-start.2
  248.8 1.7 copy-start.3
  250.2 1.0 copy-start.4
  251.8 1.2 copy-start.6
  265.3 226.3 %copy-start.5 = (bf16[32,4,128,16]{2,1,3,0:T(4,128)(2,1)S(1)}, bf16[32,4,128,16]{2,1,3,0:T(4,128)(2,1)}, u32[]{:S(2)}) copy-start(bf16[32,4,128,16]{2,1,3,0:T(4,128)(2,1)} %copy.43) | copy-start | bytes 1572868
  265.3 227.6 %all-to-all-start.2 = ((bf16[32,32,512]{2,1,0:T(8,128)(2,1)}), bf16[32,32,512]{2,1,0:T(8,128)(2,1)S(1)}, u32[]{:S(2)}, u32[]{:S(2)}) async-start(bf16[32,32,512]{2,1,0:T(8,128)(2,1)} %bitcast.39), calls=%async_computation.2 | async-start | bytes 2097152 | tf_op jit(solution)/shard_map/all_to_all | solution.py:161
  273.7 336.1 %all-reduce.3.cloned.1.call-start = ((), (), s32[]{:S(2)}) async-start(), calls=%async_computation.6 | async-start | bytes 262144 | tf_op jit(solution)/shard_map/psum | solution.py:169
Sparse Core Ops, SparseCore 0:
  11.2 87.5 all-gather.1
  256.7 234.8 reduce-scatter.1
  494.0 115.6 all-reduce.2
where the time goes:
time: 623 us; the launch traced here: 619 us
  waiting for transfers between devices  338 us (54%)
  matrix products  134 us (22%)
  blocking collectives  58.2 us (9%)
  local copies, waits for them, and re-layouts  41.3 us (7%)
  starting transfers between devices  26.9 us (4%)
  between operations  14.1 us (2%)
  other arithmetic  7.26 us (1%)
    reduce_scatter x1, waiting for transfers between devices, local(): lax.psum_scatter(summed, 'seq', scatter_dimension=0, tiled=True)  218 us
    psum x1, waiting for transfers between devices, local(): summed = lax.psum(grad_term, 'batch')  114 us
    all_gather x1, blocking collectives, local(): lax.all_gather(w_out, 'seq', axis=0, tiled=True)  58.2 us
    sub x16, matrix products, attn_probs(): return jax.nn.softmax(score_matrix, axis=-1)  29.9 us
    dot_general x8, matrix products, head_backward(): jnp.einsum('nlm,nld->nmd', score_gradient, query_matrix, preferred_elemen...  21.4 us
    dot_general x8, matrix products, head_backward(): jnp.einsum('nlm,nmd->nld', score_gradient, key_matrix, preferred_element_...  21.3 us
    dot_general x8, matrix products, head_backward(): jnp.einsum('nlm,nld->nmd', probability_table.astype(jnp.bfloat16), incomi...  17.7 us
    dot_general x8, matrix products, head_forward(): jnp.einsum('nlm,nmd->nld', weights_p, value_matrix, preferred_element_typ...  14.6 us
  transfers between devices with their start and end apart: 6, of which 3 were waited for; matrix products, arithmetic and copies ran while one was open for 5% of the time, Pallas kernels for 0%

commit v1 on v0

v1 whole, which is shorter than its diff:
```python
import functools
import math

import jax
import jax.numpy as jnp
from jax import lax
from jax.experimental import pallas as pl
from jax.experimental.pallas import tpu as pltpu
from jax.sharding import Mesh
from jax.sharding import PartitionSpec as P

HEADS = 32
HEAD_CHANNELS = 16
PATCH = 128
WIDTH = 512
POINTS = 512
SHARDS = 32
CAP = 32
SLOTS = SHARDS * CAP
LANES = 128
EPS = 1e-05
SCALE = HEAD_CHANNELS ** (-0.5)

BF = jnp.bfloat16
F32 = jnp.float32
SEQ = ("x", "z")
BATCH = ("y", "core")

FEAT_ROWS = 4 * CAP
POS_ROWS = CAP
W_ROWS = 8 * 16
SEND_ROWS = FEAT_ROWS + POS_ROWS + W_ROWS


def iota(shape, dim):
    return lax.broadcasted_iota(jnp.int32, shape, dim)


def onehot(condition):
    return jnp.where(condition, 1.0, 0.0).astype(BF)


def dot(left, right):
    return jnp.dot(left, right, preferred_element_type=F32)


def dot_t(left, right):
    return lax.dot_general(left, right, (((1,), (1,)), ((), ())), preferred_element_type=F32)


def pack_kernel(core_ref, pos_ref, feats_ref, wqkv_ref, wout_ref, out_ref, slot_ref):
    group = core_ref[0]
    target = pos_ref[...]
    owner = target // POINTS
    place = target % POINTS + 1
    mine = iota((SHARDS, POINTS), 0) == owner
    before = onehot(iota((POINTS, POINTS), 0) < iota((POINTS, POINTS), 1))
    ranks = dot(onehot(mine), before)
    rank = jnp.sum(jnp.where(mine, ranks, 0.0), axis=0, keepdims=True).astype(jnp.int32)
    slot = owner * CAP + rank
    slot_ref[...] = jnp.broadcast_to(slot, slot_ref.shape)
    place_of = onehot(iota((SLOTS, POINTS), 0) == slot)
    row = iota((LANES, POINTS), 0)
    digits = jnp.where(row == 0, place // 32, jnp.where(row == 1, place % 32, 0))
    pos = dot_t(place_of, digits.astype(F32).astype(BF)).astype(BF)
    out_ref[:, FEAT_ROWS : FEAT_ROWS + POS_ROWS, :] = pos.reshape(SHARDS, CAP, LANES)
    for c in range(4):
        rows = dot(place_of, feats_ref[:, c * LANES : (c + 1) * LANES]).astype(BF)
        out_ref[:, c * CAP : (c + 1) * CAP, :] = rows.reshape(SHARDS, CAP, LANES)
    base = FEAT_ROWS + POS_ROWS
    for part in range(4):
        for b in range(2):
            at = (2 * part + b) * 16
            lanes = pl.ds(pl.multiple_of(group * 256 + b * LANES, LANES), LANES)
            if part < 3:
                lanes = pl.ds(pl.multiple_of(group * 256 + part * WIDTH + b * LANES, LANES), LANES)
                piece = wqkv_ref[:, lanes]
            else:
                piece = wout_ref[:, lanes]
            out_ref[:, base + at : base + at + 16, :] = jnp.broadcast_to(
                piece[None], (SHARDS, 16, LANES)
            )


def main_kernel(
    core_ref,
    recv_ref,
    other_ref,
    gout_ref,
    mixed_ref,
    back_ref,
    keep_ref,
    send_ref,
    wqkv,
    wout,
    hil,
    nrm,
    qkv,
    cgrad,
    ctx_t,
    qg_t,
):
    group = core_ref[0]
    for part in range(4):
        for b in range(2):
            at = (2 * part + b) * 16
            mine = recv_ref[:, FEAT_ROWS + POS_ROWS + at : FEAT_ROWS + POS_ROWS + at + 16, :]
            theirs = other_ref[:, at : at + 16, :]
            for piece, g in ((mine, group), (theirs, 1 - group)):
                piece = piece.reshape(WIDTH, LANES)
                if part < 3:
                    wqkv[
                        :, pl.ds(pl.multiple_of(g * 256 + part * WIDTH + b * LANES, LANES), LANES)
                    ] = piece
                else:
                    wout[:, pl.ds(pl.multiple_of(g * 256 + b * LANES, LANES), LANES)] = piece
    pos = recv_ref[:, FEAT_ROWS : FEAT_ROWS + POS_ROWS, :].reshape(SLOTS, LANES)
    pick = onehot(iota((16, LANES), 0) == iota((16, LANES), 1))
    digits = dot_t(pick, pos)
    place_row = (digits[0:1] * 32.0 + digits[1:2]).astype(jnp.int32) - 1
    arrive = onehot(iota((POINTS, SLOTS), 0) == place_row)
    for c in range(4):
        got = recv_ref[:, c * CAP : (c + 1) * CAP, :].reshape(SLOTS, LANES)
        hil[:, c * LANES : (c + 1) * LANES] = dot(arrive, got)
    rows = hil[...]
    centred = rows - jnp.mean(rows, axis=-1, keepdims=True)
    inv_scale = lax.rsqrt(jnp.mean(centred * centred, axis=-1, keepdims=True) + EPS)
    normed = (centred * inv_scale).astype(BF)
    nrm[...] = normed
    for part in range(6):
        cols = slice(part * 256, (part + 1) * 256)
        qkv[:, cols] = dot(normed, wqkv[:, cols]).astype(BF)
    cgrad[...] = dot_t(gout_ref[...], wout[...]).astype(BF)

    lane_head = iota((1, LANES), 1) // HEAD_CHANNELS

    def unit(u, carry):
        p = u // 4
        o = u % 4
        pts = pl.ds(pl.multiple_of(p * PATCH, PATCH), PATCH)
        lane = lambda part: pl.ds(pl.multiple_of(o * LANES + part * WIDTH, LANES), LANES)
        qs = qkv[pts, lane(0)] * BF(SCALE)
        k = qkv[pts, lane(1)]
        v = qkv[pts, lane(2)]
        dc = cgrad[pts, lane(0)]
        qs_t = qs.T
        ks_t = (k * BF(SCALE)).T
        v_t = v.T
        dc_t = dc.T
        for h in range(8):
            head = jnp.where(lane_head == h, 1.0, 0.0).astype(BF)
            chans = slice(h * HEAD_CHANNELS, (h + 1) * HEAD_CHANNELS)
            scores = dot_t(k * head, qs)
            exps = jnp.exp(scores - jnp.max(scores, axis=0, keepdims=True))
            probs = exps * (1.0 / jnp.sum(exps, axis=0, keepdims=True))
            probs_b = probs.astype(BF)
            prob_grad = dot_t(v * head, dc)
            total = jnp.sum(probs * prob_grad, axis=0, keepdims=True)
            score_grad = (probs * (prob_grad - total)).astype(BF)
            at = lambda part: pl.ds(
                pl.multiple_of(o * LANES + part * WIDTH + h * HEAD_CHANNELS, HEAD_CHANNELS),
                HEAD_CHANNELS,
            )
            ctx_t[at(0), pts] = dot(v_t[chans], probs_b).astype(BF)
            qg_t[at(0), pts] = dot(ks_t[chans], score_grad).astype(BF)
            qg_t[at(1), pts] = dot_t(qs_t[chans], score_grad).astype(BF)
            qg_t[at(2), pts] = dot_t(dc_t[chans], probs_b).astype(BF)
        return carry

    lax.fori_loop(0, 16, unit, 0)

    mixed_ref[...] = (hil[...] + dot(ctx_t[...].T, wout[...])).astype(BF)
    normed_t = nrm[...].T
    for g, ref in ((1 - group, send_ref), (group, keep_ref)):
        for part in range(3):
            chans = pl.ds(pl.multiple_of(g * 256 + part * WIDTH, 256), 256)
            term = dot_t(normed_t, qg_t[chans, :]).astype(BF)
            ref[2 * part] = term[:, :LANES]
            ref[2 * part + 1] = term[:, LANES:]
        cols = pl.ds(pl.multiple_of(g * 256, 256), 256)
        term = dot(ctx_t[...], gout_ref[:, cols]).astype(BF)
        ref[6] = term[:, :LANES]
        ref[7] = term[:, LANES:]
    rows = hil[...]
    centred = rows - jnp.mean(rows, axis=-1, keepdims=True)
    inv_scale = lax.rsqrt(jnp.mean(centred * centred, axis=-1, keepdims=True) + EPS)
    xhat = centred * inv_scale
    ngrad = dot(wqkv[...], qg_t[...]).T
    cent = ngrad - jnp.mean(ngrad, axis=-1, keepdims=True)
    cent = cent - xhat * jnp.mean(ngrad * xhat, axis=-1, keepdims=True)
    hgrad = (gout_ref[...].astype(F32) + inv_scale * cent).astype(BF)
    wide = pos.astype(F32)
    place_col = (wide[:, 0:1] * 32.0 + wide[:, 1:2]).astype(jnp.int32) - 1
    leave = onehot(iota((SLOTS, POINTS), 1) == place_col)
    for c in range(4):
        out = dot(leave, hgrad[:, c * LANES : (c + 1) * LANES]).astype(BF)
        back_ref[:, c * CAP : (c + 1) * CAP, :] = out.reshape(SHARDS, CAP, LANES)


def unpack_kernel(slot_ref, back_ref, out_ref):
    slot = slot_ref[0:1, :]
    row = iota((LANES, POINTS), 0)
    digits = jnp.where(row == 0, slot // 32, jnp.where(row == 1, slot % 32, 0))
    eye = onehot(iota((POINTS, POINTS), 0) == iota((POINTS, POINTS), 1))
    cols = dot_t(eye, digits.astype(F32).astype(BF))
    slot_col = (cols[:, 0:1] * 32.0 + cols[:, 1:2]).astype(jnp.int32)
    take = onehot(iota((POINTS, SLOTS), 1) == slot_col)
    for c in range(4):
        got = back_ref[:, c * CAP : (c + 1) * CAP, :].reshape(SLOTS, LANES)
        out_ref[:, c * LANES : (c + 1) * LANES] = dot(take, got).astype(BF)


VMEM = pl.BlockSpec(memory_space=pltpu.VMEM)
SMEM = pl.BlockSpec(memory_space=pltpu.SMEM)


def params(mib):
    return pltpu.CompilerParams(vmem_limit_bytes=mib * 1024 * 1024)


def exchange(array, axes):
    return lax.all_to_all(array, axes, split_axis=0, concat_axis=0, tiled=True)


def local(feats, hilbert_pos, w_qkv, w_out, grad_out):
    core = lax.axis_index("core").astype(jnp.int32)[None]
    send, slot = pl.pallas_call(
        pack_kernel,
        out_shape=(
            jax.ShapeDtypeStruct((SHARDS, SEND_ROWS, LANES), BF),
            jax.ShapeDtypeStruct((8, POINTS), jnp.int32),
        ),
        in_specs=[SMEM, VMEM, VMEM, VMEM, VMEM],
        out_specs=(VMEM, VMEM),
        compiler_params=params(32),
        name="pack",
    )(core, hilbert_pos, feats[0], w_qkv, w_out)
    recv = exchange(send, SEQ)
    swap = [(0, 1), (1, 0)]
    other = lax.ppermute(recv[:, FEAT_ROWS + POS_ROWS :, :], "core", swap)
    gout = grad_out[0]
    mixed, back, keep, give = pl.pallas_call(
        main_kernel,
        out_shape=(
            jax.ShapeDtypeStruct((POINTS, WIDTH), BF),
            jax.ShapeDtypeStruct((SHARDS, FEAT_ROWS, LANES), BF),
            jax.ShapeDtypeStruct((8, WIDTH, LANES), BF),
            jax.ShapeDtypeStruct((8, WIDTH, LANES), BF),
        ),
        in_specs=[SMEM, VMEM, VMEM, VMEM],
        out_specs=(VMEM, VMEM, VMEM, VMEM),
        scratch_shapes=[
            pltpu.VMEM((WIDTH, 3 * WIDTH), BF),
            pltpu.VMEM((WIDTH, WIDTH), BF),
            pltpu.VMEM((POINTS, WIDTH), F32),
            pltpu.VMEM((POINTS, WIDTH), BF),
            pltpu.VMEM((POINTS, 3 * WIDTH), BF),
            pltpu.VMEM((POINTS, WIDTH), BF),
            pltpu.VMEM((WIDTH, POINTS), BF),
            pltpu.VMEM((3 * WIDTH, POINTS), BF),
        ],
        compiler_params=params(50),
        name="attention",
    )(core, recv, other, gout)
    returned = exchange(back, SEQ)
    theirs = lax.ppermute(give, "core", swap)
    pair = (keep.astype(F32) + theirs.astype(F32)).astype(BF)
    by_y = exchange(pair, "y")
    share = jnp.sum(by_y.astype(F32), axis=0).astype(BF)
    by_seq = exchange(share.reshape(SHARDS, WIDTH // SHARDS, LANES), SEQ)
    factor = 1.0 / math.sqrt(16 * POINTS * SHARDS)
    total = jnp.sum(by_seq.astype(F32), axis=0) * factor
    whole = exchange(jnp.broadcast_to(total[None], (16,) + total.shape), BATCH)
    whole = whole.reshape(4, 2, 2, WIDTH // SHARDS, LANES)
    cols = whole.transpose(3, 0, 2, 1, 4).reshape(WIDTH // SHARDS, 4 * WIDTH)
    feat_grad = pl.pallas_call(
        unpack_kernel,
        out_shape=jax.ShapeDtypeStruct((POINTS, WIDTH), BF),
        in_specs=[VMEM, VMEM],
        out_specs=VMEM,
        compiler_params=params(32),
        name="unpack",
    )(slot, returned)
    return (mixed[None], feat_grad[None], cols[:, : 3 * WIDTH], cols[:, 3 * WIDTH :])


def solution(mesh):
    mesh = Mesh(mesh.devices.reshape(4, 8, 8, 2), ("x", "z", "y", "core"))
    rows = P(BATCH, SEQ, None)
    return jax.shard_map(
        local,
        mesh=mesh,
        in_specs=(rows, P(BATCH, SEQ), P(SEQ, None), P(SEQ, None), rows),
        out_specs=(rows, rows, P(SEQ, None), P(SEQ, None)),
        check_vma=False,
    )
```

time: 623 us -> 232 us (0.37)
  waiting for transfers between devices: 338 us -> 33 us
  matrix products: 134 us -> 0 us
  blocking collectives: 58.2 us -> 116 us
  Pallas kernels: 0 us -> 51.3 us
  local copies, waits for them, and re-layouts: 41.3 us -> 6.48 us
  between operations: 14.1 us -> 0.73 us
  other arithmetic: 7.26 us -> 0.46 us
    reduce_scatter x1 -> x0, waiting for transfers between devices: 218 us -> none  [local(): lax.psum_scatter(summed, 'seq', scatter_dimension=0, tiled=True)]
    all_to_all x0 -> x3, blocking collectives: none -> 116 us  [exchange(): return lax.all_to_all(array, axes, split_axis=0, concat_axis=0, tiled=True)]
    psum x1 -> x0, waiting for transfers between devices: 114 us -> none  [local(): summed = lax.psum(grad_term, 'batch')]
    dot_general x54 -> x0, matrix products: 104 us -> none  [the longest x8 21.4 us: head_backward(): jnp.einsum('nlm,nld->nmd', score_gradient, query_matrix, preferred_elemen...]
    all_gather x1 -> x0, blocking collectives: 58.2 us -> none  [local(): lax.all_gather(w_out, 'seq', axis=0, tiled=True)]
    pallas_call x0 -> x3, Pallas kernels: none -> 51.3 us  [the longest x1 47.1 us: local(): pl.pallas_call(main_kernel, out_shape=(jax.ShapeDtypeStruct((POINTS, WIDT...]
    sub x16 -> x0, matrix products: 29.9 us -> none  [attn_probs(): return jax.nn.softmax(score_matrix, axis=-1)]
    all_to_all x3 -> x2, waiting for transfers between devices: 5.01 us -> 28.5 us  [exchange(): return lax.all_to_all(array, axes, split_axis=0, concat_axis=0, tiled=True)]
  transfers between devices with their start and end apart: 6 -> 4, of which waited for: 3 -> 4; matrix products, arithmetic and copies ran while one was open for 5% -> 0% of each run, Pallas kernels for 0% -> 1%
where the time goes in v1:
time: 232 us; the launch traced here: 231 us
  blocking collectives  116 us (50%)
  Pallas kernels  51.3 us (22%)
  waiting for transfers between devices  33 us (14%)
  starting transfers between devices  23 us (10%)
  local copies, waits for them, and re-layouts  6.48 us (3%)
    all_to_all x3, blocking collectives, exchange(): return lax.all_to_all(array, axes, split_axis=0, concat_axis=0, tiled=True)  116 us
    pallas_call x1, Pallas kernels, local(): pl.pallas_call(main_kernel, out_shape=(jax.ShapeDtypeStruct((POINTS, WIDT...  47.1 us
    all_to_all x2, waiting for transfers between devices, exchange(): return lax.all_to_all(array, axes, split_axis=0, concat_axis=0, tiled=True)  28.5 us
    all_to_all x2, starting transfers between devices, exchange(): return lax.all_to_all(array, axes, split_axis=0, concat_axis=0, tiled=True)  15.1 us
    ppermute x1, starting transfers between devices, local(): other = lax.ppermute(recv[:, FEAT_ROWS + POS_ROWS:, :], 'core', swap)  5.61 us
  transfers between devices with their start and end apart: 4, of which 4 were waited for; matrix products, arithmetic and copies ran while one was open for 0% of the time, Pallas kernels for 1%

profile of v1, /device:TPU:1, one launch (start us, length us, event | category | flops | bytes accessed | tf_op | source)
XLA Modules:
  0.0 230.9 jit_solution(16663146982242898548)
XLA Ops:
  0.6 1.0 copy-done.1
  1.7 0.8 copy-done.2
  2.5 0.7 copy-done.3
  3.2 0.7 copy-done.4
  3.9 1.8 pack.1
  5.7 68.4 %all_to_all.25.recv_ref = bf16[32,288,128]{2,1,0:T(8,128)(2,1)S(1)} all-to-all(bf16[32,288,128]{2,1,0:T(8,128)(2,1)S(1)} %get-tuple-element.10), channel_id=1, replica_groups=mesh['x'=4,'z'=8,'y'=8,'core'=2] {'x','z'}, dimensions={0} | all-to-all | bytes 4718592 | tf_op jit(solution)/shard_map/all_to_all | solution.py:222
  74.2 5.6 %collective-permute-start = (bf16[32,128,128]{2,1,0:T(8,128)(2,1)S(1)}, bf16[32,128,128]{2,1,0:T(8,128)(2,1)S(1)}, u32[]{:S(2)}, u32[]{:S(2)}) collective-permute-start(bf16[32,128,128]{2,1,0:T(8,128)(2,1)S(1)} %slice.12), channel_id=1, source_target_pairs={{0,1},{1,0},{2,3},{3,2},{4,5},{5,4},{6,7},{7,6},{8,9},{9,8},{10,11... | collective-permute-start | bytes 3145736 | tf_op jit(solution)/shard_map/ppermute | solution.py:240
  79.9 2.3 collective-permute-done.other_ref
  82.1 1.0 copy-done.6
  83.1 47.1 %attention.1 = (bf16[512,512]{1,0:T(8,128)(2,1)}, bf16[32,128,128]{2,1,0:T(8,128)(2,1)}, bf16[8,512,128]{2,1,0:T(8,128)(2,1)S(1)}, bf16[8,512,128]{2,1,0:T(8,128)(2,1)S(1)}) custom-call(s32[1]{0:T(128)} %bitcast.core_ref, bf16[32,288,128]{2,1,0:T(8,128)(2,1)} %copy-done.5, bf16[32,128,128]{2,1,0:T(8,128)(2,1)} %copy-done.6, bf16[512,512]{1,0:T(8,128)(2,1)S(1)} %bitcast.9), custom_call_target="tpu_custom_call" | custom-call | tf_op jit(solution)/shard_map/attention/pallas_call | solution.py:242
  130.2 2.3 collective-permute-start.1
  132.5 2.3 collective-permute-done.1
  134.8 0.3 add_convert_fusion
  135.0 34.5 %all_to_all.26 = bf16[8,512,128]{2,1,0:T(8,128)(2,1)S(1)} all-to-all(bf16[8,512,128]{2,1,0:T(8,128)(2,1)S(1)} %add_convert_fusion), channel_id=1, replica_groups=mesh['x'=4,'z'=8,'y'=8,'core'=2] {'y'}, dimensions={0} | all-to-all | bytes 2097152 | tf_op jit(solution)/shard_map/all_to_all | solution.py:222
  169.6 0.1 reduce_sum.21
  169.7 13.0 %all_to_all.27 = bf16[32,16,128]{2,1,0:T(8,128)(2,1)S(1)} all-to-all(bf16[32,16,128]{2,1,0:T(8,128)(2,1)S(1)} %bitcast.12), channel_id=1, replica_groups=mesh['x'=4,'z'=8,'y'=8,'core'=2] {'x','z'}, dimensions={0} | all-to-all | bytes 262144 | tf_op jit(solution)/shard_map/all_to_all | solution.py:222
  182.7 3.9 %all-to-all-start.1 = ((bf16[32,128,128]{2,1,0:T(8,128)(2,1)}), bf16[32,128,128]{2,1,0:T(8,128)(2,1)S(1)}, u32[]{:S(2)}, u32[]{:S(2)}) async-start(bf16[32,128,128]{2,1,0:T(8,128)(2,1)} %get-tuple-element.13), calls=%async_computation.1 | async-start | bytes 2097152 | tf_op jit(solution)/shard_map/all_to_all | solution.py:222
  186.7 21.7 %all-to-all-done.1.back_ref = bf16[32,128,128]{2,1,0:T(8,128)(2,1)S(1)} async-done(((bf16[32,128,128]{2,1,0:T(8,128)(2,1)}), bf16[32,128,128]{2,1,0:T(8,128)(2,1)S(1)}, u32[]{:S(2)}, u32[]{:S(2)}) %all-to-all-start.1) | async-done | bytes 1048608 | tf_op jit(solution)/shard_map/all_to_all | solution.py:222
  208.4 0.7 broadcast_in_dim.18
  209.1 11.2 %all-to-all-start.4 = ((f32[16,16,128]{2,1,0:T(8,128)}), f32[16,16,128]{2,1,0:T(8,128)S(1)}, u32[]{:S(2)}, u32[]{:S(2)}) async-start(f32[16,16,128]{2,1,0:T(8,128)} %broadcast_in_dim.18), calls=%async_computation.4 | async-start | bytes 262144 | tf_op jit(solution)/shard_map/all_to_all | solution.py:222
  220.2 2.4 %unpack.1 = bf16[512,512]{1,0:T(8,128)(2,1)} custom-call(s32[8,512]{1,0:T(8,128)S(1)} %get-tuple-element.12.slot_ref, bf16[32,128,128]{2,1,0:T(8,128)(2,1)S(1)} %all-to-all-done.1.back_ref), custom_call_target="tpu_custom_call" | custom-call | tf_op jit(solution)/shard_map/unpack/pallas_call | solution.py:276
  222.7 6.8 %all-to-all-done.4 = f32[16,16,128]{2,1,0:T(8,128)S(1)} async-done(((f32[16,16,128]{2,1,0:T(8,128)}), f32[16,16,128]{2,1,0:T(8,128)S(1)}, u32[]{:S(2)}, u32[]{:S(2)}) %all-to-all-start.4) | async-done | bytes 131104 | tf_op jit(solution)/shard_map/all_to_all | solution.py:222
  229.7 0.6 slice.14
  230.3 0.6 slice.13
  (14 shorter events, 0.4 us)
Async XLA Ops:
  0.6 1.0 copy-start.1
  1.7 0.8 copy-start.2
  2.5 0.7 copy-start.3
  3.2 0.7 copy-start.4
  74.1 8.0 %copy-start.5 = (bf16[32,288,128]{2,1,0:T(8,128)(2,1)}, bf16[32,288,128]{2,1,0:T(8,128)(2,1)S(1)}, u32[]{:S(2)}) copy-start(bf16[32,288,128]{2,1,0:T(8,128)(2,1)S(1)} %all_to_all.25.recv_ref) | copy-start | bytes 7077892
  74.1 9.0 %copy-start = (bf16[1,512,512]{2,1,0:T(8,128)(2,1)S(1)}, bf16[1,512,512]{2,1,0:T(8,128)(2,1)}, u32[]{:S(2)}) copy-start(bf16[1,512,512]{2,1,0:T(8,128)(2,1)} %param.9) | copy-start | bytes 1572868
  74.2 7.9 %collective-permute-start = (bf16[32,128,128]{2,1,0:T(8,128)(2,1)S(1)}, bf16[32,128,128]{2,1,0:T(8,128)(2,1)S(1)}, u32[]{:S(2)}, u32[]{:S(2)}) collective-permute-start(bf16[32,128,128]{2,1,0:T(8,128)(2,1)S(1)} %slice.12), channel_id=1, source_target_pairs={{0,1},{1,0},{2,3},{3,2},{4,5},{5,4},{6,7},{7,6},{8,9},{9,8},{10,11... | collective-permute-start | bytes 3145736 | tf_op jit(solution)/shard_map/ppermute | solution.py:240
  82.1 1.0 copy-start.6
  130.2 4.5 %collective-permute-start.1 = (bf16[8,512,128]{2,1,0:T(8,128)(2,1)S(1)}, bf16[8,512,128]{2,1,0:T(8,128)(2,1)S(1)}, u32[]{:S(2)}, u32[]{:S(2)}) collective-permute-start(bf16[8,512,128]{2,1,0:T(8,128)(2,1)S(1)} %get-tuple-element.15), channel_id=1, source_target_pairs={{0,1},{1,0},{2,3},{3,2},{4,5},{5,4},{6,7},{7,6},{8,9},{9,8},{10,11... | collective-permute-start | bytes 3145736 | tf_op jit(solution)/shard_map/ppermute | solution.py:266
  182.7 25.7 %all-to-all-start.1 = ((bf16[32,128,128]{2,1,0:T(8,128)(2,1)}), bf16[32,128,128]{2,1,0:T(8,128)(2,1)S(1)}, u32[]{:S(2)}, u32[]{:S(2)}) async-start(bf16[32,128,128]{2,1,0:T(8,128)(2,1)} %get-tuple-element.13), calls=%async_computation.1 | async-start | bytes 2097152 | tf_op jit(solution)/shard_map/all_to_all | solution.py:222
  209.1 20.4 %all-to-all-start.4 = ((f32[16,16,128]{2,1,0:T(8,128)}), f32[16,16,128]{2,1,0:T(8,128)S(1)}, u32[]{:S(2)}, u32[]{:S(2)}) async-start(f32[16,16,128]{2,1,0:T(8,128)} %broadcast_in_dim.18), calls=%async_computation.4 | async-start | bytes 262144 | tf_op jit(solution)/shard_map/all_to_all | solution.py:222

commit v2 on v1

v2 whole, which is shorter than its diff:
```python
import math

import jax
import jax.numpy as jnp
from jax import lax
from jax.experimental import pallas as pl
from jax.experimental.pallas import tpu as pltpu
from jax.sharding import Mesh
from jax.sharding import PartitionSpec as P

HEADS = 32
HEAD_CHANNELS = 16
PATCH = 128
WIDTH = 512
POINTS = 512
SHARDS = 32
CAP = 32
SLOTS = SHARDS * CAP
LANES = 128
EPS = 1e-05
SCALE = HEAD_CHANNELS ** (-0.5)

BF = jnp.bfloat16
F32 = jnp.float32
SEQ = ("x", "z")
BATCH = ("y", "core")

FEAT_ROWS = 4 * CAP
SEND_ROWS = FEAT_ROWS + 16
W_COLS = 1024


def iota(shape, dim):
    return lax.broadcasted_iota(jnp.int32, shape, dim)


def onehot(condition):
    return jnp.where(condition, 1.0, 0.0).astype(BF)


def dot(left, right):
    return jnp.dot(left, right, preferred_element_type=F32)


def dot_t(left, right):
    return lax.dot_general(left, right, (((1,), (1,)), ((), ())), preferred_element_type=F32)


def pack_kernel(pos_ref, feats_ref, out_ref, slot_ref):
    target = pos_ref[...]
    owner = target // POINTS
    place = target % POINTS + 1
    mine = iota((SHARDS, POINTS), 0) == owner
    mine_b = onehot(mine)
    before = onehot(iota((POINTS, POINTS), 0) < iota((POINTS, POINTS), 1))
    ranks = dot(mine_b, before)
    rank = jnp.sum(jnp.where(mine, ranks, 0.0), axis=0, keepdims=True).astype(jnp.int32)
    slot = owner * CAP + rank
    slot_ref[...] = jnp.broadcast_to(slot, slot_ref.shape)
    place_of = onehot(iota((SLOTS, POINTS), 0) == slot)
    lane = iota((LANES, POINTS), 0)
    digits = jnp.where(lane == rank, place // 32, 0) + jnp.where(lane == rank + CAP, place % 32, 0)
    pos = dot_t(mine_b, digits.astype(F32).astype(BF)).astype(BF)
    out_ref[:, FEAT_ROWS:SEND_ROWS, :] = jnp.broadcast_to(pos[:, None, :], (SHARDS, 16, LANES))
    for c in range(4):
        rows = dot(place_of, feats_ref[:, c * LANES : (c + 1) * LANES]).astype(BF)
        out_ref[:, c * CAP : (c + 1) * CAP, :] = rows.reshape(SHARDS, CAP, LANES)


def positions(recv_ref):
    return recv_ref[:, FEAT_ROWS:SEND_ROWS, :][:, 0, :]


def arrivals(digits):
    lane, slot = iota((LANES, SLOTS), 0), iota((LANES, SLOTS), 1) % CAP
    spread = jnp.where(lane == slot, 32.0, jnp.where(lane == slot + CAP, 1.0, 0.0)).astype(BF)
    each = dot(digits, spread)
    source = iota((SHARDS, SLOTS), 0) == iota((SHARDS, SLOTS), 1) // CAP
    place = jnp.sum(jnp.where(source, each, 0.0), axis=0, keepdims=True).astype(jnp.int32) - 1
    return onehot(iota((POINTS, SLOTS), 0) == place)


def departures(digits):
    source = onehot(iota((SLOTS, SHARDS), 0) // CAP == iota((SLOTS, SHARDS), 1))
    each = dot(source, digits)
    slot, lane = iota((SLOTS, LANES), 0) % CAP, iota((SLOTS, LANES), 1)
    weight = jnp.where(lane == slot, 32.0, jnp.where(lane == slot + CAP, 1.0, 0.0))
    place = jnp.sum(each * weight, axis=1, keepdims=True).astype(jnp.int32) - 1
    return onehot(iota((SLOTS, POINTS), 1) == place)


def block_kernel(
    at_ref,
    recv_hbm,
    mine0_hbm,
    mine1_hbm,
    mine2_hbm,
    mine3_hbm,
    other_hbm,
    gout_hbm,
    mixed_hbm,
    keep_hbm,
    send_hbm,
    back_hbm,
    recv,
    w,
    gout,
    mixed,
    keep,
    send,
    back,
    hil,
    nrm,
    nrm_t,
    qkv,
    cgrad,
    ctx_t,
    qg_t,
    sems,
):
    group, x = at_ref[0], at_ref[1]
    copies = []

    def start(source, target):
        copy = pltpu.make_async_copy(source, target, sems.at[len(copies)])
        copy.start()
        copies.append(copy)
        return copy

    recv_copy = start(recv_hbm, recv)
    w_copies = []
    for k, mine in enumerate((mine0_hbm, mine1_hbm, mine2_hbm, mine3_hbm)):
        rows = pl.ds(pl.multiple_of(lax.rem(x + 4 - k, 4) * 128, 128), 128)
        w_copies.append(start(mine, w.at[group, rows, :]))
        w_copies.append(start(other_hbm.at[k], w.at[1 - group, rows, :]))
    gout_copy = start(gout_hbm, gout)

    recv_copy.wait()
    digits = positions(recv)
    arrive = arrivals(digits)
    for c in range(4):
        got = recv[:, c * CAP : (c + 1) * CAP, :].reshape(SLOTS, LANES)
        hil[:, c * LANES : (c + 1) * LANES] = dot(arrive, got)
    rows = hil[...]
    centred = rows - jnp.mean(rows, axis=-1, keepdims=True)
    inv_scale = lax.rsqrt(jnp.mean(centred * centred, axis=-1, keepdims=True) + EPS)
    normed = (centred * inv_scale).astype(BF)
    nrm[...] = normed
    for copy in w_copies:
        copy.wait()
    for g in range(2):
        for part in range(3):
            cols = slice(part * 256, (part + 1) * 256)
            at = slice(g * 768 + part * 256, g * 768 + (part + 1) * 256)
            qkv[:, at] = dot(normed, w[g, :, cols]).astype(BF)
    gout_copy.wait()
    cgrad[...] = (
        dot_t(gout[:, :256], w[0, :, 768:]) + dot_t(gout[:, 256:], w[1, :, 768:])
    ).astype(BF)

    by_lane = iota((1, LANES), 1) // HEAD_CHANNELS
    by_row = iota((LANES, 1), 0) // HEAD_CHANNELS
    lane_heads = [jnp.where(by_lane == h, 1.0, 0.0).astype(BF) for h in range(8)]
    row_heads = [jnp.where(by_row == h, 1.0, 0.0).astype(BF) for h in range(8)]

    def stack(array):
        return jnp.concatenate([array * head for head in lane_heads], axis=0)

    def spread(array):
        return jnp.concatenate([array * head for head in row_heads], axis=1)

    def unit(u, carry):
        p = u // 4
        o = u % 4
        pts = pl.ds(pl.multiple_of(p * PATCH, PATCH), PATCH)
        first = (o // 2) * 768 + (o % 2) * LANES
        block = lambda part: pl.ds(pl.multiple_of(first + part * 256, LANES), LANES)
        whole = pl.ds(pl.multiple_of(o * LANES, LANES), LANES)
        qs = qkv[pts, block(0)] * BF(SCALE)
        k = qkv[pts, block(1)]
        v = qkv[pts, block(2)]
        dc = cgrad[pts, whole]
        all_scores = dot_t(stack(k), qs)
        all_prob_grads = dot_t(stack(v), dc)
        probs_b, score_grads = [], []
        for h in range(8):
            scores = all_scores[h * PATCH : (h + 1) * PATCH]
            prob_grad = all_prob_grads[h * PATCH : (h + 1) * PATCH]
            exps = jnp.exp(scores - jnp.max(scores, axis=0, keepdims=True))
            probs = exps * (1.0 / jnp.sum(exps, axis=0, keepdims=True))
            total = jnp.sum(probs * prob_grad, axis=0, keepdims=True)
            probs_b.append(probs.astype(BF))
            score_grads.append((probs * (prob_grad - total)).astype(BF))
        rows_p, cols_p = jnp.concatenate(probs_b, axis=0), jnp.concatenate(probs_b, axis=1)
        rows_s, cols_s = jnp.concatenate(score_grads, axis=0), jnp.concatenate(score_grads, axis=1)
        ctx_t[whole, pts] = dot(spread(v.T), rows_p).astype(BF)
        qg_t[block(0), pts] = dot(spread((k * BF(SCALE)).T), rows_s).astype(BF)
        qg_t[block(1), pts] = dot(cols_s, stack(qs)).astype(BF).T
        qg_t[block(2), pts] = dot(cols_p, stack(dc)).astype(BF).T
        return carry

    lax.fori_loop(0, 16, unit, 0, unroll=2)

    nrm_t[...] = nrm[...].T
    for g, ref, target in ((1 - group, send, send_hbm), (group, keep, keep_hbm)):
        for k in range(4):
            rows = pl.ds(pl.multiple_of(lax.rem(x + k, 4) * 128, 128), 128)
            for part in range(3):
                chans = pl.ds(pl.multiple_of(g * 768 + part * 256, 256), 256)
                term = dot_t(nrm_t[rows, :], qg_t[chans, :]).astype(BF)
                ref[k, 2 * part] = term[:, :LANES]
                ref[k, 2 * part + 1] = term[:, LANES:]
            cols = pl.ds(pl.multiple_of(g * 256, 256), 256)
            term = dot(ctx_t[rows, :], gout[:, cols]).astype(BF)
            ref[k, 6] = term[:, :LANES]
            ref[k, 7] = term[:, LANES:]
        start(ref, target)
    context = ctx_t[...].T
    for g in range(2):
        cols = slice(g * 256, (g + 1) * 256)
        mixed[:, cols] = (hil[:, cols] + dot(context, w[g, :, 768:])).astype(BF)
    start(mixed, mixed_hbm)
    rows = hil[...]
    centred = rows - jnp.mean(rows, axis=-1, keepdims=True)
    inv_scale = lax.rsqrt(jnp.mean(centred * centred, axis=-1, keepdims=True) + EPS)
    xhat = centred * inv_scale
    ngrad = (dot(w[0, :, :768], qg_t[:768, :]) + dot(w[1, :, :768], qg_t[768:, :])).T
    cent = ngrad - jnp.mean(ngrad, axis=-1, keepdims=True)
    cent = cent - xhat * jnp.mean(ngrad * xhat, axis=-1, keepdims=True)
    hgrad = (gout[...].astype(F32) + inv_scale * cent).astype(BF)
    leave = departures(digits)
    for c in range(4):
        out = dot(leave, hgrad[:, c * LANES : (c + 1) * LANES]).astype(BF)
        back[:, c * CAP : (c + 1) * CAP, :] = out.reshape(SHARDS, CAP, LANES)
    start(back, back_hbm)
    for copy in copies[-4:]:
        copy.wait()


def pair_kernel(keep_ref, theirs_ref, *out_refs):
    for k in range(4):
        out_refs[k][...] = (keep_ref[k].astype(F32) + theirs_ref[k].astype(F32)).astype(BF)


def unpack_kernel(slot_ref, back_ref, out_ref):
    slot = slot_ref[0:1, :]
    row = iota((LANES, POINTS), 0)
    digits = jnp.where(row == 0, slot // 32, jnp.where(row == 1, slot % 32, 0))
    eye = onehot(iota((POINTS, POINTS), 0) == iota((POINTS, POINTS), 1))
    cols = dot_t(eye, digits.astype(F32).astype(BF))
    slot_col = (cols[:, 0:1] * 32.0 + cols[:, 1:2]).astype(jnp.int32)
    take = onehot(iota((POINTS, SLOTS), 1) == slot_col)
    for c in range(4):
        got = back_ref[:, c * CAP : (c + 1) * CAP, :].reshape(SLOTS, LANES)
        out_ref[:, c * LANES : (c + 1) * LANES] = dot(take, got).astype(BF)


VMEM = pl.BlockSpec(memory_space=pltpu.VMEM)
SMEM = pl.BlockSpec(memory_space=pltpu.SMEM)
ANY = pl.BlockSpec(memory_space=pl.ANY)


def params(mib):
    return pltpu.CompilerParams(vmem_limit_bytes=mib * 1024 * 1024)


def exchange(array, axes):
    return lax.all_to_all(array, axes, split_axis=0, concat_axis=0, tiled=True)


def cost(flops, size):
    return pl.CostEstimate(flops=flops, bytes_accessed=size, transcendentals=0)


def shift(array, axis, size, by):
    return lax.ppermute(array, axis, [(i, (i + by) % size) for i in range(size)])


def local(feats, hilbert_pos, w_qkv, w_out, grad_out):
    core, x = lax.axis_index("core"), lax.axis_index("x")
    at = jnp.stack([core, x]).astype(jnp.int32)
    pieces = [w_qkv[:, :WIDTH], w_qkv[:, WIDTH : 2 * WIDTH], w_qkv[:, 2 * WIDTH :], w_out]
    by_z = jnp.concatenate(
        [jnp.where(core == 0, piece[:, :256], piece[:, 256:]) for piece in pieces], axis=1
    )[None]
    by_z = exchange(jnp.broadcast_to(by_z, (8, 16, W_COLS)), "z").reshape(128, W_COLS)
    send, slot = pl.pallas_call(
        pack_kernel,
        out_shape=(
            jax.ShapeDtypeStruct((SHARDS, SEND_ROWS, LANES), BF),
            jax.ShapeDtypeStruct((8, POINTS), jnp.int32),
        ),
        in_specs=[VMEM, VMEM],
        out_specs=(VMEM, VMEM),
        compiler_params=params(32),
        cost_estimate=cost(10**9, 4 << 20),
        name="pack",
    )(hilbert_pos, feats[0])
    recv = exchange(send, SEQ)
    mine = [by_z] + [shift(by_z, "x", 4, k) for k in (1, 2, 3)]
    other = shift(jnp.stack(mine), "core", 2, 1)
    wgrad = jax.ShapeDtypeStruct((4, 8, LANES, LANES), BF)
    out_shape = (
        jax.ShapeDtypeStruct((POINTS, WIDTH), BF),
        wgrad,
        wgrad,
        jax.ShapeDtypeStruct((SHARDS, FEAT_ROWS, LANES), BF),
    )
    mixed, keep, give, back = pl.pallas_call(
        block_kernel,
        out_shape=out_shape,
        in_specs=[SMEM] + [ANY] * 7,
        out_specs=(ANY,) * 4,
        scratch_shapes=[
            pltpu.VMEM((SHARDS, SEND_ROWS, LANES), BF),
            pltpu.VMEM((2, WIDTH, W_COLS), BF),
            pltpu.VMEM((POINTS, WIDTH), BF),
            pltpu.VMEM((POINTS, WIDTH), BF),
            pltpu.VMEM(wgrad.shape, BF),
            pltpu.VMEM(wgrad.shape, BF),
            pltpu.VMEM((SHARDS, FEAT_ROWS, LANES), BF),
            pltpu.VMEM((POINTS, WIDTH), F32),
            pltpu.VMEM((POINTS, WIDTH), BF),
            pltpu.VMEM((WIDTH, POINTS), BF),
            pltpu.VMEM((POINTS, 3 * WIDTH), BF),
            pltpu.VMEM((POINTS, WIDTH), BF),
            pltpu.VMEM((WIDTH, POINTS), BF),
            pltpu.VMEM((3 * WIDTH, POINTS), BF),
            pltpu.SemaphoreType.DMA((14,)),
        ],
        compiler_params=params(50),
        cost_estimate=cost(10**10, 8 << 20),
        name="block",
    )(at, recv, *mine, other, grad_out[0])
    theirs = shift(give, "core", 2, 1)
    pair = pl.pallas_call(
        pair_kernel,
        out_shape=(jax.ShapeDtypeStruct((8, LANES, LANES), BF),) * 4,
        in_specs=[VMEM] * 2,
        out_specs=(VMEM,) * 4,
        compiler_params=params(32),
        cost_estimate=cost(10**6, 3 << 20),
        name="pair",
    )(keep, theirs)
    returned = exchange(back, SEQ)
    by_x = [pair[0]] + [shift(pair[k], "x", 4, k) for k in (1, 2, 3)]
    *by_x, returned = lax.optimization_barrier((*by_x, returned))
    share = sum(term.astype(F32) for term in by_x).astype(BF)
    by_z = exchange(share.reshape(8, 8, 16, LANES).transpose(1, 2, 0, 3), "z")
    part = jnp.sum(by_z.astype(F32), axis=0).astype(BF)
    by_y = exchange(jnp.broadcast_to(part[None], (8,) + part.shape), "y")
    factor = 1.0 / math.sqrt(16 * POINTS * SHARDS)
    total = jnp.sum(by_y.astype(F32), axis=0).reshape(16, W_COLS) * factor
    theirs = shift(total, "core", 2, 1)
    halves = [jnp.where(core == 0, total, theirs), jnp.where(core == 0, theirs, total)]
    qkv_wgrad = jnp.concatenate(
        [half[:, part * 256 : (part + 1) * 256] for part in range(3) for half in halves], axis=1
    )
    out_wgrad = jnp.concatenate([half[:, 768:] for half in halves], axis=1)
    feat_grad = pl.pallas_call(
        unpack_kernel,
        out_shape=jax.ShapeDtypeStruct((POINTS, WIDTH), BF),
        in_specs=[VMEM, VMEM],
        out_specs=VMEM,
        compiler_params=params(32),
        cost_estimate=cost(10**9, 4 << 20),
        name="unpack",
    )(slot, returned)
    return (mixed[None], feat_grad[None], qkv_wgrad, out_wgrad)


def solution(mesh):
    mesh = Mesh(mesh.devices.reshape(4, 8, 8, 2), ("x", "z", "y", "core"))
    rows = P(BATCH, SEQ, None)
    return jax.shard_map(
        local,
        mesh=mesh,
        in_specs=(rows, P(BATCH, SEQ), P(SEQ, None), P(SEQ, None), rows),
        out_specs=(rows, rows, P(SEQ, None), P(SEQ, None)),
        check_vma=False,
    )
```

time: 232 us -> 171 us (0.74)
  blocking collectives: 116 us -> 32.2 us
  starting transfers between devices: 23 us -> 53.4 us
  Pallas kernels: 51.3 us -> 28.5 us
  waiting for transfers between devices: 33 us -> 46.7 us
  other arithmetic: 0.46 us -> 2.9 us
    all_to_all x3 -> x2, blocking collectives: 116 us -> 32.2 us  [exchange(): return lax.all_to_all(array, axes, split_axis=0, concat_axis=0, tiled=True)]
    ppermute x2 -> x9, waiting for transfers between devices: 4.53 us -> 40.6 us  [shift(): lax.ppermute(array, axis, [(i, (i + by) % size) for i in range(size)])]
    pallas_call x1 -> x2, Pallas kernels: 47.1 us -> 23.6 us  [the longest x1 23.3 us: local(): pl.pallas_call(block_kernel, out_shape=out_shape, in_specs=[SMEM] + [ANY]...]
    ppermute x2 -> x9, starting transfers between devices: 7.88 us -> 31 us  [shift(): lax.ppermute(array, axis, [(i, (i + by) % size) for i in range(size)])]
    all_to_all x2 -> x3, waiting for transfers between devices: 28.5 us -> 6.1 us  [exchange(): return lax.all_to_all(array, axes, split_axis=0, concat_axis=0, tiled=True)]
    all_to_all x2 -> x3, starting transfers between devices: 15.1 us -> 22.4 us  [exchange(): return lax.all_to_all(array, axes, split_axis=0, concat_axis=0, tiled=True)]
  transfers between devices with their start and end apart: 4 -> 12, of which waited for: 4 -> 8; matrix products, arithmetic and copies ran while one was open for 0% -> 1% of each run, Pallas kernels for 1% -> 3%
where the time goes in v2:
time: 171 us; the launch traced here: 169 us
  starting transfers between devices  53.4 us (31%)
  waiting for transfers between devices  46.7 us (27%)
  blocking collectives  32.2 us (19%)
  Pallas kernels  28.5 us (17%)
  local copies, waits for them, and re-layouts  4.64 us (3%)
  other arithmetic  2.9 us (2%)
    ppermute x9, waiting for transfers between devices, shift(): lax.ppermute(array, axis, [(i, (i + by) % size) for i in range(size)])  40.6 us
    all_to_all x2, blocking collectives, exchange(): return lax.all_to_all(array, axes, split_axis=0, concat_axis=0, tiled=True)  32.2 us
    ppermute x9, starting transfers between devices, shift(): lax.ppermute(array, axis, [(i, (i + by) % size) for i in range(size)])  31 us
    pallas_call x1, Pallas kernels, local(): pl.pallas_call(block_kernel, out_shape=out_shape, in_specs=[SMEM] + [ANY]...  23.3 us
    all_to_all x3, starting transfers between devices, exchange(): return lax.all_to_all(array, axes, split_axis=0, concat_axis=0, tiled=True)  22.4 us
    all_to_all x3, waiting for transfers between devices, exchange(): return lax.all_to_all(array, axes, split_axis=0, concat_axis=0, tiled=True)  6.1 us
    unnamed x15, local copies, waits for them, and re-layouts  3.84 us
  transfers between devices with their start and end apart: 12, of which 8 were waited for; matrix products, arithmetic and copies ran while one was open for 1% of the time, Pallas kernels for 3%

profile of v2, /device:TPU:1, one launch (start us, length us, event | category | flops | bytes accessed | tf_op | source)
XLA Modules:
  0.0 169.3 jit_solution(4031634384739344336)
XLA Ops:
  2.2 10.9 %all-to-all-start.1 = ((bf16[8,16,1024]{2,1,0:T(8,128)(2,1)}), bf16[8,16,1024]{2,1,0:T(8,128)(2,1)S(1)}, u32[]{:S(2)}, u32[]{:S(2)}) async-start(bf16[8,16,1024]{2,1,0:T(8,128)(2,1)} %broadcast_in_dim.8), calls=%async_computation.1 | async-start | bytes 524288 | tf_op jit(solution)/shard_map/all_to_all | solution.py:268
  14.8 2.6 %pack.1 = (bf16[32,144,128]{2,1,0:T(8,128)(2,1)}, s32[8,512]{1,0:T(8,128)S(1)}) custom-call(s32[1,512]{1,0:T(1,128)S(1)} %copy-done.2, bf16[512,512]{1,0:T(8,128)(2,1)S(1)} %bitcast.31), custom_call_target="tpu_custom_call" | custom-call | flops 1000000000 | bytes 4194304 | tf_op jit(solution)/shard_map/pack/pallas_call | solution.py:287
  17.3 6.1 %all-to-all-done.1 = bf16[8,16,1024]{2,1,0:T(8,128)(2,1)S(1)} async-done(((bf16[8,16,1024]{2,1,0:T(8,128)(2,1)}), bf16[8,16,1024]{2,1,0:T(8,128)(2,1)S(1)}, u32[]{:S(2)}, u32[]{:S(2)}) %all-to-all-start.1) | async-done | bytes 262176 | tf_op jit(solution)/shard_map/all_to_all | solution.py:268
  23.4 5.6 %all-to-all-start = ((bf16[32,144,128]{2,1,0:T(8,128)(2,1)}), bf16[32,144,128]{2,1,0:T(8,128)(2,1)S(1)}, u32[]{:S(2)}, u32[]{:S(2)}) async-start(bf16[32,144,128]{2,1,0:T(8,128)(2,1)} %get-tuple-element.19), calls=%async_computation | async-start | bytes 2359296 | tf_op jit(solution)/shard_map/all_to_all | solution.py:268
  29.1 4.4 %collective-permute-start.2 = (bf16[128,1024]{1,0:T(8,128)(2,1)S(1)}, bf16[128,1024]{1,0:T(8,128)(2,1)S(1)}, u32[]{:S(2)}, u32[]{:S(2)}) collective-permute-start(bf16[128,1024]{1,0:T(8,128)(2,1)S(1)} %bitcast.23), channel_id=1, source_target_pairs={{0,384},{128,0},{256,128},{384,256},{1,385},{129,1},{257,129},{385... | collective-permute-start | bytes 786440 | tf_op jit(solution)/shard_map/ppermute | solution.py:276
  33.5 2.4 %collective-permute-start.1 = (bf16[128,1024]{1,0:T(8,128)(2,1)S(1)}, bf16[128,1024]{1,0:T(8,128)(2,1)S(1)}, u32[]{:S(2)}, u32[]{:S(2)}) collective-permute-start(bf16[128,1024]{1,0:T(8,128)(2,1)S(1)} %bitcast.24), channel_id=1, source_target_pairs={{0,256},{128,384},{256,0},{384,128},{1,257},{129,385},{257,1},{385... | collective-permute-start | bytes 786440 | tf_op jit(solution)/shard_map/ppermute | solution.py:276
  35.9 2.5 %collective-permute-start = (bf16[128,1024]{1,0:T(8,128)(2,1)S(1)}, bf16[128,1024]{1,0:T(8,128)(2,1)S(1)}, u32[]{:S(2)}, u32[]{:S(2)}) collective-permute-start(bf16[128,1024]{1,0:T(8,128)(2,1)S(1)} %bitcast.25), channel_id=1, source_target_pairs={{0,128},{128,256},{256,384},{384,0},{1,129},{129,257},{257,385},{3... | collective-permute-start | bytes 786440 | tf_op jit(solution)/shard_map/ppermute | solution.py:276
  38.4 4.6 %collective-permute-done.2.mine3_hbm = bf16[128,1024]{1,0:T(8,128)(2,1)S(1)} collective-permute-done((bf16[128,1024]{1,0:T(8,128)(2,1)S(1)}, bf16[128,1024]{1,0:T(8,128)(2,1)S(1)}, u32[]{:S(2)}, u32[]{:S(2)}) %collective-permute-start.2) | collective-permute-done | bytes 262176 | tf_op jit(solution)/shard_map/ppermute | solution.py:276
  43.0 5.5 %collective-permute-done.1.mine2_hbm = bf16[128,1024]{1,0:T(8,128)(2,1)S(1)} collective-permute-done((bf16[128,1024]{1,0:T(8,128)(2,1)S(1)}, bf16[128,1024]{1,0:T(8,128)(2,1)S(1)}, u32[]{:S(2)}, u32[]{:S(2)}) %collective-permute-start.1) | collective-permute-done | bytes 262176 | tf_op jit(solution)/shard_map/ppermute | solution.py:276
  48.5 11.3 %collective-permute-done.mine1_hbm = bf16[128,1024]{1,0:T(8,128)(2,1)S(1)} collective-permute-done((bf16[128,1024]{1,0:T(8,128)(2,1)S(1)}, bf16[128,1024]{1,0:T(8,128)(2,1)S(1)}, u32[]{:S(2)}, u32[]{:S(2)}) %collective-permute-start) | collective-permute-done | bytes 262176 | tf_op jit(solution)/shard_map/ppermute | solution.py:276
  60.9 2.3 %collective-permute-start.3 = (bf16[4,128,1024]{2,1,0:T(8,128)(2,1)}, bf16[4,128,1024]{2,1,0:T(8,128)(2,1)}, u32[]{:S(2)}, u32[]{:S(2)}) collective-permute-start(bf16[4,128,1024]{2,1,0:T(8,128)(2,1)} %pad_maximum_fusion), channel_id=1, source_target_pairs={{0,1},{1,0},{2,3},{3,2},{4,5},{5,4},{6,7},{7,6},{8,9},{9,8},{10,11... | collective-permute-start | bytes 3145736 | tf_op jit(solution)/shard_map/ppermute | solution.py:276
  63.4 2.5 %collective-permute-done.3.other_hbm = bf16[4,128,1024]{2,1,0:T(8,128)(2,1)} collective-permute-done((bf16[4,128,1024]{2,1,0:T(8,128)(2,1)}, bf16[4,128,1024]{2,1,0:T(8,128)(2,1)}, u32[]{:S(2)}, u32[]{:S(2)}) %collective-permute-start.3) | collective-permute-done | bytes 1048608 | tf_op jit(solution)/shard_map/ppermute | solution.py:276
  68.0 23.3 %block.1 = (bf16[512,512]{1,0:T(8,128)(2,1)}, bf16[4,8,128,128]{3,2,1,0:T(8,128)(2,1)S(1)}, bf16[4,8,128,128]{3,2,1,0:T(8,128)(2,1)S(1)}, bf16[32,128,128]{2,1,0:T(8,128)(2,1)}) custom-call(s32[2]{0:T(128)S(1)} %pad_add_fusion.at_ref, bf16[32,144,128]{2,1,0:T(8,128)(2,1)} %copy-done.3, bf16[128,1024]{1,0:T(8,128)(2,1)S(1)} %bitcast.27, ...), custom_call_target="tpu_custom_call" | custom-call | flops 10000000000 | bytes 8388608 | tf_op jit(solution)/shard_map/block/pallas_call | solution.py:309
  91.3 5.9 %all-to-all-start.2 = ((bf16[32,128,128]{2,1,0:T(8,128)(2,1)}), bf16[32,128,128]{2,1,0:T(8,128)(2,1)S(1)}, u32[]{:S(2)}, u32[]{:S(2)}) async-start(bf16[32,128,128]{2,1,0:T(8,128)(2,1)} %get-tuple-element.28), calls=%async_computation.2 | async-start | bytes 2097152 | tf_op jit(solution)/shard_map/all_to_all | solution.py:268
  97.3 2.6 %collective-permute-start.4 = (bf16[4,8,128,128]{3,2,1,0:T(8,128)(2,1)S(1)}, bf16[4,8,128,128]{3,2,1,0:T(8,128)(2,1)S(1)}, u32[]{:S(2)}, u32[]{:S(2)}) collective-permute-start(bf16[4,8,128,128]{3,2,1,0:T(8,128)(2,1)S(1)} %get-tuple-element.23), channel_id=1, source_target_pairs={{0,1},{1,0},{2,3},{3,2},{4,5},{5,4},{6,7},{7,6},{8,9},{9,8},{10,11... | collective-permute-start | bytes 3145736 | tf_op jit(solution)/shard_map/ppermute | solution.py:276
  102.4 3.4 %collective-permute-start.5 = (bf16[8,128,128]{2,1,0:T(8,128)(2,1)S(1)}, bf16[8,128,128]{2,1,0:T(8,128)(2,1)S(1)}, u32[]{:S(2)}, u32[]{:S(2)}) collective-permute-start(bf16[8,128,128]{2,1,0:T(8,128)(2,1)S(1)} %get-tuple-element.25), channel_id=1, source_target_pairs={{0,128},{128,256},{256,384},{384,0},{1,129},{129,257},{257,385},{3... | collective-permute-start | bytes 786440 | tf_op jit(solution)/shard_map/ppermute | solution.py:276
  105.8 4.3 %collective-permute-start.6 = (bf16[8,128,128]{2,1,0:T(8,128)(2,1)S(1)}, bf16[8,128,128]{2,1,0:T(8,128)(2,1)S(1)}, u32[]{:S(2)}, u32[]{:S(2)}) collective-permute-start(bf16[8,128,128]{2,1,0:T(8,128)(2,1)S(1)} %get-tuple-element.26), channel_id=1, source_target_pairs={{0,256},{128,384},{256,0},{384,128},{1,257},{129,385},{257,1},{385... | collective-permute-start | bytes 786440 | tf_op jit(solution)/shard_map/ppermute | solution.py:276
  110.2 3.1 %collective-permute-start.7 = (bf16[8,128,128]{2,1,0:T(8,128)(2,1)S(1)}, bf16[8,128,128]{2,1,0:T(8,128)(2,1)S(1)}, u32[]{:S(2)}, u32[]{:S(2)}) collective-permute-start(bf16[8,128,128]{2,1,0:T(8,128)(2,1)S(1)} %get-tuple-element.27), channel_id=1, source_target_pairs={{0,384},{128,0},{256,128},{384,256},{1,385},{129,1},{257,129},{385... | collective-permute-start | bytes 786440 | tf_op jit(solution)/shard_map/ppermute | solution.py:276
  113.2 5.7 %collective-permute-done.5 = bf16[8,128,128]{2,1,0:T(8,128)(2,1)S(1)} collective-permute-done((bf16[8,128,128]{2,1,0:T(8,128)(2,1)S(1)}, bf16[8,128,128]{2,1,0:T(8,128)(2,1)S(1)}, u32[]{:S(2)}, u32[]{:S(2)}) %collective-permute-start.5) | collective-permute-done | bytes 262176 | tf_op jit(solution)/shard_map/ppermute | solution.py:276
  118.9 8.8 %collective-permute-done.6 = bf16[8,128,128]{2,1,0:T(8,128)(2,1)S(1)} collective-permute-done((bf16[8,128,128]{2,1,0:T(8,128)(2,1)S(1)}, bf16[8,128,128]{2,1,0:T(8,128)(2,1)S(1)}, u32[]{:S(2)}, u32[]{:S(2)}) %collective-permute-start.6) | collective-permute-done | bytes 262176 | tf_op jit(solution)/shard_map/ppermute | solution.py:276
  127.8 16.2 %all_to_all.25 = bf16[8,16,8,128]{3,1,2,0:T(8,128)(2,1)S(1)} all-to-all(bf16[8,16,8,128]{3,1,2,0:T(8,128)(2,1)S(1)} %bitcast.34), channel_id=1, replica_groups=mesh['x'=4,'z'=8,'y'=8,'core'=2] {'z'}, dimensions={0} | all-to-all | bytes 524288 | tf_op jit(solution)/shard_map/all_to_all | solution.py:268
  144.1 16.0 %all_to_all.26 = bf16[8,16,8,128]{3,2,1,0:T(8,128)(2,1)S(1)} all-to-all(bf16[8,16,8,128]{3,2,1,0:T(8,128)(2,1)S(1)} %broadcast_in_dim.21), channel_id=1, replica_groups=mesh['x'=4,'z'=8,'y'=8,'core'=2] {'y'}, dimensions={0} | all-to-all | bytes 524288 | tf_op jit(solution)/shard_map/all_to_all | solution.py:268
  160.2 5.9 %collective-permute-start.8 = (f32[16,1024]{1,0:T(8,128)S(1)}, f32[16,1024]{1,0:T(8,128)S(1)}, u32[]{:S(2)}, u32[]{:S(2)}) collective-permute-start(f32[16,1024]{1,0:T(8,128)S(1)} %bitcast.37), channel_id=1, source_target_pairs={{0,1},{1,0},{2,3},{3,2},{4,5},{5,4},{6,7},{7,6},{8,9},{9,8},{10,11... | collective-permute-start | bytes 196616 | tf_op jit(solution)/shard_map/ppermute | solution.py:276
  166.1 2.4 %unpack.1 = bf16[512,512]{1,0:T(8,128)(2,1)} custom-call(s32[8,512]{1,0:T(8,128)S(1)} %get-tuple-element.21.slot_ref, bf16[32,128,128]{2,1,0:T(8,128)(2,1)S(1)} %all-to-all-done.2.back_ref), custom_call_target="tpu_custom_call" | custom-call | flops 1000000000 | bytes 4194304 | tf_op jit(solution)/shard_map/unpack/pallas_call | solution.py:360
  (37 shorter events, 10.1 us)
Async XLA Ops:
  2.2 21.2 %all-to-all-start.1 = ((bf16[8,16,1024]{2,1,0:T(8,128)(2,1)}), bf16[8,16,1024]{2,1,0:T(8,128)(2,1)S(1)}, u32[]{:S(2)}, u32[]{:S(2)}) async-start(bf16[8,16,1024]{2,1,0:T(8,128)(2,1)} %broadcast_in_dim.8), calls=%async_computation.1 | async-start | bytes 524288 | tf_op jit(solution)/shard_map/all_to_all | solution.py:268
  13.1 1.0 copy-start
  14.1 0.7 copy-start.2
  23.4 42.5 %all-to-all-start = ((bf16[32,144,128]{2,1,0:T(8,128)(2,1)}), bf16[32,144,128]{2,1,0:T(8,128)(2,1)S(1)}, u32[]{:S(2)}, u32[]{:S(2)}) async-start(bf16[32,144,128]{2,1,0:T(8,128)(2,1)} %get-tuple-element.19), calls=%async_computation | async-start | bytes 2359296 | tf_op jit(solution)/shard_map/all_to_all | solution.py:268
  29.1 13.9 %collective-permute-start.2 = (bf16[128,1024]{1,0:T(8,128)(2,1)S(1)}, bf16[128,1024]{1,0:T(8,128)(2,1)S(1)}, u32[]{:S(2)}, u32[]{:S(2)}) collective-permute-start(bf16[128,1024]{1,0:T(8,128)(2,1)S(1)} %bitcast.23), channel_id=1, source_target_pairs={{0,384},{128,0},{256,128},{384,256},{1,385},{129,1},{257,129},{385... | collective-permute-start | bytes 786440 | tf_op jit(solution)/shard_map/ppermute | solution.py:276
  33.5 15.0 %collective-permute-start.1 = (bf16[128,1024]{1,0:T(8,128)(2,1)S(1)}, bf16[128,1024]{1,0:T(8,128)(2,1)S(1)}, u32[]{:S(2)}, u32[]{:S(2)}) collective-permute-start(bf16[128,1024]{1,0:T(8,128)(2,1)S(1)} %bitcast.24), channel_id=1, source_target_pairs={{0,256},{128,384},{256,0},{384,128},{1,257},{129,385},{257,1},{385... | collective-permute-start | bytes 786440 | tf_op jit(solution)/shard_map/ppermute | solution.py:276
  35.9 23.9 %collective-permute-start = (bf16[128,1024]{1,0:T(8,128)(2,1)S(1)}, bf16[128,1024]{1,0:T(8,128)(2,1)S(1)}, u32[]{:S(2)}, u32[]{:S(2)}) collective-permute-start(bf16[128,1024]{1,0:T(8,128)(2,1)S(1)} %bitcast.25), channel_id=1, source_target_pairs={{0,128},{128,256},{256,384},{384,0},{1,129},{129,257},{257,385},{3... | collective-permute-start | bytes 786440 | tf_op jit(solution)/shard_map/ppermute | solution.py:276
  60.9 5.0 %collective-permute-start.3 = (bf16[4,128,1024]{2,1,0:T(8,128)(2,1)}, bf16[4,128,1024]{2,1,0:T(8,128)(2,1)}, u32[]{:S(2)}, u32[]{:S(2)}) collective-permute-start(bf16[4,128,1024]{2,1,0:T(8,128)(2,1)} %pad_maximum_fusion), channel_id=1, source_target_pairs={{0,1},{1,0},{2,3},{3,2},{4,5},{5,4},{6,7},{7,6},{8,9},{9,8},{10,11... | collective-permute-start | bytes 3145736 | tf_op jit(solution)/shard_map/ppermute | solution.py:276
  65.9 1.0 copy-start.3
  66.9 1.0 copy-start.1
  91.3 36.3 %all-to-all-start.2 = ((bf16[32,128,128]{2,1,0:T(8,128)(2,1)}), bf16[32,128,128]{2,1,0:T(8,128)(2,1)S(1)}, u32[]{:S(2)}, u32[]{:S(2)}) async-start(bf16[32,128,128]{2,1,0:T(8,128)(2,1)} %get-tuple-element.28), calls=%async_computation.2 | async-start | bytes 2097152 | tf_op jit(solution)/shard_map/all_to_all | solution.py:268
  97.3 4.8 %collective-permute-start.4 = (bf16[4,8,128,128]{3,2,1,0:T(8,128)(2,1)S(1)}, bf16[4,8,128,128]{3,2,1,0:T(8,128)(2,1)S(1)}, u32[]{:S(2)}, u32[]{:S(2)}) collective-permute-start(bf16[4,8,128,128]{3,2,1,0:T(8,128)(2,1)S(1)} %get-tuple-element.23), channel_id=1, source_target_pairs={{0,1},{1,0},{2,3},{3,2},{4,5},{5,4},{6,7},{7,6},{8,9},{9,8},{10,11... | collective-permute-start | bytes 3145736 | tf_op jit(solution)/shard_map/ppermute | solution.py:276
  102.4 16.5 %collective-permute-start.5 = (bf16[8,128,128]{2,1,0:T(8,128)(2,1)S(1)}, bf16[8,128,128]{2,1,0:T(8,128)(2,1)S(1)}, u32[]{:S(2)}, u32[]{:S(2)}) collective-permute-start(bf16[8,128,128]{2,1,0:T(8,128)(2,1)S(1)} %get-tuple-element.25), channel_id=1, source_target_pairs={{0,128},{128,256},{256,384},{384,0},{1,129},{129,257},{257,385},{3... | collective-permute-start | bytes 786440 | tf_op jit(solution)/shard_map/ppermute | solution.py:276
  105.8 21.8 %collective-permute-start.6 = (bf16[8,128,128]{2,1,0:T(8,128)(2,1)S(1)}, bf16[8,128,128]{2,1,0:T(8,128)(2,1)S(1)}, u32[]{:S(2)}, u32[]{:S(2)}) collective-permute-start(bf16[8,128,128]{2,1,0:T(8,128)(2,1)S(1)} %get-tuple-element.26), channel_id=1, source_target_pairs={{0,256},{128,384},{256,0},{384,128},{1,257},{129,385},{257,1},{385... | collective-permute-start | bytes 786440 | tf_op jit(solution)/shard_map/ppermute | solution.py:276
  110.2 17.5 %collective-permute-start.7 = (bf16[8,128,128]{2,1,0:T(8,128)(2,1)S(1)}, bf16[8,128,128]{2,1,0:T(8,128)(2,1)S(1)}, u32[]{:S(2)}, u32[]{:S(2)}) collective-permute-start(bf16[8,128,128]{2,1,0:T(8,128)(2,1)S(1)} %get-tuple-element.27), channel_id=1, source_target_pairs={{0,384},{128,0},{256,128},{384,256},{1,385},{129,1},{257,129},{385... | collective-permute-start | bytes 786440 | tf_op jit(solution)/shard_map/ppermute | solution.py:276
  160.2 8.4 %collective-permute-start.8 = (f32[16,1024]{1,0:T(8,128)S(1)}, f32[16,1024]{1,0:T(8,128)S(1)}, u32[]{:S(2)}, u32[]{:S(2)}) collective-permute-start(f32[16,1024]{1,0:T(8,128)S(1)} %bitcast.37), channel_id=1, source_target_pairs={{0,1},{1,0},{2,3},{3,2},{4,5},{5,4},{6,7},{7,6},{8,9},{9,8},{10,11... | collective-permute-start | bytes 196616 | tf_op jit(solution)/shard_map/ppermute | solution.py:276
  168.7 0.7 copy-start.4

commit v3 on v2

--- a/solution.py
+++ b/solution.py
@@ -62,13 +62,22 @@
     digits = jnp.where(lane == rank, place // 32, 0) + jnp.where(lane == rank + CAP, place % 32, 0)
     pos = dot_t(mine_b, digits.astype(F32).astype(BF)).astype(BF)
     out_ref[:, FEAT_ROWS:SEND_ROWS, :] = jnp.broadcast_to(pos[:, None, :], (SHARDS, 16, LANES))
-    for c in range(4):
-        rows = dot(place_of, feats_ref[:, c * LANES : (c + 1) * LANES]).astype(BF)
-        out_ref[:, c * CAP : (c + 1) * CAP, :] = rows.reshape(SHARDS, CAP, LANES)
+    for c in range(0, 4, 2):
+        rows = dot(place_of, feats_ref[:, c * LANES : (c + 2) * LANES]).astype(BF)
+        for b in range(2):
+            block = rows[:, b * LANES : (b + 1) * LANES]
+            out_ref[:, (c + b) * CAP : (c + b + 1) * CAP, :] = block.reshape(SHARDS, CAP, LANES)
 
 
 def positions(recv_ref):
     return recv_ref[:, FEAT_ROWS:SEND_ROWS, :][:, 0, :]
+
+
+def slot_rows(ref, c):
+    blocks = [
+        ref[:, b * CAP : (b + 1) * CAP, :].reshape(SLOTS, LANES) for b in (c, c + 1)
+    ]
+    return jnp.concatenate(blocks, axis=1)
 
 
 def arrivals(digits):
@@ -89,33 +98,47 @@
     return onehot(iota((SLOTS, POINTS), 1) == place)
 
 
+def arrive_kernel(recv, hil, nrm, digits_ref):
+    digits = positions(recv)
+    digits_ref[...] = digits
+    arrive = arrivals(digits)
+    rows = []
+    for c in range(0, 4, 2):
+        rows.append(dot(arrive, slot_rows(recv, c)))
+        hil[:, c * LANES : (c + 2) * LANES] = rows[-1].astype(BF)
+    rows = jnp.concatenate(rows, axis=1)
+    centred = rows - jnp.mean(rows, axis=-1, keepdims=True)
+    inv_scale = lax.rsqrt(jnp.mean(centred * centred, axis=-1, keepdims=True) + EPS)
+    nrm[...] = (centred * inv_scale).astype(BF)
+
+
 def block_kernel(
     at_ref,
-    recv_hbm,
-    mine0_hbm,
-    mine1_hbm,
-    mine2_hbm,
-    mine3_hbm,
-    other_hbm,
+    hil,
+    nrm,
+    digits_ref,
+    mine0_ref,
+    mine1_ref,
+    mine2_ref,
+    mine3_ref,
+    other_ref,
     gout_hbm,
     mixed_hbm,
     keep_hbm,
     send_hbm,
     back_hbm,
-    recv,
     w,
     gout,
     mixed,
     keep,
     send,
     back,
-    hil,
-    nrm,
     nrm_t,
     qkv,
     cgrad,
     ctx_t,
     qg_t,
+    sd,
     sems,
 ):
     group, x = at_ref[0], at_ref[1]
@@ -127,25 +150,14 @@
         copies.append(copy)
         return copy
 
-    recv_copy = start(recv_hbm, recv)
     w_copies = []
-    for k, mine in enumerate((mine0_hbm, mine1_hbm, mine2_hbm, mine3_hbm)):
+    for k, mine in enumerate((mine0_ref, mine1_ref, mine2_ref, mine3_ref)):
         rows = pl.ds(pl.multiple_of(lax.rem(x + 4 - k, 4) * 128, 128), 128)
         w_copies.append(start(mine, w.at[group, rows, :]))
-        w_copies.append(start(other_hbm.at[k], w.at[1 - group, rows, :]))
+        w_copies.append(start(other_ref.at[k], w.at[1 - group, rows, :]))
     gout_copy = start(gout_hbm, gout)
-
-    recv_copy.wait()
-    digits = positions(recv)
-    arrive = arrivals(digits)
-    for c in range(4):
-        got = recv[:, c * CAP : (c + 1) * CAP, :].reshape(SLOTS, LANES)
-        hil[:, c * LANES : (c + 1) * LANES] = dot(arrive, got)
-    rows = hil[...]
-    centred = rows - jnp.mean(rows, axis=-1, keepdims=True)
-    inv_scale = lax.rsqrt(jnp.mean(centred * centred, axis=-1, keepdims=True) + EPS)
-    normed = (centred * inv_scale).astype(BF)
-    nrm[...] = normed
+    nrm_t[...] = nrm[...].T
+    normed = nrm[...]
     for copy in w_copies:
         copy.wait()
     for g in range(2):
@@ -169,23 +181,30 @@
     def spread(array):
         return jnp.concatenate([array * head for head in row_heads], axis=1)
 
-    def unit(u, carry):
+    def places(u):
         p = u // 4
         o = u % 4
         pts = pl.ds(pl.multiple_of(p * PATCH, PATCH), PATCH)
         first = (o // 2) * 768 + (o % 2) * LANES
         block = lambda part: pl.ds(pl.multiple_of(first + part * 256, LANES), LANES)
         whole = pl.ds(pl.multiple_of(o * LANES, LANES), LANES)
+        return pts, block, whole
+
+    def scores_of(u, slot):
+        pts, block, whole = places(u)
+        sd[slot, 0] = dot_t(stack(qkv[pts, block(1)]), qkv[pts, block(0)] * BF(SCALE))
+        sd[slot, 1] = dot_t(stack(qkv[pts, block(2)]), cgrad[pts, whole])
+
+    def unit(u, slot):
+        pts, block, whole = places(u)
         qs = qkv[pts, block(0)] * BF(SCALE)
         k = qkv[pts, block(1)]
         v = qkv[pts, block(2)]
         dc = cgrad[pts, whole]
-        all_scores = dot_t(stack(k), qs)
-        all_prob_grads = dot_t(stack(v), dc)
         probs_b, score_grads = [], []
         for h in range(8):
-            scores = all_scores[h * PATCH : (h + 1) * PATCH]
-            prob_grad = all_prob_grads[h * PATCH : (h + 1) * PATCH]
+            scores = sd[slot, 0, h * PATCH : (h + 1) * PATCH, :]
+            prob_grad = sd[slot, 1, h * PATCH : (h + 1) * PATCH, :]
             exps = jnp.exp(scores - jnp.max(scores, axis=0, keepdims=True))
             probs = exps * (1.0 / jnp.sum(exps, axis=0, keepdims=True))
             total = jnp.sum(probs * prob_grad, axis=0, keepdims=True)
@@ -193,34 +212,45 @@
             score_grads.append((probs * (prob_grad - total)).astype(BF))
         rows_p, cols_p = jnp.concatenate(probs_b, axis=0), jnp.concatenate(probs_b, axis=1)
         rows_s, cols_s = jnp.concatenate(score_grads, axis=0), jnp.concatenate(score_grads, axis=1)
-        ctx_t[whole, pts] = dot(spread(v.T), rows_p).astype(BF)
-        qg_t[block(0), pts] = dot(spread((k * BF(SCALE)).T), rows_s).astype(BF)
+        both = dot(
+            jnp.concatenate([spread(v.T), spread((k * BF(SCALE)).T)], axis=0),
+            jnp.concatenate([rows_p, rows_s], axis=1),
+        ).astype(BF)
+        ctx_t[whole, pts] = both[:LANES, :PATCH]
+        qg_t[block(0), pts] = both[LANES:, PATCH:]
         qg_t[block(1), pts] = dot(cols_s, stack(qs)).astype(BF).T
         qg_t[block(2), pts] = dot(cols_p, stack(dc)).astype(BF).T
+
+    def two_units(t, carry):
+        scores_of(2 * t + 1, 1)
+        unit(2 * t, 0)
+        scores_of(jnp.minimum(2 * t + 2, 15), 0)
+        unit(2 * t + 1, 1)
         return carry
 
-    lax.fori_loop(0, 16, unit, 0, unroll=2)
-
-    nrm_t[...] = nrm[...].T
+    scores_of(0, 0)
+    lax.fori_loop(0, 8, two_units, 0, unroll=2)
+
+    def keep_term(ref, part, term):
+        for b in range(4):
+            k = lax.rem(b + 4 - x, 4)
+            rows = slice(b * LANES, (b + 1) * LANES)
+            ref[k, 2 * part] = term[rows, :LANES]
+            ref[k, 2 * part + 1] = term[rows, LANES:]
+
     for g, ref, target in ((1 - group, send, send_hbm), (group, keep, keep_hbm)):
-        for k in range(4):
-            rows = pl.ds(pl.multiple_of(lax.rem(x + k, 4) * 128, 128), 128)
-            for part in range(3):
-                chans = pl.ds(pl.multiple_of(g * 768 + part * 256, 256), 256)
-                term = dot_t(nrm_t[rows, :], qg_t[chans, :]).astype(BF)
-                ref[k, 2 * part] = term[:, :LANES]
-                ref[k, 2 * part + 1] = term[:, LANES:]
-            cols = pl.ds(pl.multiple_of(g * 256, 256), 256)
-            term = dot(ctx_t[rows, :], gout[:, cols]).astype(BF)
-            ref[k, 6] = term[:, :LANES]
-            ref[k, 7] = term[:, LANES:]
+        for part in range(3):
+            chans = pl.ds(pl.multiple_of(g * 768 + part * 256, 256), 256)
+            keep_term(ref, part, dot_t(nrm_t[...], qg_t[chans, :]).astype(BF))
+        cols = pl.ds(pl.multiple_of(g * 256, 256), 256)
+        keep_term(ref, 3, dot(ctx_t[...], gout[:, cols]).astype(BF))
         start(ref, target)
     context = ctx_t[...].T
     for g in range(2):
         cols = slice(g * 256, (g + 1) * 256)
-        mixed[:, cols] = (hil[:, cols] + dot(context, w[g, :, 768:])).astype(BF)
+        mixed[:, cols] = (hil[:, cols].astype(F32) + dot(context, w[g, :, 768:])).astype(BF)
     start(mixed, mixed_hbm)
-    rows = hil[...]
+    rows = hil[...].astype(F32)
     centred = rows - jnp.mean(rows, axis=-1, keepdims=True)
     inv_scale = lax.rsqrt(jnp.mean(centred * centred, axis=-1, keepdims=True) + EPS)
     xhat = centred * inv_scale
@@ -228,10 +258,12 @@
     cent = ngrad - jnp.mean(ngrad, axis=-1, keepdims=True)
     cent = cent - xhat * jnp.mean(ngrad * xhat, axis=-1, keepdims=True)
     hgrad = (gout[...].astype(F32) + inv_scale * cent).astype(BF)
-    leave = departures(digits)
-    for c in range(4):
-        out = dot(leave, hgrad[:, c * LANES : (c + 1) * LANES]).astype(BF)
-        back[:, c * CAP : (c + 1) * CAP, :] = out.reshape(SHARDS, CAP, LANES)
+    leave = departures(digits_ref[...])
+    for c in range(0, 4, 2):
+        out = dot(leave, hgrad[:, c * LANES : (c + 2) * LANES]).astype(BF)
+        for b in range(2):
+            block = out[:, b * LANES : (b + 1) * LANES]
+            back[:, (c + b) * CAP : (c + b + 1) * CAP, :] = block.reshape(SHARDS, CAP, LANES)
     start(back, back_hbm)
     for copy in copies[-4:]:
         copy.wait()
@@ -240,6 +272,17 @@
 def pair_kernel(keep_ref, theirs_ref, *out_refs):
     for k in range(4):
         out_refs[k][...] = (keep_ref[k].astype(F32) + theirs_ref[k].astype(F32)).astype(BF)
+
+
+def columns_kernel(blocks_ref, qkv_ref, out_ref):
+    for y in range(8):
+        for core in range(2):
+            first = y // 2 * WIDTH + core * 256 + y % 2 * LANES
+            block = blocks_ref[2 * y + core]
+            if first < 3 * WIDTH:
+                qkv_ref[:, first : first + LANES] = block
+            else:
+                out_ref[:, first - 3 * WIDTH : first - 3 * WIDTH + LANES] = block
 
 
 def unpack_kernel(slot_ref, back_ref, out_ref):
@@ -250,14 +293,14 @@
     cols = dot_t(eye, digits.astype(F32).astype(BF))
     slot_col = (cols[:, 0:1] * 32.0 + cols[:, 1:2]).astype(jnp.int32)
     take = onehot(iota((POINTS, SLOTS), 1) == slot_col)
-    for c in range(4):
-        got = back_ref[:, c * CAP : (c + 1) * CAP, :].reshape(SLOTS, LANES)
-        out_ref[:, c * LANES : (c + 1) * LANES] = dot(take, got).astype(BF)
+    for c in range(0, 4, 2):
+        out_ref[:, c * LANES : (c + 2) * LANES] = dot(take, slot_rows(back_ref, c)).astype(BF)
 
 
 VMEM = pl.BlockSpec(memory_space=pltpu.VMEM)
 SMEM = pl.BlockSpec(memory_space=pltpu.SMEM)
 ANY = pl.BlockSpec(memory_space=pl.ANY)
+HBM = pl.BlockSpec(memory_space=pltpu.HBM)
 
 
 def params(mib):
@@ -306,37 +349,48 @@
         wgrad,
         jax.ShapeDtypeStruct((SHARDS, FEAT_ROWS, LANES), BF),
     )
+    hilbert, normed, digits = pl.pallas_call(
+        arrive_kernel,
+        out_shape=(
+            jax.ShapeDtypeStruct((POINTS, WIDTH), BF),
+            jax.ShapeDtypeStruct((POINTS, WIDTH), BF),
+            jax.ShapeDtypeStruct((SHARDS, LANES), BF),
+        ),
+        in_specs=[VMEM],
+        out_specs=(VMEM,) * 3,
+        compiler_params=params(32),
+        cost_estimate=cost(2 * 10**9, 4 << 20),
+        name="arrive",
+    )(recv)
     mixed, keep, give, back = pl.pallas_call(
         block_kernel,
         out_shape=out_shape,
-        in_specs=[SMEM] + [ANY] * 7,
+        in_specs=[SMEM] + [VMEM] * 8 + [HBM],
         out_specs=(ANY,) * 4,
         scratch_shapes=[
-            pltpu.VMEM((SHARDS, SEND_ROWS, LANES), BF),
             pltpu.VMEM((2, WIDTH, W_COLS), BF),
             pltpu.VMEM((POINTS, WIDTH), BF),
             pltpu.VMEM((POINTS, WIDTH), BF),
             pltpu.VMEM(wgrad.shape, BF),
             pltpu.VMEM(wgrad.shape, BF),
             pltpu.VMEM((SHARDS, FEAT_ROWS, LANES), BF),
-            pltpu.VMEM((POINTS, WIDTH), F32),
-            pltpu.VMEM((POINTS, WIDTH), BF),
             pltpu.VMEM((WIDTH, POINTS), BF),
             pltpu.VMEM((POINTS, 3 * WIDTH), BF),
             pltpu.VMEM((POINTS, WIDTH), BF),
             pltpu.VMEM((WIDTH, POINTS), BF),
             pltpu.VMEM((3 * WIDTH, POINTS), BF),
-            pltpu.SemaphoreType.DMA((14,)),
+            pltpu.VMEM((2, 2, 8 * PATCH, PATCH), F32),
+            pltpu.SemaphoreType.DMA((13,)),
         ],
         compiler_params=params(50),
         cost_estimate=cost(10**10, 8 << 20),
         name="block",
-    )(at, recv, *mine, other, grad_out[0])
+    )(at, hilbert, normed, digits, *mine, other, grad_out[0])
     theirs = shift(give, "core", 2, 1)
     pair = pl.pallas_call(
         pair_kernel,
         out_shape=(jax.ShapeDtypeStruct((8, LANES, LANES), BF),) * 4,
-        in_specs=[VMEM] * 2,
+        in_specs=[VMEM, VMEM],
         out_specs=(VMEM,) * 4,
         compiler_params=params(32),
         cost_estimate=cost(10**6, 3 << 20),
@@ -346,17 +400,22 @@
     by_x = [pair[0]] + [shift(pair[k], "x", 4, k) for k in (1, 2, 3)]
     *by_x, returned = lax.optimization_barrier((*by_x, returned))
     share = sum(term.astype(F32) for term in by_x).astype(BF)
-    by_z = exchange(share.reshape(8, 8, 16, LANES).transpose(1, 2, 0, 3), "z")
-    part = jnp.sum(by_z.astype(F32), axis=0).astype(BF)
-    by_y = exchange(jnp.broadcast_to(part[None], (8,) + part.shape), "y")
+    by_seq = exchange(share.reshape(64, WIDTH // SHARDS, LANES), ("y", "z"))
     factor = 1.0 / math.sqrt(16 * POINTS * SHARDS)
-    total = jnp.sum(by_y.astype(F32), axis=0).reshape(16, W_COLS) * factor
-    theirs = shift(total, "core", 2, 1)
-    halves = [jnp.where(core == 0, total, theirs), jnp.where(core == 0, theirs, total)]
-    qkv_wgrad = jnp.concatenate(
-        [half[:, part * 256 : (part + 1) * 256] for part in range(3) for half in halves], axis=1
-    )
-    out_wgrad = jnp.concatenate([half[:, 768:] for half in halves], axis=1)
+    total = jnp.sum(by_seq.astype(F32), axis=0) * factor
+    whole = exchange(jnp.broadcast_to(total[None], (16,) + total.shape), BATCH)
+    qkv_wgrad, out_wgrad = pl.pallas_call(
+        columns_kernel,
+        out_shape=(
+            jax.ShapeDtypeStruct((WIDTH // SHARDS, 3 * WIDTH), F32),
+            jax.ShapeDtypeStruct((WIDTH // SHARDS, WIDTH), F32),
+        ),
+        in_specs=[VMEM],
+        out_specs=(VMEM, VMEM),
+        compiler_params=params(32),
+        cost_estimate=cost(10**6, 1 << 18),
+        name="columns",
+    )(whole)
     feat_grad = pl.pallas_call(
         unpack_kernel,
         out_shape=jax.ShapeDtypeStruct((POINTS, WIDTH), BF),

time: 171 us -> 162 us (0.947)
  blocking collectives: 32.2 us -> 24.8 us
  waiting for transfers between devices: 46.7 us -> 53.4 us
  Pallas kernels: 28.5 us -> 23.2 us
    all_to_all x3 -> x4, waiting for transfers between devices: 6.1 us -> 14 us  [exchange(): return lax.all_to_all(array, axes, split_axis=0, concat_axis=0, tiled=True)]
    all_to_all x2 -> x1, blocking collectives: 32.2 us -> 24.8 us  [exchange(): return lax.all_to_all(array, axes, split_axis=0, concat_axis=0, tiled=True)]
    all_to_all x3 -> x4, starting transfers between devices: 22.4 us -> 29.3 us  [exchange(): return lax.all_to_all(array, axes, split_axis=0, concat_axis=0, tiled=True)]
    ppermute x9 -> x8, starting transfers between devices: 31 us -> 25.1 us  [shift(): lax.ppermute(array, axis, [(i, (i + by) % size) for i in range(size)])]
    pallas_call x1 -> x3, Pallas kernels: 23.3 us -> 19 us  [the longest x1 17.4 us: local(): pl.pallas_call(block_kernel, out_shape=out_shape, in_specs=[SMEM] + [VMEM...]
    unnamed x15 -> x8, local copies, waits for them, and re-layouts: 3.84 us -> 1.73 us
    ppermute x9 -> x8, waiting for transfers between devices: 40.6 us -> 39.4 us  [shift(): lax.ppermute(array, axis, [(i, (i + by) % size) for i in range(size)])]
  transfers between devices with their start and end apart: 12 -> 12, of which waited for: 8 -> 9; matrix products, arithmetic and copies ran while one was open for 1% -> 0% of each run, Pallas kernels for 3% -> 3%
where the time goes in v3:
time: 162 us; the launch traced here: 161 us
  starting transfers between devices  54.4 us (34%)
  waiting for transfers between devices  53.4 us (33%)
  blocking collectives  24.8 us (15%)
  Pallas kernels  23.2 us (14%)
  local copies, waits for them, and re-layouts  3.12 us (2%)
    ppermute x8, waiting for transfers between devices, shift(): lax.ppermute(array, axis, [(i, (i + by) % size) for i in range(size)])  39.4 us
    all_to_all x4, starting transfers between devices, exchange(): return lax.all_to_all(array, axes, split_axis=0, concat_axis=0, tiled=True)  29.3 us
    ppermute x8, starting transfers between devices, shift(): lax.ppermute(array, axis, [(i, (i + by) % size) for i in range(size)])  25.1 us
    all_to_all x1, blocking collectives, exchange(): return lax.all_to_all(array, axes, split_axis=0, concat_axis=0, tiled=True)  24.8 us
    pallas_call x1, Pallas kernels, local(): pl.pallas_call(block_kernel, out_shape=out_shape, in_specs=[SMEM] + [VMEM...  17.4 us
    all_to_all x4, waiting for transfers between devices, exchange(): return lax.all_to_all(array, axes, split_axis=0, concat_axis=0, tiled=True)  14 us
  transfers between devices with their start and end apart: 12, of which 9 were waited for; matrix products, arithmetic and copies ran while one was open for 0% of the time, Pallas kernels for 3%

profile of v3, /device:TPU:1, one launch (start us, length us, event | category | flops | bytes accessed | tf_op | source)
XLA Modules:
  0.0 160.9 jit_solution(6701716936725932232)
XLA Ops:
  2.2 10.9 %all-to-all-start.1 = ((bf16[8,16,1024]{2,1,0:T(8,128)(2,1)}), bf16[8,16,1024]{2,1,0:T(8,128)(2,1)S(1)}, u32[]{:S(2)}, u32[]{:S(2)}) async-start(bf16[8,16,1024]{2,1,0:T(8,128)(2,1)} %broadcast_in_dim.8), calls=%async_computation.1 | async-start | bytes 524288 | tf_op jit(solution)/shard_map/all_to_all | solution.py:311
  14.8 2.0 %pack.1 = (bf16[32,144,128]{2,1,0:T(8,128)(2,1)}, s32[8,512]{1,0:T(8,128)S(1)}) custom-call(s32[1,512]{1,0:T(1,128)S(1)} %copy-done.2, bf16[512,512]{1,0:T(8,128)(2,1)S(1)} %bitcast.20), custom_call_target="tpu_custom_call" | custom-call | flops 1000000000 | bytes 4194304 | tf_op jit(solution)/shard_map/pack/pallas_call | solution.py:330
  16.8 6.7 %all-to-all-done.1 = bf16[8,16,1024]{2,1,0:T(8,128)(2,1)S(1)} async-done(((bf16[8,16,1024]{2,1,0:T(8,128)(2,1)}), bf16[8,16,1024]{2,1,0:T(8,128)(2,1)S(1)}, u32[]{:S(2)}, u32[]{:S(2)}) %all-to-all-start.1) | async-done | bytes 262176 | tf_op jit(solution)/shard_map/all_to_all | solution.py:311
  23.4 5.6 %all-to-all-start = ((bf16[32,144,128]{2,1,0:T(8,128)(2,1)}), bf16[32,144,128]{2,1,0:T(8,128)(2,1)S(1)}, u32[]{:S(2)}, u32[]{:S(2)}) async-start(bf16[32,144,128]{2,1,0:T(8,128)(2,1)} %get-tuple-element.24), calls=%async_computation | async-start | bytes 2359296 | tf_op jit(solution)/shard_map/all_to_all | solution.py:311
  29.1 4.4 %collective-permute-start.2 = (bf16[128,1024]{1,0:T(8,128)(2,1)S(1)}, bf16[128,1024]{1,0:T(8,128)(2,1)S(1)}, u32[]{:S(2)}, u32[]{:S(2)}) collective-permute-start(bf16[128,1024]{1,0:T(8,128)(2,1)S(1)} %bitcast.12), channel_id=1, source_target_pairs={{0,384},{128,0},{256,128},{384,256},{1,385},{129,1},{257,129},{385... | collective-permute-start | bytes 786440 | tf_op jit(solution)/shard_map/ppermute | solution.py:319
  33.5 2.4 %collective-permute-start.1 = (bf16[128,1024]{1,0:T(8,128)(2,1)S(1)}, bf16[128,1024]{1,0:T(8,128)(2,1)S(1)}, u32[]{:S(2)}, u32[]{:S(2)}) collective-permute-start(bf16[128,1024]{1,0:T(8,128)(2,1)S(1)} %bitcast.13), channel_id=1, source_target_pairs={{0,256},{128,384},{256,0},{384,128},{1,257},{129,385},{257,1},{385... | collective-permute-start | bytes 786440 | tf_op jit(solution)/shard_map/ppermute | solution.py:319
  35.9 2.5 %collective-permute-start = (bf16[128,1024]{1,0:T(8,128)(2,1)S(1)}, bf16[128,1024]{1,0:T(8,128)(2,1)S(1)}, u32[]{:S(2)}, u32[]{:S(2)}) collective-permute-start(bf16[128,1024]{1,0:T(8,128)(2,1)S(1)} %bitcast.14), channel_id=1, source_target_pairs={{0,128},{128,256},{256,384},{384,0},{1,129},{129,257},{257,385},{3... | collective-permute-start | bytes 786440 | tf_op jit(solution)/shard_map/ppermute | solution.py:319
  38.4 4.6 %collective-permute-done.2.mine3_ref = bf16[128,1024]{1,0:T(8,128)(2,1)S(1)} collective-permute-done((bf16[128,1024]{1,0:T(8,128)(2,1)S(1)}, bf16[128,1024]{1,0:T(8,128)(2,1)S(1)}, u32[]{:S(2)}, u32[]{:S(2)}) %collective-permute-start.2) | collective-permute-done | bytes 262176 | tf_op jit(solution)/shard_map/ppermute | solution.py:319
  43.0 5.5 %collective-permute-done.1.mine2_ref = bf16[128,1024]{1,0:T(8,128)(2,1)S(1)} collective-permute-done((bf16[128,1024]{1,0:T(8,128)(2,1)S(1)}, bf16[128,1024]{1,0:T(8,128)(2,1)S(1)}, u32[]{:S(2)}, u32[]{:S(2)}) %collective-permute-start.1) | collective-permute-done | bytes 262176 | tf_op jit(solution)/shard_map/ppermute | solution.py:319
  48.5 11.3 %collective-permute-done.mine1_ref = bf16[128,1024]{1,0:T(8,128)(2,1)S(1)} collective-permute-done((bf16[128,1024]{1,0:T(8,128)(2,1)S(1)}, bf16[128,1024]{1,0:T(8,128)(2,1)S(1)}, u32[]{:S(2)}, u32[]{:S(2)}) %collective-permute-start) | collective-permute-done | bytes 262176 | tf_op jit(solution)/shard_map/ppermute | solution.py:319
  60.0 2.4 %collective-permute-start.3 = (bf16[4,128,1024]{2,1,0:T(8,128)(2,1)S(1)}, bf16[4,128,1024]{2,1,0:T(8,128)(2,1)}, u32[]{:S(2)}, u32[]{:S(2)}) collective-permute-start(bf16[4,128,1024]{2,1,0:T(8,128)(2,1)S(1)} %pad_maximum_fusion), channel_id=1, source_target_pairs={{0,1},{1,0},{2,3},{3,2},{4,5},{5,4},{6,7},{7,6},{8,9},{9,8},{10,11... | collective-permute-start | bytes 3145736 | tf_op jit(solution)/shard_map/ppermute | solution.py:319
  64.7 17.4 %block.1 = (bf16[512,512]{1,0:T(8,128)(2,1)}, bf16[4,8,128,128]{3,2,1,0:T(8,128)(2,1)S(1)}, bf16[4,8,128,128]{3,2,1,0:T(8,128)(2,1)}, bf16[32,128,128]{2,1,0:T(8,128)(2,1)}) custom-call(s32[2]{0:T(128)S(1)} %pad_add_fusion.at_ref, bf16[512,512]{1,0:T(8,128)(2,1)S(1)} %get-tuple-element.25.hil, bf16[512,512]{1,0:T(8,128)(2,1)S(1)} %get-tuple-element.26.nrm, ...), custom_call_target="tpu_custom_call" | custom-call | flops 10000000000 | bytes 8388608 | tf_op jit(solution)/shard_map/block/pallas_call | solution.py:365
  82.1 6.1 %all-to-all-start.2 = ((bf16[32,128,128]{2,1,0:T(8,128)(2,1)}), bf16[32,128,128]{2,1,0:T(8,128)(2,1)S(1)}, u32[]{:S(2)}, u32[]{:S(2)}) async-start(bf16[32,128,128]{2,1,0:T(8,128)(2,1)} %get-tuple-element.36), calls=%async_computation.2 | async-start | bytes 2097152 | tf_op jit(solution)/shard_map/all_to_all | solution.py:311
  88.2 2.6 %collective-permute-start.4 = (bf16[4,8,128,128]{3,2,1,0:T(8,128)(2,1)S(1)}, bf16[4,8,128,128]{3,2,1,0:T(8,128)(2,1)S(1)}, u32[]{:S(2)}, u32[]{:S(2)}) collective-permute-start(bf16[4,8,128,128]{3,2,1,0:T(8,128)(2,1)S(1)} %copy-done.3), channel_id=1, source_target_pairs={{0,1},{1,0},{2,3},{3,2},{4,5},{5,4},{6,7},{7,6},{8,9},{9,8},{10,11... | collective-permute-start | bytes 3145736 | tf_op jit(solution)/shard_map/ppermute | solution.py:319
  90.8 2.3 %collective-permute-done.4.theirs_ref = bf16[4,8,128,128]{3,2,1,0:T(8,128)(2,1)S(1)} collective-permute-done((bf16[4,8,128,128]{3,2,1,0:T(8,128)(2,1)S(1)}, bf16[4,8,128,128]{3,2,1,0:T(8,128)(2,1)S(1)}, u32[]{:S(2)}, u32[]{:S(2)}) %collective-permute-start.4) | collective-permute-done | bytes 1048608 | tf_op jit(solution)/shard_map/ppermute | solution.py:319
  93.3 3.4 %collective-permute-start.5 = (bf16[8,128,128]{2,1,0:T(8,128)(2,1)S(1)}, bf16[8,128,128]{2,1,0:T(8,128)(2,1)S(1)}, u32[]{:S(2)}, u32[]{:S(2)}) collective-permute-start(bf16[8,128,128]{2,1,0:T(8,128)(2,1)S(1)} %get-tuple-element.33), channel_id=1, source_target_pairs={{0,128},{128,256},{256,384},{384,0},{1,129},{129,257},{257,385},{3... | collective-permute-start | bytes 786440 | tf_op jit(solution)/shard_map/ppermute | solution.py:319
  96.7 4.3 %collective-permute-start.6 = (bf16[8,128,128]{2,1,0:T(8,128)(2,1)S(1)}, bf16[8,128,128]{2,1,0:T(8,128)(2,1)S(1)}, u32[]{:S(2)}, u32[]{:S(2)}) collective-permute-start(bf16[8,128,128]{2,1,0:T(8,128)(2,1)S(1)} %get-tuple-element.34), channel_id=1, source_target_pairs={{0,256},{128,384},{256,0},{384,128},{1,257},{129,385},{257,1},{385... | collective-permute-start | bytes 786440 | tf_op jit(solution)/shard_map/ppermute | solution.py:319
  101.1 3.1 %collective-permute-start.7 = (bf16[8,128,128]{2,1,0:T(8,128)(2,1)S(1)}, bf16[8,128,128]{2,1,0:T(8,128)(2,1)S(1)}, u32[]{:S(2)}, u32[]{:S(2)}) collective-permute-start(bf16[8,128,128]{2,1,0:T(8,128)(2,1)S(1)} %get-tuple-element.35), channel_id=1, source_target_pairs={{0,384},{128,0},{256,128},{384,256},{1,385},{129,1},{257,129},{385... | collective-permute-start | bytes 786440 | tf_op jit(solution)/shard_map/ppermute | solution.py:319
  104.1 5.7 %collective-permute-done.5 = bf16[8,128,128]{2,1,0:T(8,128)(2,1)S(1)} collective-permute-done((bf16[8,128,128]{2,1,0:T(8,128)(2,1)S(1)}, bf16[8,128,128]{2,1,0:T(8,128)(2,1)S(1)}, u32[]{:S(2)}, u32[]{:S(2)}) %collective-permute-start.5) | collective-permute-done | bytes 262176 | tf_op jit(solution)/shard_map/ppermute | solution.py:319
  109.8 8.7 %collective-permute-done.6 = bf16[8,128,128]{2,1,0:T(8,128)(2,1)S(1)} collective-permute-done((bf16[8,128,128]{2,1,0:T(8,128)(2,1)S(1)}, bf16[8,128,128]{2,1,0:T(8,128)(2,1)S(1)}, u32[]{:S(2)}, u32[]{:S(2)}) %collective-permute-start.6) | collective-permute-done | bytes 262176 | tf_op jit(solution)/shard_map/ppermute | solution.py:319
  118.7 24.8 %all_to_all.25 = bf16[64,16,128]{2,1,0:T(8,128)(2,1)S(1)} all-to-all(bf16[64,16,128]{2,1,0:T(8,128)(2,1)S(1)} %bitcast.22), channel_id=1, replica_groups=mesh['x'=4,'z'=8,'y'=8,'core'=2] {'y','z'}, dimensions={0} | all-to-all | bytes 524288 | tf_op jit(solution)/shard_map/all_to_all | solution.py:311
  144.3 6.8 %all-to-all-start.4 = ((f32[16,16,128]{2,1,0:T(8,128)}), f32[16,16,128]{2,1,0:T(8,128)S(1)}, u32[]{:S(2)}, u32[]{:S(2)}) async-start(f32[16,16,128]{2,1,0:T(8,128)} %broadcast_in_dim.21), calls=%async_computation.4 | async-start | bytes 262144 | tf_op jit(solution)/shard_map/all_to_all | solution.py:311
  151.0 1.9 %unpack.1 = bf16[512,512]{1,0:T(8,128)(2,1)} custom-call(s32[8,512]{1,0:T(8,128)S(1)} %get-tuple-element.29.slot_ref, bf16[32,128,128]{2,1,0:T(8,128)(2,1)S(1)} %all-to-all-done.2.back_ref), custom_call_target="tpu_custom_call" | custom-call | flops 1000000000 | bytes 4194304 | tf_op jit(solution)/shard_map/unpack/pallas_call | solution.py:419
  152.9 7.3 %all-to-all-done.4.blocks_ref = f32[16,16,128]{2,1,0:T(8,128)S(1)} async-done(((f32[16,16,128]{2,1,0:T(8,128)}), f32[16,16,128]{2,1,0:T(8,128)S(1)}, u32[]{:S(2)}, u32[]{:S(2)}) %all-to-all-start.4) | async-done | bytes 131104 | tf_op jit(solution)/shard_map/all_to_all | solution.py:311
  (24 shorter events, 7.6 us)
Async XLA Ops:
  2.2 21.2 %all-to-all-start.1 = ((bf16[8,16,1024]{2,1,0:T(8,128)(2,1)}), bf16[8,16,1024]{2,1,0:T(8,128)(2,1)S(1)}, u32[]{:S(2)}, u32[]{:S(2)}) async-start(bf16[8,16,1024]{2,1,0:T(8,128)(2,1)} %broadcast_in_dim.8), calls=%async_computation.1 | async-start | bytes 524288 | tf_op jit(solution)/shard_map/all_to_all | solution.py:311
  13.1 1.0 copy-start
  14.1 0.7 copy-start.2
  23.4 39.0 %all-to-all-start = ((bf16[32,144,128]{2,1,0:T(8,128)(2,1)}), bf16[32,144,128]{2,1,0:T(8,128)(2,1)S(1)}, u32[]{:S(2)}, u32[]{:S(2)}) async-start(bf16[32,144,128]{2,1,0:T(8,128)(2,1)} %get-tuple-element.24), calls=%async_computation | async-start | bytes 2359296 | tf_op jit(solution)/shard_map/all_to_all | solution.py:311
  29.1 13.9 %collective-permute-start.2 = (bf16[128,1024]{1,0:T(8,128)(2,1)S(1)}, bf16[128,1024]{1,0:T(8,128)(2,1)S(1)}, u32[]{:S(2)}, u32[]{:S(2)}) collective-permute-start(bf16[128,1024]{1,0:T(8,128)(2,1)S(1)} %bitcast.12), channel_id=1, source_target_pairs={{0,384},{128,0},{256,128},{384,256},{1,385},{129,1},{257,129},{385... | collective-permute-start | bytes 786440 | tf_op jit(solution)/shard_map/ppermute | solution.py:319
  33.5 15.0 %collective-permute-start.1 = (bf16[128,1024]{1,0:T(8,128)(2,1)S(1)}, bf16[128,1024]{1,0:T(8,128)(2,1)S(1)}, u32[]{:S(2)}, u32[]{:S(2)}) collective-permute-start(bf16[128,1024]{1,0:T(8,128)(2,1)S(1)} %bitcast.13), channel_id=1, source_target_pairs={{0,256},{128,384},{256,0},{384,128},{1,257},{129,385},{257,1},{385... | collective-permute-start | bytes 786440 | tf_op jit(solution)/shard_map/ppermute | solution.py:319
  35.9 23.9 %collective-permute-start = (bf16[128,1024]{1,0:T(8,128)(2,1)S(1)}, bf16[128,1024]{1,0:T(8,128)(2,1)S(1)}, u32[]{:S(2)}, u32[]{:S(2)}) collective-permute-start(bf16[128,1024]{1,0:T(8,128)(2,1)S(1)} %bitcast.14), channel_id=1, source_target_pairs={{0,128},{128,256},{256,384},{384,0},{1,129},{129,257},{257,385},{3... | collective-permute-start | bytes 786440 | tf_op jit(solution)/shard_map/ppermute | solution.py:319
  60.0 4.8 %collective-permute-start.3 = (bf16[4,128,1024]{2,1,0:T(8,128)(2,1)S(1)}, bf16[4,128,1024]{2,1,0:T(8,128)(2,1)}, u32[]{:S(2)}, u32[]{:S(2)}) collective-permute-start(bf16[4,128,1024]{2,1,0:T(8,128)(2,1)S(1)} %pad_maximum_fusion), channel_id=1, source_target_pairs={{0,1},{1,0},{2,3},{3,2},{4,5},{5,4},{6,7},{7,6},{8,9},{9,8},{10,11... | collective-permute-start | bytes 3145736 | tf_op jit(solution)/shard_map/ppermute | solution.py:319
  62.4 2.3 %copy-start.1 = (bf16[1,512,512]{2,1,0:T(8,128)(2,1)S(1)}, bf16[1,512,512]{2,1,0:T(8,128)(2,1)}, u32[]{:S(2)}) copy-start(bf16[1,512,512]{2,1,0:T(8,128)(2,1)} %param.9) | copy-start | bytes 1572868
  82.1 6.1 %copy-start.3 = (bf16[4,8,128,128]{3,2,1,0:T(8,128)(2,1)S(1)}, bf16[4,8,128,128]{3,2,1,0:T(8,128)(2,1)}, u32[]{:S(2)}) copy-start(bf16[4,8,128,128]{3,2,1,0:T(8,128)(2,1)} %get-tuple-element.31) | copy-start | bytes 3145732
  82.1 36.5 %all-to-all-start.2 = ((bf16[32,128,128]{2,1,0:T(8,128)(2,1)}), bf16[32,128,128]{2,1,0:T(8,128)(2,1)S(1)}, u32[]{:S(2)}, u32[]{:S(2)}) async-start(bf16[32,128,128]{2,1,0:T(8,128)(2,1)} %get-tuple-element.36), calls=%async_computation.2 | async-start | bytes 2097152 | tf_op jit(solution)/shard_map/all_to_all | solution.py:311
  88.2 4.8 %collective-permute-start.4 = (bf16[4,8,128,128]{3,2,1,0:T(8,128)(2,1)S(1)}, bf16[4,8,128,128]{3,2,1,0:T(8,128)(2,1)S(1)}, u32[]{:S(2)}, u32[]{:S(2)}) collective-permute-start(bf16[4,8,128,128]{3,2,1,0:T(8,128)(2,1)S(1)} %copy-done.3), channel_id=1, source_target_pairs={{0,1},{1,0},{2,3},{3,2},{4,5},{5,4},{6,7},{7,6},{8,9},{9,8},{10,11... | collective-permute-start | bytes 3145736 | tf_op jit(solution)/shard_map/ppermute | solution.py:319
  93.3 16.5 %collective-permute-start.5 = (bf16[8,128,128]{2,1,0:T(8,128)(2,1)S(1)}, bf16[8,128,128]{2,1,0:T(8,128)(2,1)S(1)}, u32[]{:S(2)}, u32[]{:S(2)}) collective-permute-start(bf16[8,128,128]{2,1,0:T(8,128)(2,1)S(1)} %get-tuple-element.33), channel_id=1, source_target_pairs={{0,128},{128,256},{256,384},{384,0},{1,129},{129,257},{257,385},{3... | collective-permute-start | bytes 786440 | tf_op jit(solution)/shard_map/ppermute | solution.py:319
  96.7 21.8 %collective-permute-start.6 = (bf16[8,128,128]{2,1,0:T(8,128)(2,1)S(1)}, bf16[8,128,128]{2,1,0:T(8,128)(2,1)S(1)}, u32[]{:S(2)}, u32[]{:S(2)}) collective-permute-start(bf16[8,128,128]{2,1,0:T(8,128)(2,1)S(1)} %get-tuple-element.34), channel_id=1, source_target_pairs={{0,256},{128,384},{256,0},{384,128},{1,257},{129,385},{257,1},{385... | collective-permute-start | bytes 786440 | tf_op jit(solution)/shard_map/ppermute | solution.py:319
  101.1 17.5 %collective-permute-start.7 = (bf16[8,128,128]{2,1,0:T(8,128)(2,1)S(1)}, bf16[8,128,128]{2,1,0:T(8,128)(2,1)S(1)}, u32[]{:S(2)}, u32[]{:S(2)}) collective-permute-start(bf16[8,128,128]{2,1,0:T(8,128)(2,1)S(1)} %get-tuple-element.35), channel_id=1, source_target_pairs={{0,384},{128,0},{256,128},{384,256},{1,385},{129,1},{257,129},{385... | collective-permute-start | bytes 786440 | tf_op jit(solution)/shard_map/ppermute | solution.py:319
  144.3 16.0 %all-to-all-start.4 = ((f32[16,16,128]{2,1,0:T(8,128)}), f32[16,16,128]{2,1,0:T(8,128)S(1)}, u32[]{:S(2)}, u32[]{:S(2)}) async-start(f32[16,16,128]{2,1,0:T(8,128)} %broadcast_in_dim.21), calls=%async_computation.4 | async-start | bytes 262144 | tf_op jit(solution)/shard_map/all_to_all | solution.py:311

commit v4 on v3

--- a/solution.py
+++ b/solution.py
@@ -1,3 +1,4 @@
+import functools
 import math
 
 import jax
@@ -28,6 +29,7 @@
 FEAT_ROWS = 4 * CAP
 SEND_ROWS = FEAT_ROWS + 16
 W_COLS = 1024
+X_SHIFTS = (0, 1, 3, 2)
 
 
 def iota(shape, dim):
@@ -124,14 +126,12 @@
     other_ref,
     gout_hbm,
     mixed_hbm,
-    keep_hbm,
-    send_hbm,
+    keep,
+    send,
     back_hbm,
     w,
     gout,
     mixed,
-    keep,
-    send,
     back,
     nrm_t,
     qkv,
@@ -152,7 +152,7 @@
 
     w_copies = []
     for k, mine in enumerate((mine0_ref, mine1_ref, mine2_ref, mine3_ref)):
-        rows = pl.ds(pl.multiple_of(lax.rem(x + 4 - k, 4) * 128, 128), 128)
+        rows = pl.ds(pl.multiple_of(lax.rem(x + 4 - X_SHIFTS[k], 4) * 128, 128), 128)
         w_copies.append(start(mine, w.at[group, rows, :]))
         w_copies.append(start(other_ref.at[k], w.at[1 - group, rows, :]))
     gout_copy = start(gout_hbm, gout)
@@ -218,8 +218,12 @@
         ).astype(BF)
         ctx_t[whole, pts] = both[:LANES, :PATCH]
         qg_t[block(0), pts] = both[LANES:, PATCH:]
-        qg_t[block(1), pts] = dot(cols_s, stack(qs)).astype(BF).T
-        qg_t[block(2), pts] = dot(cols_p, stack(dc)).astype(BF).T
+        both = dot(
+            jnp.concatenate([cols_s, cols_p], axis=0),
+            jnp.concatenate([stack(qs), stack(dc)], axis=1),
+        ).astype(BF)
+        qg_t[block(1), pts] = both[:PATCH, :LANES].T
+        qg_t[block(2), pts] = both[PATCH:, LANES:].T
 
     def two_units(t, carry):
         scores_of(2 * t + 1, 1)
@@ -229,27 +233,8 @@
         return carry
 
     scores_of(0, 0)
-    lax.fori_loop(0, 8, two_units, 0, unroll=2)
-
-    def keep_term(ref, part, term):
-        for b in range(4):
-            k = lax.rem(b + 4 - x, 4)
-            rows = slice(b * LANES, (b + 1) * LANES)
-            ref[k, 2 * part] = term[rows, :LANES]
-            ref[k, 2 * part + 1] = term[rows, LANES:]
-
-    for g, ref, target in ((1 - group, send, send_hbm), (group, keep, keep_hbm)):
-        for part in range(3):
-            chans = pl.ds(pl.multiple_of(g * 768 + part * 256, 256), 256)
-            keep_term(ref, part, dot_t(nrm_t[...], qg_t[chans, :]).astype(BF))
-        cols = pl.ds(pl.multiple_of(g * 256, 256), 256)
-        keep_term(ref, 3, dot(ctx_t[...], gout[:, cols]).astype(BF))
-        start(ref, target)
-    context = ctx_t[...].T
-    for g in range(2):
-        cols = slice(g * 256, (g + 1) * 256)
-        mixed[:, cols] = (hil[:, cols].astype(F32) + dot(context, w[g, :, 768:])).astype(BF)
-    start(mixed, mixed_hbm)
+    lax.fori_loop(0, 8, two_units, 0, unroll=4)
+
     rows = hil[...].astype(F32)
     centred = rows - jnp.mean(rows, axis=-1, keepdims=True)
     inv_scale = lax.rsqrt(jnp.mean(centred * centred, axis=-1, keepdims=True) + EPS)
@@ -265,13 +250,38 @@
             block = out[:, b * LANES : (b + 1) * LANES]
             back[:, (c + b) * CAP : (c + b + 1) * CAP, :] = block.reshape(SHARDS, CAP, LANES)
     start(back, back_hbm)
-    for copy in copies[-4:]:
+    context = ctx_t[...].T
+    for g in range(2):
+        cols = slice(g * 256, (g + 1) * 256)
+        mixed[:, cols] = (hil[:, cols].astype(F32) + dot(context, w[g, :, 768:])).astype(BF)
+    start(mixed, mixed_hbm)
+    def keep_term(ref, part, term):
+        for b in range(4):
+            k = lax.rem(b + 4 - x, 4)
+            rows = slice(b * LANES, (b + 1) * LANES)
+            ref[k, 2 * part] = term[rows, :LANES]
+            ref[k, 2 * part + 1] = term[rows, LANES:]
+
+    for g, ref in ((1 - group, send), (group, keep)):
+        for part in range(3):
+            chans = pl.ds(pl.multiple_of(g * 768 + part * 256, 256), 256)
+            keep_term(ref, part, dot_t(nrm_t[...], qg_t[chans, :]).astype(BF))
+        cols = pl.ds(pl.multiple_of(g * 256, 256), 256)
+        keep_term(ref, 3, dot(ctx_t[...], gout[:, cols]).astype(BF))
+    for copy in copies[-2:]:
         copy.wait()
 
 
 def pair_kernel(keep_ref, theirs_ref, *out_refs):
     for k in range(4):
         out_refs[k][...] = (keep_ref[k].astype(F32) + theirs_ref[k].astype(F32)).astype(BF)
+
+
+def total_kernel(factor, terms_ref, out_ref):
+    total = terms_ref[0].astype(F32)
+    for i in range(1, 64):
+        total = total + terms_ref[i].astype(F32)
+    out_ref[...] = jnp.broadcast_to((total * factor)[None], out_ref.shape)
 
 
 def columns_kernel(blocks_ref, qkv_ref, out_ref):
@@ -340,7 +350,7 @@
         name="pack",
     )(hilbert_pos, feats[0])
     recv = exchange(send, SEQ)
-    mine = [by_z] + [shift(by_z, "x", 4, k) for k in (1, 2, 3)]
+    mine = [by_z] + [shift(by_z, "x", 4, k) for k in X_SHIFTS[1:]]
     other = shift(jnp.stack(mine), "core", 2, 1)
     wgrad = jax.ShapeDtypeStruct((4, 8, LANES, LANES), BF)
     out_shape = (
@@ -366,13 +376,11 @@
         block_kernel,
         out_shape=out_shape,
         in_specs=[SMEM] + [VMEM] * 8 + [HBM],
-        out_specs=(ANY,) * 4,
+        out_specs=(ANY, VMEM, VMEM, ANY),
         scratch_shapes=[
             pltpu.VMEM((2, WIDTH, W_COLS), BF),
             pltpu.VMEM((POINTS, WIDTH), BF),
             pltpu.VMEM((POINTS, WIDTH), BF),
-            pltpu.VMEM(wgrad.shape, BF),
-            pltpu.VMEM(wgrad.shape, BF),
             pltpu.VMEM((SHARDS, FEAT_ROWS, LANES), BF),
             pltpu.VMEM((WIDTH, POINTS), BF),
             pltpu.VMEM((POINTS, 3 * WIDTH), BF),
@@ -380,7 +388,7 @@
             pltpu.VMEM((WIDTH, POINTS), BF),
             pltpu.VMEM((3 * WIDTH, POINTS), BF),
             pltpu.VMEM((2, 2, 8 * PATCH, PATCH), F32),
-            pltpu.SemaphoreType.DMA((13,)),
+            pltpu.SemaphoreType.DMA((11,)),
         ],
         compiler_params=params(50),
         cost_estimate=cost(10**10, 8 << 20),
@@ -397,13 +405,21 @@
         name="pair",
     )(keep, theirs)
     returned = exchange(back, SEQ)
-    by_x = [pair[0]] + [shift(pair[k], "x", 4, k) for k in (1, 2, 3)]
+    by_x = [pair[0]] + [shift(pair[k], "x", 4, k) for k in (2, 3, 1)]
     *by_x, returned = lax.optimization_barrier((*by_x, returned))
     share = sum(term.astype(F32) for term in by_x).astype(BF)
     by_seq = exchange(share.reshape(64, WIDTH // SHARDS, LANES), ("y", "z"))
     factor = 1.0 / math.sqrt(16 * POINTS * SHARDS)
-    total = jnp.sum(by_seq.astype(F32), axis=0) * factor
-    whole = exchange(jnp.broadcast_to(total[None], (16,) + total.shape), BATCH)
+    total = pl.pallas_call(
+        functools.partial(total_kernel, factor),
+        out_shape=jax.ShapeDtypeStruct((16, WIDTH // SHARDS, LANES), F32),
+        in_specs=[VMEM],
+        out_specs=VMEM,
+        compiler_params=params(16),
+        cost_estimate=cost(10**6, 1 << 18),
+        name="total",
+    )(by_seq)
+    whole = exchange(total, BATCH)
     qkv_wgrad, out_wgrad = pl.pallas_call(
         columns_kernel,
         out_shape=(

time: 162 us -> 159 us (0.981)
  waiting for transfers between devices: 53.4 us -> 50.8 us
  starting transfers between devices: 54.4 us -> 56.6 us
    ppermute x8, waiting for transfers between devices: 39.4 us -> 36.8 us  [shift(): lax.ppermute(array, axis, [(i, (i + by) % size) for i in range(size)])]
    all_to_all x4, starting transfers between devices: 29.3 us -> 31.6 us  [exchange(): return lax.all_to_all(array, axes, split_axis=0, concat_axis=0, tiled=True)]
  transfers between devices with their start and end apart: 12 -> 12, of which waited for: 9 -> 10; matrix products, arithmetic and copies ran while one was open for 0% -> 0% of each run, Pallas kernels for 3% -> 3%
where the time goes in v4:
time: 159 us; the launch traced here: 158 us
  starting transfers between devices  56.6 us (36%)
  waiting for transfers between devices  50.8 us (32%)
  blocking collectives  23.9 us (15%)
  Pallas kernels  22.6 us (14%)
  local copies, waits for them, and re-layouts  2.46 us (2%)
    ppermute x8, waiting for transfers between devices, shift(): lax.ppermute(array, axis, [(i, (i + by) % size) for i in range(size)])  36.8 us
    all_to_all x4, starting transfers between devices, exchange(): return lax.all_to_all(array, axes, split_axis=0, concat_axis=0, tiled=True)  31.6 us
    ppermute x8, starting transfers between devices, shift(): lax.ppermute(array, axis, [(i, (i + by) % size) for i in range(size)])  25.1 us
    all_to_all x1, blocking collectives, exchange(): return lax.all_to_all(array, axes, split_axis=0, concat_axis=0, tiled=True)  23.9 us
    pallas_call x1, Pallas kernels, local(): pl.pallas_call(block_kernel, out_shape=out_shape, in_specs=[SMEM] + [VMEM...  16.1 us
    all_to_all x4, waiting for transfers between devices, exchange(): return lax.all_to_all(array, axes, split_axis=0, concat_axis=0, tiled=True)  14 us
  transfers between devices with their start and end apart: 12, of which 10 were waited for; matrix products, arithmetic and copies ran while one was open for 0% of the time, Pallas kernels for 3%

profile of v4, /device:TPU:1, one launch (start us, length us, event | category | flops | bytes accessed | tf_op | source)
XLA Modules:
  0.0 158.3 jit_solution(637036161373484637)
XLA Ops:
  2.2 10.9 %all-to-all-start.1 = ((bf16[8,16,1024]{2,1,0:T(8,128)(2,1)}), bf16[8,16,1024]{2,1,0:T(8,128)(2,1)S(1)}, u32[]{:S(2)}, u32[]{:S(2)}) async-start(bf16[8,16,1024]{2,1,0:T(8,128)(2,1)} %broadcast_in_dim.12), calls=%async_computation.1 | async-start | bytes 524288 | tf_op jit(solution)/shard_map/all_to_all | solution.py:321
  14.8 2.0 %pack.1 = (bf16[32,144,128]{2,1,0:T(8,128)(2,1)}, s32[8,512]{1,0:T(8,128)S(1)}) custom-call(s32[1,512]{1,0:T(1,128)S(1)} %copy-done.2, bf16[512,512]{1,0:T(8,128)(2,1)S(1)} %bitcast.20), custom_call_target="tpu_custom_call" | custom-call | flops 1000000000 | bytes 4194304 | tf_op jit(solution)/shard_map/pack/pallas_call | solution.py:340
  16.8 6.7 %all-to-all-done.1 = bf16[8,16,1024]{2,1,0:T(8,128)(2,1)S(1)} async-done(((bf16[8,16,1024]{2,1,0:T(8,128)(2,1)}), bf16[8,16,1024]{2,1,0:T(8,128)(2,1)S(1)}, u32[]{:S(2)}, u32[]{:S(2)}) %all-to-all-start.1) | async-done | bytes 262176 | tf_op jit(solution)/shard_map/all_to_all | solution.py:321
  23.4 5.6 %all-to-all-start = ((bf16[32,144,128]{2,1,0:T(8,128)(2,1)}), bf16[32,144,128]{2,1,0:T(8,128)(2,1)S(1)}, u32[]{:S(2)}, u32[]{:S(2)}) async-start(bf16[32,144,128]{2,1,0:T(8,128)(2,1)} %get-tuple-element.24), calls=%async_computation | async-start | bytes 2359296 | tf_op jit(solution)/shard_map/all_to_all | solution.py:321
  29.1 4.7 %collective-permute-start.2 = (bf16[128,1024]{1,0:T(8,128)(2,1)S(1)}, bf16[128,1024]{1,0:T(8,128)(2,1)S(1)}, u32[]{:S(2)}, u32[]{:S(2)}) collective-permute-start(bf16[128,1024]{1,0:T(8,128)(2,1)S(1)} %bitcast.12), channel_id=1, source_target_pairs={{0,256},{128,384},{256,0},{384,128},{1,257},{129,385},{257,1},{385... | collective-permute-start | bytes 786440 | tf_op jit(solution)/shard_map/ppermute | solution.py:329
  33.7 2.8 %collective-permute-start.1 = (bf16[128,1024]{1,0:T(8,128)(2,1)S(1)}, bf16[128,1024]{1,0:T(8,128)(2,1)S(1)}, u32[]{:S(2)}, u32[]{:S(2)}) collective-permute-start(bf16[128,1024]{1,0:T(8,128)(2,1)S(1)} %bitcast.13), channel_id=1, source_target_pairs={{0,384},{128,0},{256,128},{384,256},{1,385},{129,1},{257,129},{385... | collective-permute-start | bytes 786440 | tf_op jit(solution)/shard_map/ppermute | solution.py:329
  36.5 2.5 %collective-permute-start = (bf16[128,1024]{1,0:T(8,128)(2,1)S(1)}, bf16[128,1024]{1,0:T(8,128)(2,1)S(1)}, u32[]{:S(2)}, u32[]{:S(2)}) collective-permute-start(bf16[128,1024]{1,0:T(8,128)(2,1)S(1)} %bitcast.14), channel_id=1, source_target_pairs={{0,128},{128,256},{256,384},{384,0},{1,129},{129,257},{257,385},{3... | collective-permute-start | bytes 786440 | tf_op jit(solution)/shard_map/ppermute | solution.py:329
  39.0 6.0 %collective-permute-done.2.mine3_ref = bf16[128,1024]{1,0:T(8,128)(2,1)S(1)} collective-permute-done((bf16[128,1024]{1,0:T(8,128)(2,1)S(1)}, bf16[128,1024]{1,0:T(8,128)(2,1)S(1)}, u32[]{:S(2)}, u32[]{:S(2)}) %collective-permute-start.2) | collective-permute-done | bytes 262176 | tf_op jit(solution)/shard_map/ppermute | solution.py:329
  45.0 10.0 %collective-permute-done.1.mine2_ref = bf16[128,1024]{1,0:T(8,128)(2,1)S(1)} collective-permute-done((bf16[128,1024]{1,0:T(8,128)(2,1)S(1)}, bf16[128,1024]{1,0:T(8,128)(2,1)S(1)}, u32[]{:S(2)}, u32[]{:S(2)}) %collective-permute-start.1) | collective-permute-done | bytes 262176 | tf_op jit(solution)/shard_map/ppermute | solution.py:329
  55.0 2.3 %collective-permute-done.mine1_ref = bf16[128,1024]{1,0:T(8,128)(2,1)S(1)} collective-permute-done((bf16[128,1024]{1,0:T(8,128)(2,1)S(1)}, bf16[128,1024]{1,0:T(8,128)(2,1)S(1)}, u32[]{:S(2)}, u32[]{:S(2)}) %collective-permute-start) | collective-permute-done | bytes 262176 | tf_op jit(solution)/shard_map/ppermute | solution.py:329
  57.4 2.3 %collective-permute-start.3 = (bf16[4,128,1024]{2,1,0:T(8,128)(2,1)S(1)}, bf16[4,128,1024]{2,1,0:T(8,128)(2,1)}, u32[]{:S(2)}, u32[]{:S(2)}) collective-permute-start(bf16[4,128,1024]{2,1,0:T(8,128)(2,1)S(1)} %pad_maximum_fusion), channel_id=1, source_target_pairs={{0,1},{1,0},{2,3},{3,2},{4,5},{5,4},{6,7},{7,6},{8,9},{9,8},{10,11... | collective-permute-start | bytes 3145736 | tf_op jit(solution)/shard_map/ppermute | solution.py:329
  62.2 16.1 %block.1 = (bf16[512,512]{1,0:T(8,128)(2,1)}, bf16[4,8,128,128]{3,2,1,0:T(8,128)(2,1)S(1)}, bf16[4,8,128,128]{3,2,1,0:T(8,128)(2,1)}, bf16[32,128,128]{2,1,0:T(8,128)(2,1)}) custom-call(s32[2]{0:T(128)S(1)} %pad_add_fusion.at_ref, bf16[512,512]{1,0:T(8,128)(2,1)S(1)} %get-tuple-element.25.hil, bf16[512,512]{1,0:T(8,128)(2,1)S(1)} %get-tuple-element.26.nrm, ...), custom_call_target="tpu_custom_call" | custom-call | flops 10000000000 | bytes 8388608 | tf_op jit(solution)/shard_map/block/pallas_call | solution.py:375
  78.3 8.2 %all-to-all-start.2 = ((bf16[32,128,128]{2,1,0:T(8,128)(2,1)}), bf16[32,128,128]{2,1,0:T(8,128)(2,1)S(1)}, u32[]{:S(2)}, u32[]{:S(2)}) async-start(bf16[32,128,128]{2,1,0:T(8,128)(2,1)} %get-tuple-element.36), calls=%async_computation.2 | async-start | bytes 2097152 | tf_op jit(solution)/shard_map/all_to_all | solution.py:321
  86.5 2.6 %collective-permute-start.4 = (bf16[4,8,128,128]{3,2,1,0:T(8,128)(2,1)S(1)}, bf16[4,8,128,128]{3,2,1,0:T(8,128)(2,1)S(1)}, u32[]{:S(2)}, u32[]{:S(2)}) collective-permute-start(bf16[4,8,128,128]{3,2,1,0:T(8,128)(2,1)S(1)} %copy-done.3), channel_id=1, source_target_pairs={{0,1},{1,0},{2,3},{3,2},{4,5},{5,4},{6,7},{7,6},{8,9},{9,8},{10,11... | collective-permute-start | bytes 3145736 | tf_op jit(solution)/shard_map/ppermute | solution.py:329
  89.1 2.3 %collective-permute-done.4.theirs_ref = bf16[4,8,128,128]{3,2,1,0:T(8,128)(2,1)S(1)} collective-permute-done((bf16[4,8,128,128]{3,2,1,0:T(8,128)(2,1)S(1)}, bf16[4,8,128,128]{3,2,1,0:T(8,128)(2,1)S(1)}, u32[]{:S(2)}, u32[]{:S(2)}) %collective-permute-start.4) | collective-permute-done | bytes 1048608 | tf_op jit(solution)/shard_map/ppermute | solution.py:329
  91.6 4.9 %collective-permute-start.5 = (bf16[8,128,128]{2,1,0:T(8,128)(2,1)S(1)}, bf16[8,128,128]{2,1,0:T(8,128)(2,1)S(1)}, u32[]{:S(2)}, u32[]{:S(2)}) collective-permute-start(bf16[8,128,128]{2,1,0:T(8,128)(2,1)S(1)} %get-tuple-element.33), channel_id=1, source_target_pairs={{0,256},{128,384},{256,0},{384,128},{1,257},{129,385},{257,1},{385... | collective-permute-start | bytes 786440 | tf_op jit(solution)/shard_map/ppermute | solution.py:329
  96.6 2.8 %collective-permute-start.6 = (bf16[8,128,128]{2,1,0:T(8,128)(2,1)S(1)}, bf16[8,128,128]{2,1,0:T(8,128)(2,1)S(1)}, u32[]{:S(2)}, u32[]{:S(2)}) collective-permute-start(bf16[8,128,128]{2,1,0:T(8,128)(2,1)S(1)} %get-tuple-element.34), channel_id=1, source_target_pairs={{0,384},{128,0},{256,128},{384,256},{1,385},{129,1},{257,129},{385... | collective-permute-start | bytes 786440 | tf_op jit(solution)/shard_map/ppermute | solution.py:329
  99.4 2.5 %collective-permute-start.7 = (bf16[8,128,128]{2,1,0:T(8,128)(2,1)S(1)}, bf16[8,128,128]{2,1,0:T(8,128)(2,1)S(1)}, u32[]{:S(2)}, u32[]{:S(2)}) collective-permute-start(bf16[8,128,128]{2,1,0:T(8,128)(2,1)S(1)} %get-tuple-element.35), channel_id=1, source_target_pairs={{0,128},{128,256},{256,384},{384,0},{1,129},{129,257},{257,385},{3... | collective-permute-start | bytes 786440 | tf_op jit(solution)/shard_map/ppermute | solution.py:329
  101.8 6.4 %collective-permute-done.5 = bf16[8,128,128]{2,1,0:T(8,128)(2,1)S(1)} collective-permute-done((bf16[8,128,128]{2,1,0:T(8,128)(2,1)S(1)}, bf16[8,128,128]{2,1,0:T(8,128)(2,1)S(1)}, u32[]{:S(2)}, u32[]{:S(2)}) %collective-permute-start.5) | collective-permute-done | bytes 262176 | tf_op jit(solution)/shard_map/ppermute | solution.py:329
  108.3 7.2 %collective-permute-done.6 = bf16[8,128,128]{2,1,0:T(8,128)(2,1)S(1)} collective-permute-done((bf16[8,128,128]{2,1,0:T(8,128)(2,1)S(1)}, bf16[8,128,128]{2,1,0:T(8,128)(2,1)S(1)}, u32[]{:S(2)}, u32[]{:S(2)}) %collective-permute-start.6) | collective-permute-done | bytes 262176 | tf_op jit(solution)/shard_map/ppermute | solution.py:329
  117.0 23.9 %all_to_all.25.terms_ref = bf16[64,16,128]{2,1,0:T(8,128)(2,1)S(1)} all-to-all(bf16[64,16,128]{2,1,0:T(8,128)(2,1)S(1)} %bitcast.22), channel_id=1, replica_groups=mesh['x'=4,'z'=8,'y'=8,'core'=2] {'y','z'}, dimensions={0} | all-to-all | bytes 524288 | tf_op jit(solution)/shard_map/all_to_all | solution.py:321
  141.5 6.9 %all-to-all-start.4 = ((f32[16,16,128]{2,1,0:T(8,128)}), f32[16,16,128]{2,1,0:T(8,128)S(1)}, u32[]{:S(2)}, u32[]{:S(2)}) async-start(f32[16,16,128]{2,1,0:T(8,128)} %total.1), calls=%async_computation.4 | async-start | bytes 262144 | tf_op jit(solution)/shard_map/all_to_all | solution.py:321
  148.4 1.9 %unpack.1 = bf16[512,512]{1,0:T(8,128)(2,1)} custom-call(s32[8,512]{1,0:T(8,128)S(1)} %get-tuple-element.29.slot_ref, bf16[32,128,128]{2,1,0:T(8,128)(2,1)S(1)} %all-to-all-done.2.back_ref), custom_call_target="tpu_custom_call" | custom-call | flops 1000000000 | bytes 4194304 | tf_op jit(solution)/shard_map/unpack/pallas_call | solution.py:435
  150.3 7.3 %all-to-all-done.4.blocks_ref = f32[16,16,128]{2,1,0:T(8,128)S(1)} async-done(((f32[16,16,128]{2,1,0:T(8,128)}), f32[16,16,128]{2,1,0:T(8,128)S(1)}, u32[]{:S(2)}, u32[]{:S(2)}) %all-to-all-start.4) | async-done | bytes 131104 | tf_op jit(solution)/shard_map/all_to_all | solution.py:321
  (22 shorter events, 8.9 us)
Async XLA Ops:
  2.2 21.2 %all-to-all-start.1 = ((bf16[8,16,1024]{2,1,0:T(8,128)(2,1)}), bf16[8,16,1024]{2,1,0:T(8,128)(2,1)S(1)}, u32[]{:S(2)}, u32[]{:S(2)}) async-start(bf16[8,16,1024]{2,1,0:T(8,128)(2,1)} %broadcast_in_dim.12), calls=%async_computation.1 | async-start | bytes 524288 | tf_op jit(solution)/shard_map/all_to_all | solution.py:321
  13.1 1.0 copy-start
  14.1 0.7 copy-start.2
  23.4 36.4 %all-to-all-start = ((bf16[32,144,128]{2,1,0:T(8,128)(2,1)}), bf16[32,144,128]{2,1,0:T(8,128)(2,1)S(1)}, u32[]{:S(2)}, u32[]{:S(2)}) async-start(bf16[32,144,128]{2,1,0:T(8,128)(2,1)} %get-tuple-element.24), calls=%async_computation | async-start | bytes 2359296 | tf_op jit(solution)/shard_map/all_to_all | solution.py:321
  29.1 16.0 %collective-permute-start.2 = (bf16[128,1024]{1,0:T(8,128)(2,1)S(1)}, bf16[128,1024]{1,0:T(8,128)(2,1)S(1)}, u32[]{:S(2)}, u32[]{:S(2)}) collective-permute-start(bf16[128,1024]{1,0:T(8,128)(2,1)S(1)} %bitcast.12), channel_id=1, source_target_pairs={{0,256},{128,384},{256,0},{384,128},{1,257},{129,385},{257,1},{385... | collective-permute-start | bytes 786440 | tf_op jit(solution)/shard_map/ppermute | solution.py:329
  33.7 21.3 %collective-permute-start.1 = (bf16[128,1024]{1,0:T(8,128)(2,1)S(1)}, bf16[128,1024]{1,0:T(8,128)(2,1)S(1)}, u32[]{:S(2)}, u32[]{:S(2)}) collective-permute-start(bf16[128,1024]{1,0:T(8,128)(2,1)S(1)} %bitcast.13), channel_id=1, source_target_pairs={{0,384},{128,0},{256,128},{384,256},{1,385},{129,1},{257,129},{385... | collective-permute-start | bytes 786440 | tf_op jit(solution)/shard_map/ppermute | solution.py:329
  36.5 20.8 %collective-permute-start = (bf16[128,1024]{1,0:T(8,128)(2,1)S(1)}, bf16[128,1024]{1,0:T(8,128)(2,1)S(1)}, u32[]{:S(2)}, u32[]{:S(2)}) collective-permute-start(bf16[128,1024]{1,0:T(8,128)(2,1)S(1)} %bitcast.14), channel_id=1, source_target_pairs={{0,128},{128,256},{256,384},{384,0},{1,129},{129,257},{257,385},{3... | collective-permute-start | bytes 786440 | tf_op jit(solution)/shard_map/ppermute | solution.py:329
  57.4 4.8 %collective-permute-start.3 = (bf16[4,128,1024]{2,1,0:T(8,128)(2,1)S(1)}, bf16[4,128,1024]{2,1,0:T(8,128)(2,1)}, u32[]{:S(2)}, u32[]{:S(2)}) collective-permute-start(bf16[4,128,1024]{2,1,0:T(8,128)(2,1)S(1)} %pad_maximum_fusion), channel_id=1, source_target_pairs={{0,1},{1,0},{2,3},{3,2},{4,5},{5,4},{6,7},{7,6},{8,9},{9,8},{10,11... | collective-permute-start | bytes 3145736 | tf_op jit(solution)/shard_map/ppermute | solution.py:329
  59.9 2.3 %copy-start.1 = (bf16[1,512,512]{2,1,0:T(8,128)(2,1)S(1)}, bf16[1,512,512]{2,1,0:T(8,128)(2,1)}, u32[]{:S(2)}) copy-start(bf16[1,512,512]{2,1,0:T(8,128)(2,1)} %param.9) | copy-start | bytes 1572868
  78.3 8.3 %copy-start.3 = (bf16[4,8,128,128]{3,2,1,0:T(8,128)(2,1)S(1)}, bf16[4,8,128,128]{3,2,1,0:T(8,128)(2,1)}, u32[]{:S(2)}) copy-start(bf16[4,8,128,128]{3,2,1,0:T(8,128)(2,1)} %get-tuple-element.31) | copy-start | bytes 3145732
  78.3 38.5 %all-to-all-start.2 = ((bf16[32,128,128]{2,1,0:T(8,128)(2,1)}), bf16[32,128,128]{2,1,0:T(8,128)(2,1)S(1)}, u32[]{:S(2)}, u32[]{:S(2)}) async-start(bf16[32,128,128]{2,1,0:T(8,128)(2,1)} %get-tuple-element.36), calls=%async_computation.2 | async-start | bytes 2097152 | tf_op jit(solution)/shard_map/all_to_all | solution.py:321
  86.5 4.8 %collective-permute-start.4 = (bf16[4,8,128,128]{3,2,1,0:T(8,128)(2,1)S(1)}, bf16[4,8,128,128]{3,2,1,0:T(8,128)(2,1)S(1)}, u32[]{:S(2)}, u32[]{:S(2)}) collective-permute-start(bf16[4,8,128,128]{3,2,1,0:T(8,128)(2,1)S(1)} %copy-done.3), channel_id=1, source_target_pairs={{0,1},{1,0},{2,3},{3,2},{4,5},{5,4},{6,7},{7,6},{8,9},{9,8},{10,11... | collective-permute-start | bytes 3145736 | tf_op jit(solution)/shard_map/ppermute | solution.py:329
  91.6 16.7 %collective-permute-start.5 = (bf16[8,128,128]{2,1,0:T(8,128)(2,1)S(1)}, bf16[8,128,128]{2,1,0:T(8,128)(2,1)S(1)}, u32[]{:S(2)}, u32[]{:S(2)}) collective-permute-start(bf16[8,128,128]{2,1,0:T(8,128)(2,1)S(1)} %get-tuple-element.33), channel_id=1, source_target_pairs={{0,256},{128,384},{256,0},{384,128},{1,257},{129,385},{257,1},{385... | collective-permute-start | bytes 786440 | tf_op jit(solution)/shard_map/ppermute | solution.py:329
  96.6 18.9 %collective-permute-start.6 = (bf16[8,128,128]{2,1,0:T(8,128)(2,1)S(1)}, bf16[8,128,128]{2,1,0:T(8,128)(2,1)S(1)}, u32[]{:S(2)}, u32[]{:S(2)}) collective-permute-start(bf16[8,128,128]{2,1,0:T(8,128)(2,1)S(1)} %get-tuple-element.34), channel_id=1, source_target_pairs={{0,384},{128,0},{256,128},{384,256},{1,385},{129,1},{257,129},{385... | collective-permute-start | bytes 786440 | tf_op jit(solution)/shard_map/ppermute | solution.py:329
  99.4 17.5 %collective-permute-start.7 = (bf16[8,128,128]{2,1,0:T(8,128)(2,1)S(1)}, bf16[8,128,128]{2,1,0:T(8,128)(2,1)S(1)}, u32[]{:S(2)}, u32[]{:S(2)}) collective-permute-start(bf16[8,128,128]{2,1,0:T(8,128)(2,1)S(1)} %get-tuple-element.35), channel_id=1, source_target_pairs={{0,128},{128,256},{256,384},{384,0},{1,129},{129,257},{257,385},{3... | collective-permute-start | bytes 786440 | tf_op jit(solution)/shard_map/ppermute | solution.py:329
  141.5 16.1 %all-to-all-start.4 = ((f32[16,16,128]{2,1,0:T(8,128)}), f32[16,16,128]{2,1,0:T(8,128)S(1)}, u32[]{:S(2)}, u32[]{:S(2)}) async-start(f32[16,16,128]{2,1,0:T(8,128)} %total.1), calls=%async_computation.4 | async-start | bytes 262144 | tf_op jit(solution)/shard_map/all_to_all | solution.py:321

commit v5 on v4

--- a/solution.py
+++ b/solution.py
@@ -116,28 +116,22 @@
 
 def block_kernel(
     at_ref,
-    hil,
     nrm,
-    digits_ref,
     mine0_ref,
     mine1_ref,
     mine2_ref,
     mine3_ref,
     other_ref,
     gout_hbm,
-    mixed_hbm,
     keep,
     send,
-    back_hbm,
     w,
+    ctx_t,
+    qg_t,
     gout,
-    mixed,
-    back,
     nrm_t,
     qkv,
     cgrad,
-    ctx_t,
-    qg_t,
     sd,
     sems,
 ):
@@ -235,6 +229,29 @@
     scores_of(0, 0)
     lax.fori_loop(0, 8, two_units, 0, unroll=4)
 
+    def keep_term(ref, part, term):
+        for b in range(4):
+            k = lax.rem(b + 4 - x, 4)
+            rows = slice(b * LANES, (b + 1) * LANES)
+            ref[k, 2 * part] = term[rows, :LANES]
+            ref[k, 2 * part + 1] = term[rows, LANES:]
+
+    for g, ref in ((1 - group, send), (group, keep)):
+        for part in range(3):
+            chans = pl.ds(pl.multiple_of(g * 768 + part * 256, 256), 256)
+            keep_term(ref, part, dot_t(nrm_t[...], qg_t[chans, :]).astype(BF))
+        cols = pl.ds(pl.multiple_of(g * 256, 256), 256)
+        keep_term(ref, 3, dot(ctx_t[...], gout[:, cols]).astype(BF))
+
+def finish_kernel(hil, digits_ref, w, ctx_t, qg_t, gout_hbm, mixed_hbm, back, gout, mixed, sems):
+    gout_copy = pltpu.make_async_copy(gout_hbm, gout, sems.at[0])
+    gout_copy.start()
+    context = ctx_t[...].T
+    for g in range(2):
+        cols = slice(g * 256, (g + 1) * 256)
+        mixed[:, cols] = (hil[:, cols].astype(F32) + dot(context, w[g, :, 768:])).astype(BF)
+    mixed_copy = pltpu.make_async_copy(mixed, mixed_hbm, sems.at[1])
+    mixed_copy.start()
     rows = hil[...].astype(F32)
     centred = rows - jnp.mean(rows, axis=-1, keepdims=True)
     inv_scale = lax.rsqrt(jnp.mean(centred * centred, axis=-1, keepdims=True) + EPS)
@@ -242,34 +259,13 @@
     ngrad = (dot(w[0, :, :768], qg_t[:768, :]) + dot(w[1, :, :768], qg_t[768:, :])).T
     cent = ngrad - jnp.mean(ngrad, axis=-1, keepdims=True)
     cent = cent - xhat * jnp.mean(ngrad * xhat, axis=-1, keepdims=True)
+    gout_copy.wait()
     hgrad = (gout[...].astype(F32) + inv_scale * cent).astype(BF)
     leave = departures(digits_ref[...])
     for c in range(0, 4, 2):
         out = dot(leave, hgrad[:, c * LANES : (c + 2) * LANES]).astype(BF)
-        for b in range(2):
-            block = out[:, b * LANES : (b + 1) * LANES]
-            back[:, (c + b) * CAP : (c + b + 1) * CAP, :] = block.reshape(SHARDS, CAP, LANES)
-    start(back, back_hbm)
-    context = ctx_t[...].T
-    for g in range(2):
-        cols = slice(g * 256, (g + 1) * 256)
-        mixed[:, cols] = (hil[:, cols].astype(F32) + dot(context, w[g, :, 768:])).astype(BF)
-    start(mixed, mixed_hbm)
-    def keep_term(ref, part, term):
-        for b in range(4):
-            k = lax.rem(b + 4 - x, 4)
-            rows = slice(b * LANES, (b + 1) * LANES)
-            ref[k, 2 * part] = term[rows, :LANES]
-            ref[k, 2 * part + 1] = term[rows, LANES:]
-
-    for g, ref in ((1 - group, send), (group, keep)):
-        for part in range(3):
-            chans = pl.ds(pl.multiple_of(g * 768 + part * 256, 256), 256)
-            keep_term(ref, part, dot_t(nrm_t[...], qg_t[chans, :]).astype(BF))
-        cols = pl.ds(pl.multiple_of(g * 256, 256), 256)
-        keep_term(ref, 3, dot(ctx_t[...], gout[:, cols]).astype(BF))
-    for copy in copies[-2:]:
-        copy.wait()
+        back[:, :, c * LANES : (c + 2) * LANES] = out.reshape(SHARDS, CAP, 2 * LANES)
+    mixed_copy.wait()
 
 
 def pair_kernel(keep_ref, theirs_ref, *out_refs):
@@ -281,14 +277,14 @@
     total = terms_ref[0].astype(F32)
     for i in range(1, 64):
         total = total + terms_ref[i].astype(F32)
-    out_ref[...] = jnp.broadcast_to((total * factor)[None], out_ref.shape)
+    out_ref[...] = jnp.broadcast_to((total * factor).astype(BF)[None], out_ref.shape)
 
 
 def columns_kernel(blocks_ref, qkv_ref, out_ref):
     for y in range(8):
         for core in range(2):
             first = y // 2 * WIDTH + core * 256 + y % 2 * LANES
-            block = blocks_ref[2 * y + core]
+            block = blocks_ref[2 * y + core].astype(F32)
             if first < 3 * WIDTH:
                 qkv_ref[:, first : first + LANES] = block
             else:
@@ -304,7 +300,9 @@
     slot_col = (cols[:, 0:1] * 32.0 + cols[:, 1:2]).astype(jnp.int32)
     take = onehot(iota((POINTS, SLOTS), 1) == slot_col)
     for c in range(0, 4, 2):
-        out_ref[:, c * LANES : (c + 2) * LANES] = dot(take, slot_rows(back_ref, c)).astype(BF)
+        cols = slice(c * LANES, (c + 2) * LANES)
+        got = back_ref[:, :, cols].reshape(SLOTS, 2 * LANES)
+        out_ref[:, cols] = dot(take, got).astype(BF)
 
 
 VMEM = pl.BlockSpec(memory_space=pltpu.VMEM)
@@ -345,7 +343,7 @@
         ),
         in_specs=[VMEM, VMEM],
         out_specs=(VMEM, VMEM),
-        compiler_params=params(32),
+        compiler_params=params(12),
         cost_estimate=cost(10**9, 4 << 20),
         name="pack",
     )(hilbert_pos, feats[0])
@@ -353,12 +351,6 @@
     mine = [by_z] + [shift(by_z, "x", 4, k) for k in X_SHIFTS[1:]]
     other = shift(jnp.stack(mine), "core", 2, 1)
     wgrad = jax.ShapeDtypeStruct((4, 8, LANES, LANES), BF)
-    out_shape = (
-        jax.ShapeDtypeStruct((POINTS, WIDTH), BF),
-        wgrad,
-        wgrad,
-        jax.ShapeDtypeStruct((SHARDS, FEAT_ROWS, LANES), BF),
-    )
     hilbert, normed, digits = pl.pallas_call(
         arrive_kernel,
         out_shape=(
@@ -368,42 +360,61 @@
         ),
         in_specs=[VMEM],
         out_specs=(VMEM,) * 3,
-        compiler_params=params(32),
+        compiler_params=params(12),
         cost_estimate=cost(2 * 10**9, 4 << 20),
         name="arrive",
     )(recv)
-    mixed, keep, give, back = pl.pallas_call(
+    keep, give, weights, context_t, qkv_grad_t = pl.pallas_call(
         block_kernel,
-        out_shape=out_shape,
-        in_specs=[SMEM] + [VMEM] * 8 + [HBM],
-        out_specs=(ANY, VMEM, VMEM, ANY),
+        out_shape=(
+            wgrad,
+            wgrad,
+            jax.ShapeDtypeStruct((2, WIDTH, W_COLS), BF),
+            jax.ShapeDtypeStruct((WIDTH, POINTS), BF),
+            jax.ShapeDtypeStruct((3 * WIDTH, POINTS), BF),
+        ),
+        in_specs=[SMEM] + [VMEM] * 6 + [HBM],
+        out_specs=(VMEM,) * 5,
         scratch_shapes=[
-            pltpu.VMEM((2, WIDTH, W_COLS), BF),
             pltpu.VMEM((POINTS, WIDTH), BF),
-            pltpu.VMEM((POINTS, WIDTH), BF),
-            pltpu.VMEM((SHARDS, FEAT_ROWS, LANES), BF),
             pltpu.VMEM((WIDTH, POINTS), BF),
             pltpu.VMEM((POINTS, 3 * WIDTH), BF),
             pltpu.VMEM((POINTS, WIDTH), BF),
-            pltpu.VMEM((WIDTH, POINTS), BF),
-            pltpu.VMEM((3 * WIDTH, POINTS), BF),
             pltpu.VMEM((2, 2, 8 * PATCH, PATCH), F32),
-            pltpu.SemaphoreType.DMA((11,)),
+            pltpu.SemaphoreType.DMA((9,)),
         ],
-        compiler_params=params(50),
+        compiler_params=params(24),
         cost_estimate=cost(10**10, 8 << 20),
         name="block",
-    )(at, hilbert, normed, digits, *mine, other, grad_out[0])
+    )(at, normed, *mine, other, grad_out[0])
+    mixed, back = pl.pallas_call(
+        finish_kernel,
+        out_shape=(
+            jax.ShapeDtypeStruct((POINTS, WIDTH), BF),
+            jax.ShapeDtypeStruct((SHARDS, CAP, WIDTH), BF),
+        ),
+        in_specs=[VMEM] * 5 + [HBM],
+        out_specs=(ANY, VMEM),
+        scratch_shapes=[
+            pltpu.VMEM((POINTS, WIDTH), BF),
+            pltpu.VMEM((POINTS, WIDTH), BF),
+            pltpu.SemaphoreType.DMA((2,)),
+        ],
+        compiler_params=params(12),
+        cost_estimate=cost(4 * 10**9, 8 << 20),
+        name="finish",
+    )(hilbert, digits, weights, context_t, qkv_grad_t, grad_out[0])
     theirs = shift(give, "core", 2, 1)
     pair = pl.pallas_call(
         pair_kernel,
         out_shape=(jax.ShapeDtypeStruct((8, LANES, LANES), BF),) * 4,
         in_specs=[VMEM, VMEM],
         out_specs=(VMEM,) * 4,
-        compiler_params=params(32),
+        compiler_params=params(12),
         cost_estimate=cost(10**6, 3 << 20),
         name="pair",
     )(keep, theirs)
+    *pair, back = lax.optimization_barrier((*pair, back))
     returned = exchange(back, SEQ)
     by_x = [pair[0]] + [shift(pair[k], "x", 4, k) for k in (2, 3, 1)]
     *by_x, returned = lax.optimization_barrier((*by_x, returned))
@@ -412,7 +423,7 @@
     factor = 1.0 / math.sqrt(16 * POINTS * SHARDS)
     total = pl.pallas_call(
         functools.partial(total_kernel, factor),
-        out_shape=jax.ShapeDtypeStruct((16, WIDTH // SHARDS, LANES), F32),
+        out_shape=jax.ShapeDtypeStruct((16, WIDTH // SHARDS, LANES), BF),
         in_specs=[VMEM],
         out_specs=VMEM,
         compiler_params=params(16),
@@ -428,7 +439,7 @@
         ),
         in_specs=[VMEM],
         out_specs=(VMEM, VMEM),
-        compiler_params=params(32),
+        compiler_params=params(12),
         cost_estimate=cost(10**6, 1 << 18),
         name="columns",
     )(whole)
@@ -437,7 +448,7 @@
         out_shape=jax.ShapeDtypeStruct((POINTS, WIDTH), BF),
         in_specs=[VMEM, VMEM],
         out_specs=VMEM,
-        compiler_params=params(32),
+        compiler_params=params(12),
         cost_estimate=cost(10**9, 4 << 20),
         name="unpack",
     )(slot, returned)

time: 159 us -> 158 us (level)
  waiting for transfers between devices: 50.8 us -> 48.9 us
  blocking collectives: 23.9 us -> 25.5 us
    all_to_all x1, blocking collectives: 23.9 us -> 25.5 us  [exchange(): return lax.all_to_all(array, axes, split_axis=0, concat_axis=0, tiled=True)]
    pallas_call x1 -> x2, Pallas kernels: 16.1 us -> 15.5 us  [the longest x1 11.7 us: local(): pl.pallas_call(block_kernel, out_shape=(wgrad, wgrad, jax.ShapeDtypeStruc...]
  transfers between devices with their start and end apart: 12 -> 12, of which waited for: 10 -> 8; matrix products, arithmetic and copies ran while one was open for 0% -> 1% of each run, Pallas kernels for 3% -> 6%
where the time goes in v5:
time: 158 us; the launch traced here: 157 us
  starting transfers between devices  55.4 us (35%)
  waiting for transfers between devices  48.9 us (31%)
  blocking collectives  25.5 us (16%)
  Pallas kernels  22.1 us (14%)
  local copies, waits for them, and re-layouts  2.45 us (2%)
  other arithmetic  2.15 us (1%)
    ppermute x8, waiting for transfers between devices, shift(): lax.ppermute(array, axis, [(i, (i + by) % size) for i in range(size)])  36.3 us
    all_to_all x4, starting transfers between devices, exchange(): return lax.all_to_all(array, axes, split_axis=0, concat_axis=0, tiled=True)  30.8 us
    all_to_all x1, blocking collectives, exchange(): return lax.all_to_all(array, axes, split_axis=0, concat_axis=0, tiled=True)  25.5 us
    ppermute x8, starting transfers between devices, shift(): lax.ppermute(array, axis, [(i, (i + by) % size) for i in range(size)])  24.7 us
    all_to_all x4, waiting for transfers between devices, exchange(): return lax.all_to_all(array, axes, split_axis=0, concat_axis=0, tiled=True)  12.6 us
    pallas_call x1, Pallas kernels, local(): pl.pallas_call(block_kernel, out_shape=(wgrad, wgrad, jax.ShapeDtypeStruc...  11.7 us
    pallas_call x1, Pallas kernels, local(): pl.pallas_call(finish_kernel, out_shape=(jax.ShapeDtypeStruct((POINTS, WI...  3.82 us
  transfers between devices with their start and end apart: 12, of which 8 were waited for; matrix products, arithmetic and copies ran while one was open for 1% of the time, Pallas kernels for 6%

profile of v5, /device:TPU:1, one launch (start us, length us, event | category | flops | bytes accessed | tf_op | source)
XLA Modules:
  0.0 157.3 jit_solution(5231065382123086891)
XLA Ops:
  2.2 10.9 %all-to-all-start.1 = ((bf16[8,16,1024]{2,1,0:T(8,128)(2,1)}), bf16[8,16,1024]{2,1,0:T(8,128)(2,1)S(1)}, u32[]{:S(2)}, u32[]{:S(2)}) async-start(bf16[8,16,1024]{2,1,0:T(8,128)(2,1)} %broadcast_in_dim.12), calls=%async_computation.1 | async-start | bytes 524288 | tf_op jit(solution)/shard_map/all_to_all | solution.py:319
  14.8 2.0 %pack.1 = (bf16[32,144,128]{2,1,0:T(8,128)(2,1)}, s32[8,512]{1,0:T(8,128)S(1)}) custom-call(s32[1,512]{1,0:T(1,128)S(1)} %copy-done.2, bf16[512,512]{1,0:T(8,128)(2,1)S(1)} %bitcast.20), custom_call_target="tpu_custom_call" | custom-call | flops 1000000000 | bytes 4194304 | tf_op jit(solution)/shard_map/pack/pallas_call | solution.py:338
  16.8 6.6 %all-to-all-done.1 = bf16[8,16,1024]{2,1,0:T(8,128)(2,1)S(1)} async-done(((bf16[8,16,1024]{2,1,0:T(8,128)(2,1)}), bf16[8,16,1024]{2,1,0:T(8,128)(2,1)S(1)}, u32[]{:S(2)}, u32[]{:S(2)}) %all-to-all-start.1) | async-done | bytes 262176 | tf_op jit(solution)/shard_map/all_to_all | solution.py:319
  23.4 5.6 %all-to-all-start = ((bf16[32,144,128]{2,1,0:T(8,128)(2,1)}), bf16[32,144,128]{2,1,0:T(8,128)(2,1)S(1)}, u32[]{:S(2)}, u32[]{:S(2)}) async-start(bf16[32,144,128]{2,1,0:T(8,128)(2,1)} %get-tuple-element.32), calls=%async_computation | async-start | bytes 2359296 | tf_op jit(solution)/shard_map/all_to_all | solution.py:319
  29.1 4.7 %collective-permute-start.2 = (bf16[128,1024]{1,0:T(8,128)(2,1)S(1)}, bf16[128,1024]{1,0:T(8,128)(2,1)S(1)}, u32[]{:S(2)}, u32[]{:S(2)}) collective-permute-start(bf16[128,1024]{1,0:T(8,128)(2,1)S(1)} %bitcast.12), channel_id=1, source_target_pairs={{0,256},{128,384},{256,0},{384,128},{1,257},{129,385},{257,1},{385... | collective-permute-start | bytes 786440 | tf_op jit(solution)/shard_map/ppermute | solution.py:327
  33.7 2.8 %collective-permute-start.1 = (bf16[128,1024]{1,0:T(8,128)(2,1)S(1)}, bf16[128,1024]{1,0:T(8,128)(2,1)S(1)}, u32[]{:S(2)}, u32[]{:S(2)}) collective-permute-start(bf16[128,1024]{1,0:T(8,128)(2,1)S(1)} %bitcast.13), channel_id=1, source_target_pairs={{0,384},{128,0},{256,128},{384,256},{1,385},{129,1},{257,129},{385... | collective-permute-start | bytes 786440 | tf_op jit(solution)/shard_map/ppermute | solution.py:327
  36.5 2.5 %collective-permute-start = (bf16[128,1024]{1,0:T(8,128)(2,1)S(1)}, bf16[128,1024]{1,0:T(8,128)(2,1)S(1)}, u32[]{:S(2)}, u32[]{:S(2)}) collective-permute-start(bf16[128,1024]{1,0:T(8,128)(2,1)S(1)} %bitcast.14), channel_id=1, source_target_pairs={{0,128},{128,256},{256,384},{384,0},{1,129},{129,257},{257,385},{3... | collective-permute-start | bytes 786440 | tf_op jit(solution)/shard_map/ppermute | solution.py:327
  39.0 6.0 %collective-permute-done.2.mine3_ref = bf16[128,1024]{1,0:T(8,128)(2,1)S(1)} collective-permute-done((bf16[128,1024]{1,0:T(8,128)(2,1)S(1)}, bf16[128,1024]{1,0:T(8,128)(2,1)S(1)}, u32[]{:S(2)}, u32[]{:S(2)}) %collective-permute-start.2) | collective-permute-done | bytes 262176 | tf_op jit(solution)/shard_map/ppermute | solution.py:327
  45.0 10.0 %collective-permute-done.1.mine2_ref = bf16[128,1024]{1,0:T(8,128)(2,1)S(1)} collective-permute-done((bf16[128,1024]{1,0:T(8,128)(2,1)S(1)}, bf16[128,1024]{1,0:T(8,128)(2,1)S(1)}, u32[]{:S(2)}, u32[]{:S(2)}) %collective-permute-start.1) | collective-permute-done | bytes 262176 | tf_op jit(solution)/shard_map/ppermute | solution.py:327
  55.0 2.3 %collective-permute-done.mine1_ref = bf16[128,1024]{1,0:T(8,128)(2,1)S(1)} collective-permute-done((bf16[128,1024]{1,0:T(8,128)(2,1)S(1)}, bf16[128,1024]{1,0:T(8,128)(2,1)S(1)}, u32[]{:S(2)}, u32[]{:S(2)}) %collective-permute-start) | collective-permute-done | bytes 262176 | tf_op jit(solution)/shard_map/ppermute | solution.py:327
  58.4 2.3 %collective-permute-start.3 = (bf16[4,128,1024]{2,1,0:T(8,128)(2,1)}, bf16[4,128,1024]{2,1,0:T(8,128)(2,1)S(1)}, u32[]{:S(2)}, u32[]{:S(2)}) collective-permute-start(bf16[4,128,1024]{2,1,0:T(8,128)(2,1)} %pad_maximum_fusion), channel_id=1, source_target_pairs={{0,1},{1,0},{2,3},{3,2},{4,5},{5,4},{6,7},{7,6},{8,9},{9,8},{10,11... | collective-permute-start | bytes 3145736 | tf_op jit(solution)/shard_map/ppermute | solution.py:327
  63.2 11.7 %block.1 = (bf16[4,8,128,128]{3,2,1,0:T(8,128)(2,1)S(1)}, bf16[4,8,128,128]{3,2,1,0:T(8,128)(2,1)S(1)}, bf16[2,512,1024]{2,1,0:T(8,128)(2,1)S(1)}, bf16[512,512]{1,0:T(8,128)(2,1)S(1)}, bf16[1536,512]{1,0:T(8,128)(2,1)S(1)}) custom-call(s32[2]{0:T(128)S(1)} %pad_add_fusion.at_ref, bf16[512,512]{1,0:T(8,128)(2,1)S(1)} %get-tuple-element.35.nrm, ...), custom_call_target="tpu_custom_call" | custom-call | flops 10000000000 | bytes 8388608 | tf_op jit(solution)/shard_map/block/pallas_call | solution.py:367
  74.9 2.5 %collective-permute-start.4 = (bf16[4,8,128,128]{3,2,1,0:T(8,128)(2,1)S(1)}, bf16[4,8,128,128]{3,2,1,0:T(8,128)(2,1)S(1)}, u32[]{:S(2)}, u32[]{:S(2)}) collective-permute-start(bf16[4,8,128,128]{3,2,1,0:T(8,128)(2,1)S(1)} %get-tuple-element.42), channel_id=1, source_target_pairs={{0,1},{1,0},{2,3},{3,2},{4,5},{5,4},{6,7},{7,6},{8,9},{9,8},{10,11... | collective-permute-start | bytes 3145736 | tf_op jit(solution)/shard_map/ppermute | solution.py:327
  77.4 3.8 %finish.1 = (bf16[512,512]{1,0:T(8,128)(2,1)}, bf16[32,32,512]{2,1,0:T(8,128)(2,1)}) custom-call(bf16[512,512]{1,0:T(8,128)(2,1)S(1)} %get-tuple-element.33.hil, bf16[32,128]{1,0:T(8,128)(2,1)S(1)} %get-tuple-element.34.digits_ref, bf16[2,512,1024]{2,1,0:T(8,128)(2,1)S(1)} %get-tuple-element.36.w, bf16[512,512]{1,0:T(8,128)(2,1)S(1)} %get-tuple-element.37.ctx_t, ...), custom_call_target="tpu_custom_call" | custom-call | flops 4000000000 | bytes 8388608 | tf_op jit(solution)/shard_map/finish/pallas_call | solution.py:390
  81.5 8.1 %all-to-all-start.2 = ((bf16[32,32,512]{2,1,0:T(8,128)(2,1)}), bf16[32,32,512]{2,1,0:T(8,128)(2,1)S(1)}, u32[]{:S(2)}, u32[]{:S(2)}) async-start(bf16[32,32,512]{2,1,0:T(8,128)(2,1)} %get-tuple-element.52), calls=%async_computation.2 | async-start | bytes 2097152 | tf_op jit(solution)/shard_map/all_to_all | solution.py:319
  89.6 4.7 %collective-permute-start.5 = (bf16[8,128,128]{2,1,0:T(8,128)(2,1)S(1)}, bf16[8,128,128]{2,1,0:T(8,128)(2,1)S(1)}, u32[]{:S(2)}, u32[]{:S(2)}) collective-permute-start(bf16[8,128,128]{2,1,0:T(8,128)(2,1)S(1)} %get-tuple-element.49), channel_id=1, source_target_pairs={{0,256},{128,384},{256,0},{384,128},{1,257},{129,385},{257,1},{385... | collective-permute-start | bytes 786440 | tf_op jit(solution)/shard_map/ppermute | solution.py:327
  94.3 2.8 %collective-permute-start.6 = (bf16[8,128,128]{2,1,0:T(8,128)(2,1)S(1)}, bf16[8,128,128]{2,1,0:T(8,128)(2,1)S(1)}, u32[]{:S(2)}, u32[]{:S(2)}) collective-permute-start(bf16[8,128,128]{2,1,0:T(8,128)(2,1)S(1)} %get-tuple-element.50), channel_id=1, source_target_pairs={{0,384},{128,0},{256,128},{384,256},{1,385},{129,1},{257,129},{385... | collective-permute-start | bytes 786440 | tf_op jit(solution)/shard_map/ppermute | solution.py:327
  97.1 2.5 %collective-permute-start.7 = (bf16[8,128,128]{2,1,0:T(8,128)(2,1)S(1)}, bf16[8,128,128]{2,1,0:T(8,128)(2,1)S(1)}, u32[]{:S(2)}, u32[]{:S(2)}) collective-permute-start(bf16[8,128,128]{2,1,0:T(8,128)(2,1)S(1)} %get-tuple-element.51), channel_id=1, source_target_pairs={{0,128},{128,256},{256,384},{384,0},{1,129},{129,257},{257,385},{3... | collective-permute-start | bytes 786440 | tf_op jit(solution)/shard_map/ppermute | solution.py:327
  99.6 5.3 %collective-permute-done.5 = bf16[8,128,128]{2,1,0:T(8,128)(2,1)S(1)} collective-permute-done((bf16[8,128,128]{2,1,0:T(8,128)(2,1)S(1)}, bf16[8,128,128]{2,1,0:T(8,128)(2,1)S(1)}, u32[]{:S(2)}, u32[]{:S(2)}) %collective-permute-start.5) | collective-permute-done | bytes 262176 | tf_op jit(solution)/shard_map/ppermute | solution.py:327
  104.9 11.4 %collective-permute-done.6 = bf16[8,128,128]{2,1,0:T(8,128)(2,1)S(1)} collective-permute-done((bf16[8,128,128]{2,1,0:T(8,128)(2,1)S(1)}, bf16[8,128,128]{2,1,0:T(8,128)(2,1)S(1)}, u32[]{:S(2)}, u32[]{:S(2)}) %collective-permute-start.6) | collective-permute-done | bytes 262176 | tf_op jit(solution)/shard_map/ppermute | solution.py:327
  116.4 25.5 %all_to_all.25.terms_ref = bf16[64,16,128]{2,1,0:T(8,128)(2,1)S(1)} all-to-all(bf16[64,16,128]{2,1,0:T(8,128)(2,1)S(1)} %bitcast.23), channel_id=1, replica_groups=mesh['x'=4,'z'=8,'y'=8,'core'=2] {'y','z'}, dimensions={0} | all-to-all | bytes 524288 | tf_op jit(solution)/shard_map/all_to_all | solution.py:319
  142.6 6.2 %all-to-all-start.4 = ((bf16[16,16,128]{2,1,0:T(8,128)(2,1)}), bf16[16,16,128]{2,1,0:T(8,128)(2,1)S(1)}, u32[]{:S(2)}, u32[]{:S(2)}) async-start(bf16[16,16,128]{2,1,0:T(8,128)(2,1)} %total.1), calls=%async_computation.4 | async-start | bytes 131072 | tf_op jit(solution)/shard_map/all_to_all | solution.py:319
  148.8 1.9 %unpack.1 = bf16[512,512]{1,0:T(8,128)(2,1)} custom-call(s32[8,512]{1,0:T(8,128)S(1)} %get-tuple-element.40.slot_ref, bf16[32,32,512]{2,1,0:T(8,128)(2,1)S(1)} %all-to-all-done.2.back_ref), custom_call_target="tpu_custom_call" | custom-call | flops 1000000000 | bytes 4194304 | tf_op jit(solution)/shard_map/unpack/pallas_call | solution.py:446
  150.7 6.0 %all-to-all-done.4.blocks_ref = bf16[16,16,128]{2,1,0:T(8,128)(2,1)S(1)} async-done(((bf16[16,16,128]{2,1,0:T(8,128)(2,1)}), bf16[16,16,128]{2,1,0:T(8,128)(2,1)S(1)}, u32[]{:S(2)}, u32[]{:S(2)}) %all-to-all-start.4) | async-done | bytes 65568 | tf_op jit(solution)/shard_map/all_to_all | solution.py:319
  (21 shorter events, 8.6 us)
Async XLA Ops:
  2.2 21.2 %all-to-all-start.1 = ((bf16[8,16,1024]{2,1,0:T(8,128)(2,1)}), bf16[8,16,1024]{2,1,0:T(8,128)(2,1)S(1)}, u32[]{:S(2)}, u32[]{:S(2)}) async-start(bf16[8,16,1024]{2,1,0:T(8,128)(2,1)} %broadcast_in_dim.12), calls=%async_computation.1 | async-start | bytes 524288 | tf_op jit(solution)/shard_map/all_to_all | solution.py:319
  13.1 1.0 copy-start
  14.1 0.7 copy-start.2
  23.4 37.4 %all-to-all-start = ((bf16[32,144,128]{2,1,0:T(8,128)(2,1)}), bf16[32,144,128]{2,1,0:T(8,128)(2,1)S(1)}, u32[]{:S(2)}, u32[]{:S(2)}) async-start(bf16[32,144,128]{2,1,0:T(8,128)(2,1)} %get-tuple-element.32), calls=%async_computation | async-start | bytes 2359296 | tf_op jit(solution)/shard_map/all_to_all | solution.py:319
  29.1 16.0 %collective-permute-start.2 = (bf16[128,1024]{1,0:T(8,128)(2,1)S(1)}, bf16[128,1024]{1,0:T(8,128)(2,1)S(1)}, u32[]{:S(2)}, u32[]{:S(2)}) collective-permute-start(bf16[128,1024]{1,0:T(8,128)(2,1)S(1)} %bitcast.12), channel_id=1, source_target_pairs={{0,256},{128,384},{256,0},{384,128},{1,257},{129,385},{257,1},{385... | collective-permute-start | bytes 786440 | tf_op jit(solution)/shard_map/ppermute | solution.py:327
  33.7 21.3 %collective-permute-start.1 = (bf16[128,1024]{1,0:T(8,128)(2,1)S(1)}, bf16[128,1024]{1,0:T(8,128)(2,1)S(1)}, u32[]{:S(2)}, u32[]{:S(2)}) collective-permute-start(bf16[128,1024]{1,0:T(8,128)(2,1)S(1)} %bitcast.13), channel_id=1, source_target_pairs={{0,384},{128,0},{256,128},{384,256},{1,385},{129,1},{257,129},{385... | collective-permute-start | bytes 786440 | tf_op jit(solution)/shard_map/ppermute | solution.py:327
  36.5 20.8 %collective-permute-start = (bf16[128,1024]{1,0:T(8,128)(2,1)S(1)}, bf16[128,1024]{1,0:T(8,128)(2,1)S(1)}, u32[]{:S(2)}, u32[]{:S(2)}) collective-permute-start(bf16[128,1024]{1,0:T(8,128)(2,1)S(1)} %bitcast.14), channel_id=1, source_target_pairs={{0,128},{128,256},{256,384},{384,0},{1,129},{129,257},{257,385},{3... | collective-permute-start | bytes 786440 | tf_op jit(solution)/shard_map/ppermute | solution.py:327
  58.4 4.8 %collective-permute-start.3 = (bf16[4,128,1024]{2,1,0:T(8,128)(2,1)}, bf16[4,128,1024]{2,1,0:T(8,128)(2,1)S(1)}, u32[]{:S(2)}, u32[]{:S(2)}) collective-permute-start(bf16[4,128,1024]{2,1,0:T(8,128)(2,1)} %pad_maximum_fusion), channel_id=1, source_target_pairs={{0,1},{1,0},{2,3},{3,2},{4,5},{5,4},{6,7},{7,6},{8,9},{9,8},{10,11... | collective-permute-start | bytes 3145736 | tf_op jit(solution)/shard_map/ppermute | solution.py:327
  60.8 2.4 %copy-start.1 = (bf16[1,512,512]{2,1,0:T(8,128)(2,1)S(1)}, bf16[1,512,512]{2,1,0:T(8,128)(2,1)}, u32[]{:S(2)}) copy-start(bf16[1,512,512]{2,1,0:T(8,128)(2,1)} %param.9) | copy-start | bytes 1572868
  74.9 6.3 %collective-permute-start.4 = (bf16[4,8,128,128]{3,2,1,0:T(8,128)(2,1)S(1)}, bf16[4,8,128,128]{3,2,1,0:T(8,128)(2,1)S(1)}, u32[]{:S(2)}, u32[]{:S(2)}) collective-permute-start(bf16[4,8,128,128]{3,2,1,0:T(8,128)(2,1)S(1)} %get-tuple-element.42), channel_id=1, source_target_pairs={{0,1},{1,0},{2,3},{3,2},{4,5},{5,4},{6,7},{7,6},{8,9},{9,8},{10,11... | collective-permute-start | bytes 3145736 | tf_op jit(solution)/shard_map/ppermute | solution.py:327
  81.5 34.7 %all-to-all-start.2 = ((bf16[32,32,512]{2,1,0:T(8,128)(2,1)}), bf16[32,32,512]{2,1,0:T(8,128)(2,1)S(1)}, u32[]{:S(2)}, u32[]{:S(2)}) async-start(bf16[32,32,512]{2,1,0:T(8,128)(2,1)} %get-tuple-element.52), calls=%async_computation.2 | async-start | bytes 2097152 | tf_op jit(solution)/shard_map/all_to_all | solution.py:319
  89.6 15.2 %collective-permute-start.5 = (bf16[8,128,128]{2,1,0:T(8,128)(2,1)S(1)}, bf16[8,128,128]{2,1,0:T(8,128)(2,1)S(1)}, u32[]{:S(2)}, u32[]{:S(2)}) collective-permute-start(bf16[8,128,128]{2,1,0:T(8,128)(2,1)S(1)} %get-tuple-element.49), channel_id=1, source_target_pairs={{0,256},{128,384},{256,0},{384,128},{1,257},{129,385},{257,1},{385... | collective-permute-start | bytes 786440 | tf_op jit(solution)/shard_map/ppermute | solution.py:327
  94.3 22.0 %collective-permute-start.6 = (bf16[8,128,128]{2,1,0:T(8,128)(2,1)S(1)}, bf16[8,128,128]{2,1,0:T(8,128)(2,1)S(1)}, u32[]{:S(2)}, u32[]{:S(2)}) collective-permute-start(bf16[8,128,128]{2,1,0:T(8,128)(2,1)S(1)} %get-tuple-element.50), channel_id=1, source_target_pairs={{0,384},{128,0},{256,128},{384,256},{1,385},{129,1},{257,129},{385... | collective-permute-start | bytes 786440 | tf_op jit(solution)/shard_map/ppermute | solution.py:327
  97.1 19.2 %collective-permute-start.7 = (bf16[8,128,128]{2,1,0:T(8,128)(2,1)S(1)}, bf16[8,128,128]{2,1,0:T(8,128)(2,1)S(1)}, u32[]{:S(2)}, u32[]{:S(2)}) collective-permute-start(bf16[8,128,128]{2,1,0:T(8,128)(2,1)S(1)} %get-tuple-element.51), channel_id=1, source_target_pairs={{0,128},{128,256},{256,384},{384,0},{1,129},{129,257},{257,385},{3... | collective-permute-start | bytes 786440 | tf_op jit(solution)/shard_map/ppermute | solution.py:327
  142.6 14.0 %all-to-all-start.4 = ((bf16[16,16,128]{2,1,0:T(8,128)(2,1)}), bf16[16,16,128]{2,1,0:T(8,128)(2,1)S(1)}, u32[]{:S(2)}, u32[]{:S(2)}) async-start(bf16[16,16,128]{2,1,0:T(8,128)(2,1)} %total.1), calls=%async_computation.4 | async-start | bytes 131072 | tf_op jit(solution)/shard_map/all_to_all | solution.py:319

commit v6 on v5

--- a/solution.py
+++ b/solution.py
@@ -127,7 +127,7 @@
     send,
     w,
     ctx_t,
-    qg_t,
+    qkv_grad,
     gout,
     nrm_t,
     qkv,
@@ -211,13 +211,13 @@
             jnp.concatenate([rows_p, rows_s], axis=1),
         ).astype(BF)
         ctx_t[whole, pts] = both[:LANES, :PATCH]
-        qg_t[block(0), pts] = both[LANES:, PATCH:]
+        qkv_grad[pts, block(0)] = both[LANES:, PATCH:].T
         both = dot(
             jnp.concatenate([cols_s, cols_p], axis=0),
             jnp.concatenate([stack(qs), stack(dc)], axis=1),
         ).astype(BF)
-        qg_t[block(1), pts] = both[:PATCH, :LANES].T
-        qg_t[block(2), pts] = both[PATCH:, LANES:].T
+        qkv_grad[pts, block(1)] = both[:PATCH, :LANES]
+        qkv_grad[pts, block(2)] = both[PATCH:, LANES:]
 
     def two_units(t, carry):
         scores_of(2 * t + 1, 1)
@@ -239,11 +239,11 @@
     for g, ref in ((1 - group, send), (group, keep)):
         for part in range(3):
             chans = pl.ds(pl.multiple_of(g * 768 + part * 256, 256), 256)
-            keep_term(ref, part, dot_t(nrm_t[...], qg_t[chans, :]).astype(BF))
+            keep_term(ref, part, dot(nrm_t[...], qkv_grad[:, chans]).astype(BF))
         cols = pl.ds(pl.multiple_of(g * 256, 256), 256)
         keep_term(ref, 3, dot(ctx_t[...], gout[:, cols]).astype(BF))
 
-def finish_kernel(hil, digits_ref, w, ctx_t, qg_t, gout_hbm, mixed_hbm, back, gout, mixed, sems):
+def finish_kernel(hil, digits_ref, w, ctx_t, qkv_grad, gout_hbm, mixed_hbm, back, gout, mixed, sems):
     gout_copy = pltpu.make_async_copy(gout_hbm, gout, sems.at[0])
     gout_copy.start()
     context = ctx_t[...].T
@@ -256,7 +256,7 @@
     centred = rows - jnp.mean(rows, axis=-1, keepdims=True)
     inv_scale = lax.rsqrt(jnp.mean(centred * centred, axis=-1, keepdims=True) + EPS)
     xhat = centred * inv_scale
-    ngrad = (dot(w[0, :, :768], qg_t[:768, :]) + dot(w[1, :, :768], qg_t[768:, :])).T
+    ngrad = dot_t(qkv_grad[:, :768], w[0, :, :768]) + dot_t(qkv_grad[:, 768:], w[1, :, :768])
     cent = ngrad - jnp.mean(ngrad, axis=-1, keepdims=True)
     cent = cent - xhat * jnp.mean(ngrad * xhat, axis=-1, keepdims=True)
     gout_copy.wait()
@@ -364,14 +364,14 @@
         cost_estimate=cost(2 * 10**9, 4 << 20),
         name="arrive",
     )(recv)
-    keep, give, weights, context_t, qkv_grad_t = pl.pallas_call(
+    keep, give, weights, context_t, qkv_grad = pl.pallas_call(
         block_kernel,
         out_shape=(
             wgrad,
             wgrad,
             jax.ShapeDtypeStruct((2, WIDTH, W_COLS), BF),
             jax.ShapeDtypeStruct((WIDTH, POINTS), BF),
-            jax.ShapeDtypeStruct((3 * WIDTH, POINTS), BF),
+            jax.ShapeDtypeStruct((POINTS, 3 * WIDTH), BF),
         ),
         in_specs=[SMEM] + [VMEM] * 6 + [HBM],
         out_specs=(VMEM,) * 5,
@@ -403,7 +403,7 @@
         compiler_params=params(12),
         cost_estimate=cost(4 * 10**9, 8 << 20),
         name="finish",
-    )(hilbert, digits, weights, context_t, qkv_grad_t, grad_out[0])
+    )(hilbert, digits, weights, context_t, qkv_grad, grad_out[0])
     theirs = shift(give, "core", 2, 1)
     pair = pl.pallas_call(
         pair_kernel,

time: 158 us -> 158 us (level)
  transfers between devices with their start and end apart: 12 -> 12, of which waited for: 8 -> 8; matrix products, arithmetic and copies ran while one was open for 1% -> 1% of each run, Pallas kernels for 6% -> 5%
where the time goes in v6:
time: 158 us; the launch traced here: 157 us
  starting transfers between devices  55.4 us (35%)
  waiting for transfers between devices  48.9 us (31%)
  blocking collectives  25.5 us (16%)
  Pallas kernels  22 us (14%)
  local copies, waits for them, and re-layouts  2.45 us (2%)
  other arithmetic  2.15 us (1%)
    ppermute x8, waiting for transfers between devices, shift(): lax.ppermute(array, axis, [(i, (i + by) % size) for i in range(size)])  36.3 us
    all_to_all x4, starting transfers between devices, exchange(): return lax.all_to_all(array, axes, split_axis=0, concat_axis=0, tiled=True)  30.8 us
    all_to_all x1, blocking collectives, exchange(): return lax.all_to_all(array, axes, split_axis=0, concat_axis=0, tiled=True)  25.5 us
    ppermute x8, starting transfers between devices, shift(): lax.ppermute(array, axis, [(i, (i + by) % size) for i in range(size)])  24.6 us
    all_to_all x4, waiting for transfers between devices, exchange(): return lax.all_to_all(array, axes, split_axis=0, concat_axis=0, tiled=True)  12.6 us
    pallas_call x1, Pallas kernels, local(): pl.pallas_call(block_kernel, out_shape=(wgrad, wgrad, jax.ShapeDtypeStruc...  11.9 us
    pallas_call x1, Pallas kernels, local(): pl.pallas_call(finish_kernel, out_shape=(jax.ShapeDtypeStruct((POINTS, WI...  3.53 us
  transfers between devices with their start and end apart: 12, of which 8 were waited for; matrix products, arithmetic and copies ran while one was open for 1% of the time, Pallas kernels for 5%

profile of v6, /device:TPU:1, one launch (start us, length us, event | category | flops | bytes accessed | tf_op | source)
XLA Modules:
  0.0 157.1 jit_solution(223556416048305997)
XLA Ops:
  2.2 10.9 %all-to-all-start.1 = ((bf16[8,16,1024]{2,1,0:T(8,128)(2,1)}), bf16[8,16,1024]{2,1,0:T(8,128)(2,1)S(1)}, u32[]{:S(2)}, u32[]{:S(2)}) async-start(bf16[8,16,1024]{2,1,0:T(8,128)(2,1)} %broadcast_in_dim.12), calls=%async_computation.1 | async-start | bytes 524288 | tf_op jit(solution)/shard_map/all_to_all | solution.py:319
  14.8 2.0 %pack.1 = (bf16[32,144,128]{2,1,0:T(8,128)(2,1)}, s32[8,512]{1,0:T(8,128)S(1)}) custom-call(s32[1,512]{1,0:T(1,128)S(1)} %copy-done.2, bf16[512,512]{1,0:T(8,128)(2,1)S(1)} %bitcast.20), custom_call_target="tpu_custom_call" | custom-call | flops 1000000000 | bytes 4194304 | tf_op jit(solution)/shard_map/pack/pallas_call | solution.py:338
  16.8 6.6 %all-to-all-done.1 = bf16[8,16,1024]{2,1,0:T(8,128)(2,1)S(1)} async-done(((bf16[8,16,1024]{2,1,0:T(8,128)(2,1)}), bf16[8,16,1024]{2,1,0:T(8,128)(2,1)S(1)}, u32[]{:S(2)}, u32[]{:S(2)}) %all-to-all-start.1) | async-done | bytes 262176 | tf_op jit(solution)/shard_map/all_to_all | solution.py:319
  23.4 5.6 %all-to-all-start = ((bf16[32,144,128]{2,1,0:T(8,128)(2,1)}), bf16[32,144,128]{2,1,0:T(8,128)(2,1)S(1)}, u32[]{:S(2)}, u32[]{:S(2)}) async-start(bf16[32,144,128]{2,1,0:T(8,128)(2,1)} %get-tuple-element.32), calls=%async_computation | async-start | bytes 2359296 | tf_op jit(solution)/shard_map/all_to_all | solution.py:319
  29.1 4.7 %collective-permute-start.2 = (bf16[128,1024]{1,0:T(8,128)(2,1)S(1)}, bf16[128,1024]{1,0:T(8,128)(2,1)S(1)}, u32[]{:S(2)}, u32[]{:S(2)}) collective-permute-start(bf16[128,1024]{1,0:T(8,128)(2,1)S(1)} %bitcast.12), channel_id=1, source_target_pairs={{0,256},{128,384},{256,0},{384,128},{1,257},{129,385},{257,1},{385... | collective-permute-start | bytes 786440 | tf_op jit(solution)/shard_map/ppermute | solution.py:327
  33.7 2.8 %collective-permute-start.1 = (bf16[128,1024]{1,0:T(8,128)(2,1)S(1)}, bf16[128,1024]{1,0:T(8,128)(2,1)S(1)}, u32[]{:S(2)}, u32[]{:S(2)}) collective-permute-start(bf16[128,1024]{1,0:T(8,128)(2,1)S(1)} %bitcast.13), channel_id=1, source_target_pairs={{0,384},{128,0},{256,128},{384,256},{1,385},{129,1},{257,129},{385... | collective-permute-start | bytes 786440 | tf_op jit(solution)/shard_map/ppermute | solution.py:327
  36.5 2.5 %collective-permute-start = (bf16[128,1024]{1,0:T(8,128)(2,1)S(1)}, bf16[128,1024]{1,0:T(8,128)(2,1)S(1)}, u32[]{:S(2)}, u32[]{:S(2)}) collective-permute-start(bf16[128,1024]{1,0:T(8,128)(2,1)S(1)} %bitcast.14), channel_id=1, source_target_pairs={{0,128},{128,256},{256,384},{384,0},{1,129},{129,257},{257,385},{3... | collective-permute-start | bytes 786440 | tf_op jit(solution)/shard_map/ppermute | solution.py:327
  39.0 6.0 %collective-permute-done.2.mine3_ref = bf16[128,1024]{1,0:T(8,128)(2,1)S(1)} collective-permute-done((bf16[128,1024]{1,0:T(8,128)(2,1)S(1)}, bf16[128,1024]{1,0:T(8,128)(2,1)S(1)}, u32[]{:S(2)}, u32[]{:S(2)}) %collective-permute-start.2) | collective-permute-done | bytes 262176 | tf_op jit(solution)/shard_map/ppermute | solution.py:327
  45.0 10.0 %collective-permute-done.1.mine2_ref = bf16[128,1024]{1,0:T(8,128)(2,1)S(1)} collective-permute-done((bf16[128,1024]{1,0:T(8,128)(2,1)S(1)}, bf16[128,1024]{1,0:T(8,128)(2,1)S(1)}, u32[]{:S(2)}, u32[]{:S(2)}) %collective-permute-start.1) | collective-permute-done | bytes 262176 | tf_op jit(solution)/shard_map/ppermute | solution.py:327
  55.0 2.3 %collective-permute-done.mine1_ref = bf16[128,1024]{1,0:T(8,128)(2,1)S(1)} collective-permute-done((bf16[128,1024]{1,0:T(8,128)(2,1)S(1)}, bf16[128,1024]{1,0:T(8,128)(2,1)S(1)}, u32[]{:S(2)}, u32[]{:S(2)}) %collective-permute-start) | collective-permute-done | bytes 262176 | tf_op jit(solution)/shard_map/ppermute | solution.py:327
  58.4 2.3 %collective-permute-start.3 = (bf16[4,128,1024]{2,1,0:T(8,128)(2,1)}, bf16[4,128,1024]{2,1,0:T(8,128)(2,1)S(1)}, u32[]{:S(2)}, u32[]{:S(2)}) collective-permute-start(bf16[4,128,1024]{2,1,0:T(8,128)(2,1)} %pad_maximum_fusion), channel_id=1, source_target_pairs={{0,1},{1,0},{2,3},{3,2},{4,5},{5,4},{6,7},{7,6},{8,9},{9,8},{10,11... | collective-permute-start | bytes 3145736 | tf_op jit(solution)/shard_map/ppermute | solution.py:327
  63.2 11.9 %block.1 = (bf16[4,8,128,128]{3,2,1,0:T(8,128)(2,1)S(1)}, bf16[4,8,128,128]{3,2,1,0:T(8,128)(2,1)S(1)}, bf16[2,512,1024]{2,1,0:T(8,128)(2,1)S(1)}, bf16[512,512]{1,0:T(8,128)(2,1)S(1)}, bf16[512,1536]{1,0:T(8,128)(2,1)S(1)}) custom-call(s32[2]{0:T(128)S(1)} %pad_add_fusion.at_ref, bf16[512,512]{1,0:T(8,128)(2,1)S(1)} %get-tuple-element.35.nrm, ...), custom_call_target="tpu_custom_call" | custom-call | flops 10000000000 | bytes 8388608 | tf_op jit(solution)/shard_map/block/pallas_call | solution.py:367
  75.1 2.4 %collective-permute-start.4 = (bf16[4,8,128,128]{3,2,1,0:T(8,128)(2,1)S(1)}, bf16[4,8,128,128]{3,2,1,0:T(8,128)(2,1)S(1)}, u32[]{:S(2)}, u32[]{:S(2)}) collective-permute-start(bf16[4,8,128,128]{3,2,1,0:T(8,128)(2,1)S(1)} %get-tuple-element.42), channel_id=1, source_target_pairs={{0,1},{1,0},{2,3},{3,2},{4,5},{5,4},{6,7},{7,6},{8,9},{9,8},{10,11... | collective-permute-start | bytes 3145736 | tf_op jit(solution)/shard_map/ppermute | solution.py:327
  77.6 3.5 %finish.1 = (bf16[512,512]{1,0:T(8,128)(2,1)}, bf16[32,32,512]{2,1,0:T(8,128)(2,1)}) custom-call(bf16[512,512]{1,0:T(8,128)(2,1)S(1)} %get-tuple-element.33.hil, bf16[32,128]{1,0:T(8,128)(2,1)S(1)} %get-tuple-element.34.digits_ref, bf16[2,512,1024]{2,1,0:T(8,128)(2,1)S(1)} %get-tuple-element.36.w, bf16[512,512]{1,0:T(8,128)(2,1)S(1)} %get-tuple-element.37.ctx_t, ...), custom_call_target="tpu_custom_call" | custom-call | flops 4000000000 | bytes 8388608 | tf_op jit(solution)/shard_map/finish/pallas_call | solution.py:390
  81.4 8.1 %all-to-all-start.2 = ((bf16[32,32,512]{2,1,0:T(8,128)(2,1)}), bf16[32,32,512]{2,1,0:T(8,128)(2,1)S(1)}, u32[]{:S(2)}, u32[]{:S(2)}) async-start(bf16[32,32,512]{2,1,0:T(8,128)(2,1)} %get-tuple-element.52), calls=%async_computation.2 | async-start | bytes 2097152 | tf_op jit(solution)/shard_map/all_to_all | solution.py:319
  89.5 4.7 %collective-permute-start.5 = (bf16[8,128,128]{2,1,0:T(8,128)(2,1)S(1)}, bf16[8,128,128]{2,1,0:T(8,128)(2,1)S(1)}, u32[]{:S(2)}, u32[]{:S(2)}) collective-permute-start(bf16[8,128,128]{2,1,0:T(8,128)(2,1)S(1)} %get-tuple-element.49), channel_id=1, source_target_pairs={{0,256},{128,384},{256,0},{384,128},{1,257},{129,385},{257,1},{385... | collective-permute-start | bytes 786440 | tf_op jit(solution)/shard_map/ppermute | solution.py:327
  94.2 2.8 %collective-permute-start.6 = (bf16[8,128,128]{2,1,0:T(8,128)(2,1)S(1)}, bf16[8,128,128]{2,1,0:T(8,128)(2,1)S(1)}, u32[]{:S(2)}, u32[]{:S(2)}) collective-permute-start(bf16[8,128,128]{2,1,0:T(8,128)(2,1)S(1)} %get-tuple-element.50), channel_id=1, source_target_pairs={{0,384},{128,0},{256,128},{384,256},{1,385},{129,1},{257,129},{385... | collective-permute-start | bytes 786440 | tf_op jit(solution)/shard_map/ppermute | solution.py:327
  97.0 2.5 %collective-permute-start.7 = (bf16[8,128,128]{2,1,0:T(8,128)(2,1)S(1)}, bf16[8,128,128]{2,1,0:T(8,128)(2,1)S(1)}, u32[]{:S(2)}, u32[]{:S(2)}) collective-permute-start(bf16[8,128,128]{2,1,0:T(8,128)(2,1)S(1)} %get-tuple-element.51), channel_id=1, source_target_pairs={{0,128},{128,256},{256,384},{384,0},{1,129},{129,257},{257,385},{3... | collective-permute-start | bytes 786440 | tf_op jit(solution)/shard_map/ppermute | solution.py:327
  99.5 5.3 %collective-permute-done.5 = bf16[8,128,128]{2,1,0:T(8,128)(2,1)S(1)} collective-permute-done((bf16[8,128,128]{2,1,0:T(8,128)(2,1)S(1)}, bf16[8,128,128]{2,1,0:T(8,128)(2,1)S(1)}, u32[]{:S(2)}, u32[]{:S(2)}) %collective-permute-start.5) | collective-permute-done | bytes 262176 | tf_op jit(solution)/shard_map/ppermute | solution.py:327
  104.7 11.4 %collective-permute-done.6 = bf16[8,128,128]{2,1,0:T(8,128)(2,1)S(1)} collective-permute-done((bf16[8,128,128]{2,1,0:T(8,128)(2,1)S(1)}, bf16[8,128,128]{2,1,0:T(8,128)(2,1)S(1)}, u32[]{:S(2)}, u32[]{:S(2)}) %collective-permute-start.6) | collective-permute-done | bytes 262176 | tf_op jit(solution)/shard_map/ppermute | solution.py:327
  116.3 25.5 %all_to_all.25.terms_ref = bf16[64,16,128]{2,1,0:T(8,128)(2,1)S(1)} all-to-all(bf16[64,16,128]{2,1,0:T(8,128)(2,1)S(1)} %bitcast.23), channel_id=1, replica_groups=mesh['x'=4,'z'=8,'y'=8,'core'=2] {'y','z'}, dimensions={0} | all-to-all | bytes 524288 | tf_op jit(solution)/shard_map/all_to_all | solution.py:319
  142.5 6.2 %all-to-all-start.4 = ((bf16[16,16,128]{2,1,0:T(8,128)(2,1)}), bf16[16,16,128]{2,1,0:T(8,128)(2,1)S(1)}, u32[]{:S(2)}, u32[]{:S(2)}) async-start(bf16[16,16,128]{2,1,0:T(8,128)(2,1)} %total.1), calls=%async_computation.4 | async-start | bytes 131072 | tf_op jit(solution)/shard_map/all_to_all | solution.py:319
  148.6 1.9 %unpack.1 = bf16[512,512]{1,0:T(8,128)(2,1)} custom-call(s32[8,512]{1,0:T(8,128)S(1)} %get-tuple-element.40.slot_ref, bf16[32,32,512]{2,1,0:T(8,128)(2,1)S(1)} %all-to-all-done.2.back_ref), custom_call_target="tpu_custom_call" | custom-call | flops 1000000000 | bytes 4194304 | tf_op jit(solution)/shard_map/unpack/pallas_call | solution.py:446
  150.5 5.9 %all-to-all-done.4.blocks_ref = bf16[16,16,128]{2,1,0:T(8,128)(2,1)S(1)} async-done(((bf16[16,16,128]{2,1,0:T(8,128)(2,1)}), bf16[16,16,128]{2,1,0:T(8,128)(2,1)S(1)}, u32[]{:S(2)}, u32[]{:S(2)}) %all-to-all-start.4) | async-done | bytes 65568 | tf_op jit(solution)/shard_map/all_to_all | solution.py:319
  (21 shorter events, 8.6 us)
Async XLA Ops:
  2.2 21.2 %all-to-all-start.1 = ((bf16[8,16,1024]{2,1,0:T(8,128)(2,1)}), bf16[8,16,1024]{2,1,0:T(8,128)(2,1)S(1)}, u32[]{:S(2)}, u32[]{:S(2)}) async-start(bf16[8,16,1024]{2,1,0:T(8,128)(2,1)} %broadcast_in_dim.12), calls=%async_computation.1 | async-start | bytes 524288 | tf_op jit(solution)/shard_map/all_to_all | solution.py:319
  13.1 1.0 copy-start
  14.1 0.7 copy-start.2
  23.4 37.4 %all-to-all-start = ((bf16[32,144,128]{2,1,0:T(8,128)(2,1)}), bf16[32,144,128]{2,1,0:T(8,128)(2,1)S(1)}, u32[]{:S(2)}, u32[]{:S(2)}) async-start(bf16[32,144,128]{2,1,0:T(8,128)(2,1)} %get-tuple-element.32), calls=%async_computation | async-start | bytes 2359296 | tf_op jit(solution)/shard_map/all_to_all | solution.py:319
  29.1 16.0 %collective-permute-start.2 = (bf16[128,1024]{1,0:T(8,128)(2,1)S(1)}, bf16[128,1024]{1,0:T(8,128)(2,1)S(1)}, u32[]{:S(2)}, u32[]{:S(2)}) collective-permute-start(bf16[128,1024]{1,0:T(8,128)(2,1)S(1)} %bitcast.12), channel_id=1, source_target_pairs={{0,256},{128,384},{256,0},{384,128},{1,257},{129,385},{257,1},{385... | collective-permute-start | bytes 786440 | tf_op jit(solution)/shard_map/ppermute | solution.py:327
  33.7 21.3 %collective-permute-start.1 = (bf16[128,1024]{1,0:T(8,128)(2,1)S(1)}, bf16[128,1024]{1,0:T(8,128)(2,1)S(1)}, u32[]{:S(2)}, u32[]{:S(2)}) collective-permute-start(bf16[128,1024]{1,0:T(8,128)(2,1)S(1)} %bitcast.13), channel_id=1, source_target_pairs={{0,384},{128,0},{256,128},{384,256},{1,385},{129,1},{257,129},{385... | collective-permute-start | bytes 786440 | tf_op jit(solution)/shard_map/ppermute | solution.py:327
  36.5 20.8 %collective-permute-start = (bf16[128,1024]{1,0:T(8,128)(2,1)S(1)}, bf16[128,1024]{1,0:T(8,128)(2,1)S(1)}, u32[]{:S(2)}, u32[]{:S(2)}) collective-permute-start(bf16[128,1024]{1,0:T(8,128)(2,1)S(1)} %bitcast.14), channel_id=1, source_target_pairs={{0,128},{128,256},{256,384},{384,0},{1,129},{129,257},{257,385},{3... | collective-permute-start | bytes 786440 | tf_op jit(solution)/shard_map/ppermute | solution.py:327
  58.4 4.8 %collective-permute-start.3 = (bf16[4,128,1024]{2,1,0:T(8,128)(2,1)}, bf16[4,128,1024]{2,1,0:T(8,128)(2,1)S(1)}, u32[]{:S(2)}, u32[]{:S(2)}) collective-permute-start(bf16[4,128,1024]{2,1,0:T(8,128)(2,1)} %pad_maximum_fusion), channel_id=1, source_target_pairs={{0,1},{1,0},{2,3},{3,2},{4,5},{5,4},{6,7},{7,6},{8,9},{9,8},{10,11... | collective-permute-start | bytes 3145736 | tf_op jit(solution)/shard_map/ppermute | solution.py:327
  60.8 2.4 %copy-start.1 = (bf16[1,512,512]{2,1,0:T(8,128)(2,1)S(1)}, bf16[1,512,512]{2,1,0:T(8,128)(2,1)}, u32[]{:S(2)}) copy-start(bf16[1,512,512]{2,1,0:T(8,128)(2,1)} %param.9) | copy-start | bytes 1572868
  75.1 6.0 %collective-permute-start.4 = (bf16[4,8,128,128]{3,2,1,0:T(8,128)(2,1)S(1)}, bf16[4,8,128,128]{3,2,1,0:T(8,128)(2,1)S(1)}, u32[]{:S(2)}, u32[]{:S(2)}) collective-permute-start(bf16[4,8,128,128]{3,2,1,0:T(8,128)(2,1)S(1)} %get-tuple-element.42), channel_id=1, source_target_pairs={{0,1},{1,0},{2,3},{3,2},{4,5},{5,4},{6,7},{7,6},{8,9},{9,8},{10,11... | collective-permute-start | bytes 3145736 | tf_op jit(solution)/shard_map/ppermute | solution.py:327
  81.4 34.8 %all-to-all-start.2 = ((bf16[32,32,512]{2,1,0:T(8,128)(2,1)}), bf16[32,32,512]{2,1,0:T(8,128)(2,1)S(1)}, u32[]{:S(2)}, u32[]{:S(2)}) async-start(bf16[32,32,512]{2,1,0:T(8,128)(2,1)} %get-tuple-element.52), calls=%async_computation.2 | async-start | bytes 2097152 | tf_op jit(solution)/shard_map/all_to_all | solution.py:319
  89.5 15.2 %collective-permute-start.5 = (bf16[8,128,128]{2,1,0:T(8,128)(2,1)S(1)}, bf16[8,128,128]{2,1,0:T(8,128)(2,1)S(1)}, u32[]{:S(2)}, u32[]{:S(2)}) collective-permute-start(bf16[8,128,128]{2,1,0:T(8,128)(2,1)S(1)} %get-tuple-element.49), channel_id=1, source_target_pairs={{0,256},{128,384},{256,0},{384,128},{1,257},{129,385},{257,1},{385... | collective-permute-start | bytes 786440 | tf_op jit(solution)/shard_map/ppermute | solution.py:327
  94.2 22.0 %collective-permute-start.6 = (bf16[8,128,128]{2,1,0:T(8,128)(2,1)S(1)}, bf16[8,128,128]{2,1,0:T(8,128)(2,1)S(1)}, u32[]{:S(2)}, u32[]{:S(2)}) collective-permute-start(bf16[8,128,128]{2,1,0:T(8,128)(2,1)S(1)} %get-tuple-element.50), channel_id=1, source_target_pairs={{0,384},{128,0},{256,128},{384,256},{1,385},{129,1},{257,129},{385... | collective-permute-start | bytes 786440 | tf_op jit(solution)/shard_map/ppermute | solution.py:327
  97.0 19.2 %collective-permute-start.7 = (bf16[8,128,128]{2,1,0:T(8,128)(2,1)S(1)}, bf16[8,128,128]{2,1,0:T(8,128)(2,1)S(1)}, u32[]{:S(2)}, u32[]{:S(2)}) collective-permute-start(bf16[8,128,128]{2,1,0:T(8,128)(2,1)S(1)} %get-tuple-element.51), channel_id=1, source_target_pairs={{0,128},{128,256},{256,384},{384,0},{1,129},{129,257},{257,385},{3... | collective-permute-start | bytes 786440 | tf_op jit(solution)/shard_map/ppermute | solution.py:327
  142.5 14.0 %all-to-all-start.4 = ((bf16[16,16,128]{2,1,0:T(8,128)(2,1)}), bf16[16,16,128]{2,1,0:T(8,128)(2,1)S(1)}, u32[]{:S(2)}, u32[]{:S(2)}) async-start(bf16[16,16,128]{2,1,0:T(8,128)(2,1)} %total.1), calls=%async_computation.4 | async-start | bytes 131072 | tf_op jit(solution)/shard_map/all_to_all | solution.py:319
